TPU v7x, 128 devices: a whole 4x4x4 slice. The times are simulated.
128 devices in a mesh: seq: 32 (over x, y, z_hi), dp: 4 (over z_lo, core).
Axes of the slice: x: 4, y: 4, z: 4 (z_hi: 2, z_lo: 2; z = z_hi * 2 + z_lo), core: 2. Of those that a mesh axis runs over, the one named last changes fastest.
Arguments:
- hidden: bfloat16 [4, 4096, 4096], P('dp', 'seq'), may hold values from -6 to 6
- queries: bfloat16 [4, 4096, 4096], P('dp', 'seq'), may hold values from -122 to 122
- keyvals: bfloat16 [4, 4096, 512], P('dp', 'seq'), may hold values from -5 to 5
- out_grad: bfloat16 [4, 4096, 4096], P('dp', 'seq'), may hold values from -6 to 6
- segment: int32 [4, 4096], P('dp', 'seq'), may hold values from 0 to 2, never falling along the last dimension, each value on 1 to 3072 neighbouring positions
Outputs:
- query_grad: bfloat16 [4, 4096, 4096], P('dp', 'seq')
- keyval_grad: bfloat16 [4, 4096, 512], P('dp', 'seq')
- weight_grad: float32 [4096, 512], P(('seq', 'dp'))
All inputs are finite; a program needn't handle non-finite values.
Results may differ from a plain program's by a relative error of at most 0.02.
Values may be sent and summed in bfloat16 or wider, within the bound.
No kernel may reach another device: no remote copies, remote signals or barrier semaphores. Data moves between devices by JAX's collectives and lax.ppermute only.
A program may use at most 128 MiB of HBM per device.

v0:
```python
import math

import jax
import jax.numpy as jnp
from jax import lax
from jax.sharding import PartitionSpec as P

HQ = 32
HK = 2
DH = 128


MASKED = -1e30


def make_forward(query_parts, qseg_parts, qpos_parts):
    scale = DH ** (-0.5)

    def fold(carry, piece, start):
        keyval_piece, segment_piece = piece
        count = keyval_piece.shape[0]
        span = math.gcd(count, 512)
        places = jnp.arange(count, dtype=jnp.int32)

        def block(index, state):
            first = index * span
            chosen = lax.dynamic_slice_in_dim(keyval_piece, first, span, 0)
            keys = chosen[:, : HK * DH].reshape(span, HK, DH)
            values = chosen[:, HK * DH :].reshape(span, HK, DH)
            kseg = lax.dynamic_slice_in_dim(segment_piece, first, span, 0)
            kpos = lax.dynamic_slice_in_dim(places, first, span, 0)
            updated = []
            for part in range(2):
                query = query_parts[part]
                allowed = (qseg_parts[part][:, None] == kseg[None, :]) & (
                    kpos[None, :] <= qpos_parts[part][:, None]
                )

                def update(parts):
                    top, total, accum = parts
                    scores = (
                        jnp.einsum(
                            "qhgd,khd->hgqk", query, keys, preferred_element_type=jnp.float32
                        )
                        * scale
                    )
                    newtop = jnp.maximum(top, jnp.max(jnp.where(allowed, scores, MASKED), axis=-1))
                    weights = jnp.where(allowed, jnp.exp(scores - newtop[..., None]), 0.0)
                    fade = jnp.exp(top - newtop)
                    total = total * fade + jnp.sum(weights, axis=-1)
                    accum = accum * jnp.transpose(fade, (2, 0, 1))[..., None] + jnp.einsum(
                        "hgqk,khd->qhgd",
                        weights.astype(jnp.bfloat16),
                        values,
                        preferred_element_type=jnp.float32,
                    )
                    return (newtop, total, accum)

                updated.append(lax.cond(jnp.any(allowed), update, lambda parts: parts, state[part]))
            return (updated[0], updated[1])

        return lax.fori_loop(0, count // span, block, carry)

    return fold


def make_backward(query_parts, grad_parts, qseg_parts, qpos_parts, log_totals, deltas):
    scale = DH ** (-0.5)

    def fold(carry, piece, start):
        keyval_piece, segment_piece = piece
        count = keyval_piece.shape[0]
        span = math.gcd(count, 512)
        places = jnp.arange(count, dtype=jnp.int32)

        def block(index, state):
            query_accs, keyval_all = state
            first = index * span
            chosen = lax.dynamic_slice_in_dim(keyval_piece, first, span, 0)
            keys = chosen[:, : HK * DH].reshape(span, HK, DH)
            values = chosen[:, HK * DH :].reshape(span, HK, DH)
            kseg = lax.dynamic_slice_in_dim(segment_piece, first, span, 0)
            kpos = lax.dynamic_slice_in_dim(places, first, span, 0)
            key_block = jnp.zeros((span, HK, DH), jnp.float32)
            value_block = jnp.zeros((span, HK, DH), jnp.float32)
            updated = []
            for part in range(2):
                query = query_parts[part]
                cotan = grad_parts[part]
                log_total = log_totals[part]
                delta = deltas[part]
                allowed = (qseg_parts[part][:, None] == kseg[None, :]) & (
                    kpos[None, :] <= qpos_parts[part][:, None]
                )

                def update(parts):
                    query_acc, key_acc, value_acc = parts
                    scores = (
                        jnp.einsum(
                            "qhgd,khd->hgqk", query, keys, preferred_element_type=jnp.float32
                        )
                        * scale
                    )
                    weights = jnp.where(allowed, jnp.exp(scores - log_total[..., None]), 0.0)
                    value_acc = value_acc + jnp.einsum(
                        "hgqk,qhgd->khd",
                        weights.astype(jnp.bfloat16),
                        cotan,
                        preferred_element_type=jnp.float32,
                    )
                    dprob = jnp.einsum(
                        "qhgd,khd->hgqk", cotan, values, preferred_element_type=jnp.float32
                    )
                    dscore = (weights * (dprob - delta[..., None])).astype(jnp.bfloat16)
                    query_acc = (
                        query_acc
                        + jnp.einsum(
                            "hgqk,khd->qhgd", dscore, keys, preferred_element_type=jnp.float32
                        )
                        * scale
                    )
                    key_acc = (
                        key_acc
                        + jnp.einsum(
                            "hgqk,qhgd->khd", dscore, query, preferred_element_type=jnp.float32
                        )
                        * scale
                    )
                    return (query_acc, key_acc, value_acc)

                result = lax.cond(
                    jnp.any(allowed),
                    update,
                    lambda parts: parts,
                    (query_accs[part], key_block, value_block),
                )
                updated.append(result[0])
                key_block = result[1]
                value_block = result[2]
            older = lax.dynamic_slice(keyval_all, (first, 0), (span, 2 * HK * DH))
            fresh = jnp.concatenate(
                [key_block.reshape(span, HK * DH), value_block.reshape(span, HK * DH)], axis=-1
            )
            keyval_all = lax.dynamic_update_slice(keyval_all, older + fresh, (first, 0))
            return ((updated[0], updated[1]), keyval_all)

        return lax.fori_loop(0, count // span, block, carry)

    return fold


def shards(hidden, queries, keyvals, out_grad, segment):
    groups = HQ // HK
    shard_rows = queries.shape[1]
    half = shard_rows // 2
    cycle_size = lax.axis_size("seq")
    position = lax.axis_index("seq")
    local_q = queries[0]
    local_kv = keyvals[0]
    local_grad = out_grad[0]
    local_seg = segment[0]
    local_hidden = hidden[0]
    row_index = jnp.arange(shard_rows, dtype=jnp.int32)
    qpos = position * shard_rows + row_index
    query_parts = [
        local_q[p * half : (p + 1) * half].reshape(half, HK, groups, DH) for p in range(2)
    ]
    grad_parts = [
        local_grad[p * half : (p + 1) * half].reshape(half, HK, groups, DH) for p in range(2)
    ]
    qseg_parts = [local_seg[p * half : (p + 1) * half] for p in range(2)]
    qpos_parts = [qpos[p * half : (p + 1) * half] for p in range(2)]
    forward = make_forward(query_parts, qseg_parts, qpos_parts)
    empty_part = (
        jnp.full((HK, groups, half), MASKED, jnp.float32),
        jnp.zeros((HK, groups, half), jnp.float32),
        jnp.zeros((half, HK, groups, DH), jnp.float32),
    )
    start_forward = (empty_part, empty_part)
    start_backward = (
        (
            jnp.zeros((half, HK, groups, DH), jnp.float32),
            jnp.zeros((half, HK, groups, DH), jnp.float32),
        ),
        jnp.zeros((shard_rows * cycle_size, 2 * HK * DH), jnp.float32),
    )
    whole_kv, whole_seg = (
        lax.all_gather(local_kv, "seq", axis=0, tiled=True),
        lax.all_gather(local_seg, "seq", axis=0, tiled=True),
    )
    stats = forward(start_forward, (whole_kv, whole_seg), jnp.int32(0))
    log_totals = []
    deltas = []
    for part in range(2):
        top, total, accum = stats[part]
        attended = accum / jnp.transpose(total, (2, 0, 1))[..., None]
        log_totals.append(top + jnp.log(total))
        product = jnp.sum(grad_parts[part].astype(jnp.float32) * attended, axis=-1)
        deltas.append(jnp.transpose(product, (1, 2, 0)))
    log_totals, deltas = (log_totals, deltas)
    backward = make_backward(query_parts, grad_parts, qseg_parts, qpos_parts, log_totals, deltas)
    results = backward(start_backward, (whole_kv, whole_seg), jnp.int32(0))
    query_accs, keyval_all = results
    keyval_mine = lax.psum_scatter(
        keyval_all.astype(jnp.bfloat16), "seq", scatter_dimension=0, tiled=True
    )
    query_grad = jnp.concatenate(
        [query_accs[0].reshape(half, HQ * DH), query_accs[1].reshape(half, HQ * DH)], axis=0
    ).astype(jnp.bfloat16)
    weight_grad = lax.psum_scatter(
        jnp.einsum("td,tc->dc", local_hidden, keyval_mine, preferred_element_type=jnp.float32),
        ("seq", "dp"),
        scatter_dimension=0,
        tiled=True,
    )
    return (query_grad[None], keyval_mine[None], weight_grad)


def solution(mesh):
    in_specs = (
        P("dp", "seq", None),
        P("dp", "seq", None),
        P("dp", "seq", None),
        P("dp", "seq", None),
        P("dp", "seq"),
    )
    out_specs = (P("dp", "seq", None), P("dp", "seq", None), P(("seq", "dp"), None))
    return jax.shard_map(shards, mesh=mesh, in_specs=in_specs, out_specs=out_specs, check_vma=False)
```

profile of v0, /device:TPU:0, one launch (start us, length us, event | category | flops | bytes accessed | tf_op | source)
XLA Modules:
  0.0 1284.2 jit_solution(2259804517729809675)
XLA Ops:
  13.4 95.5 %all-gather = s32[1,4096]{1,0:T(1,128)S(1)} all-gather(s32[1,128]{1,0:T(1,128)S(1)} %copy-done.20), channel_id=2, replica_groups=mesh['seq'=32,'dp'=4] {'seq'}, dimensions={1}, use_global_device_ids=true | all-gather | bytes 16896 | tf_op jit(solution)/shard_map/all_gather | solution.py:189
  109.1 3.4 all-gather.4.cloned.1.call-done
  114.6 35.1 %while.43 = (s32[]{:T(128)}, f32[2,16,64]{2,1,0:T(8,128)S(1)}, f32[2,16,64]{2,1,0:T(8,128)S(1)}, f32[64,2,16,128]{3,0,2,1:T(8,128)}, f32[2,16,64]{2,1,0:T(8,128)...) while((s32[]{:T(128)}, f32[2,16,64]{2,1,0:T(8,128)S(1)}, ...), condition=%wide.region_11.12_spmd, body=%wide.region_0.11_spmd.sunk | while | flops 1098133504 | bytes 49821280 | solution.py:62
  117.8 4.5 conditional.8
  122.3 4.5 conditional.9
  150.0 3.9 fusion.95
  156.9 4.3 broadcast_in_dim.97.clone
  161.2 126.9 %while.44 = (s32[]{:T(128)}, f32[64,2,16,128]{3,0,2,1:T(8,128)}, f32[64,2,16,128]{3,0,2,1:T(8,128)}, f32[4096,512]{1,0:T(8,128)}, s32[64]{0:T(128)S(1)}, /*index...) while((s32[]{:T(128)}, f32[64,2,16,128]{3,0,2,1:T(8,128)}, ...), condition=%wide.region_21.22_spmd, body=%wide.region_14.21_spmd.sunk | while | flops 2707685376 | bytes 91027256 | solution.py:147
  167.9 6.9 conditional.10
  174.8 8.6 conditional.11
  186.5 2.3 constant_dynamic-update-slice_fusion.2
  200.7 2.3 constant_dynamic-update-slice_fusion.2
  214.8 2.3 constant_dynamic-update-slice_fusion.2
  229.0 2.3 constant_dynamic-update-slice_fusion.2
  243.2 2.3 constant_dynamic-update-slice_fusion.2
  257.4 2.3 constant_dynamic-update-slice_fusion.2
  271.5 2.3 constant_dynamic-update-slice_fusion.2
  285.7 2.3 constant_dynamic-update-slice_fusion.2
  288.1 5.9 convert_element_type.65
  294.0 323.3 %reduce-scatter.5.cloned.1.call-done = bf16[128,512]{1,0:T(8,128)(2,1)} async-done(((bf16[4096,512]{1,0:T(8,128)(2,1)}), bf16[128,512]{1,0:T(8,128)(2,1)}) %reduce-scatter.5.cloned.1.call-update) | async-done | bytes 131088 | tf_op jit(solution)/shard_map/reduce_scatter | solution.py:204
  617.3 5.4 convolution_bitcast_fusion.2
  622.7 9.0 copy.100
  635.2 2.1 pad_maximum_fusion
  637.3 640.3 %reduce-scatter.7.cloned.1.call-done = f32[32,512]{1,0:T(8,128)} async-done(((f32[4096,512]{1,0:T(8,128)}), f32[32,512]{1,0:T(8,128)}) %reduce-scatter.7.cloned.1.call-update) | async-done | bytes 65552
  (259 shorter events, 152.7 us)
Async XLA Ops:
  7.2 610.2 %copy-start = (bf16[1,128,4096]{2,1,0:T(8,128)(2,1)S(1)}, bf16[1,128,4096]{2,1,0:T(8,128)(2,1)}, u32[]{:S(2)}) copy-start(bf16[1,128,4096]{2,1,0:T(8,128)(2,1)} %param.17) | copy-start | bytes 3145732
  7.2 105.2 %all-gather.4.cloned.1.call-start = ((), (), s32[]{:S(2)}) async-start(), calls=%async_computation.3 | async-start | bytes 4325376 | tf_op jit(solution)/shard_map/all_gather | solution.py:188
  9.0 608.3 %reduce-scatter.5.cloned.1.call-start = ((), (), s32[]{:S(2)}) async-start(), calls=%async_computation.2 | async-start | bytes 4325376 | tf_op jit(solution)/shard_map/reduce_scatter | solution.py:204
  9.0 2.0 copy-start.15
  10.8 2.7 copy-start.20
  12.4 102.3 %copy-start.10 = (bf16[8,8,32,128]{3,2,1,0:T(8,128)(2,1)}, bf16[8,8,32,128]{3,2,1,0:T(8,128)(2,1)S(1)}, u32[]{:S(2)}) copy-start(bf16[8,8,32,128]{3,2,1,0:T(8,128)(2,1)S(1)} %copy.109) | copy-start | bytes 1572868
  117.9 2.1 copy-start.13
  121.4 1.0 copy-start.14
  122.3 2.1 copy-start.11
  125.8 1.0 copy-start.12
  167.9 1.0 copy-start.17
  167.9 1.0 copy-start.19
  168.9 1.7 copy-start.8
  170.6 2.5 copy-start.4
  173.8 1.0 copy-start.5
  174.8 1.9 copy-start.18
  176.0 1.0 copy-start.7
  176.0 1.2 copy-start.16
  177.2 1.8 copy-start.9
  179.0 2.7 copy-start.1
  182.4 1.0 copy-start.2
  294.0 983.7 %reduce-scatter.7.cloned.1.call-start = ((), (), s32[]{:S(2)}) async-start(), calls=%async_computation.4 | async-start | bytes 8454144
  631.8 1.2 copy-start.6
  631.8 2.7 copy-start.3
Sparse Core Ops, SparseCore 0:
  11.4 101.0 all-gather.3
  294.1 323.1 reduce-scatter.4
  631.9 645.6 reduce-scatter.6
where the time goes:
time: 1290 us; the launch traced here: 1280 us
  waiting for transfers between devices  967 us (75%)
  local copies, waits for them, and re-layouts  123 us (10%)
  blocking collectives  95.5 us (7%)
  other arithmetic  41.7 us (3%)
  loops' own time  21.2 us (2%)
  matrix products  21.2 us (2%)
  between operations  13.9 us (1%)
    unnamed x4, waiting for transfers between devices  640 us
    reduce_scatter x1, waiting for transfers between devices, shards(): lax.psum_scatter(keyval_all.astype(jnp.bfloat16), 'seq', scatter_dimensio...  323 us
    all_gather x1, blocking collectives, shards(): lax.all_gather(local_seg, 'seq', axis=0, tiled=True)  95.5 us
    dynamic_update_slice x16, local copies, waits for them, and re-layouts, block(): keyval_all = lax.dynamic_update_slice(keyval_all, older + fresh, (first, 0))  29.2 us
  transfers between devices with their start and end apart: 3, of which 3 were waited for; matrix products, arithmetic and copies ran while one was open for 1% of the time, Pallas kernels for 0%

commit v1 on v0

v1 whole, which is shorter than its diff:
```python
import jax
import jax.numpy as jnp
from jax import lax
from jax.experimental import pallas as pl
from jax.experimental.pallas import tpu as pltpu
from jax.sharding import PartitionSpec as P

HQ = 32
HK = 2
DH = 128
SCALE = DH ** -0.5
EXP2_SCALE = SCALE * 1.4426950408889634
MASKED = -1e30
LOWEST = -1e29
SEGMENT_ROWS = 16
BQ = 512
BK = 512
NT = (((1,), (1,)), ((), ()))
NN = (((1,), (0,)), ((), ()))
TN = (((0,), (0,)), ((), ()))

def dot(a, b, dims):
    return lax.dot_general(a, b, dims, preferred_element_type=jnp.float32)

def attention_kernel(x_ref, dq_ref, dkv_ref, p_ref, dp_ref, m_ref, dk_ref, dv_ref):
    blocks = x_ref.shape[0]
    seq = blocks * 128
    qn, kn = BQ // 128, BK // 128

    def rows(first, count, slot):
        return x_ref[pl.ds(first, count), slot * 128 : (slot + 1) * 128, :].reshape(count * 128, DH)

    segments = x_ref[:, 512:513, :].astype(jnp.float32)
    count0 = jnp.sum(jnp.where(segments < 0.5, 1.0, 0.0)).astype(jnp.int32)
    count1 = jnp.sum(jnp.where(segments < 1.5, 1.0, 0.0)).astype(jnp.int32)

    def start_of(pos):
        return jnp.where(pos >= count1, count1, jnp.where(pos >= count0, count0, 0))

    dk_ref[...] = jnp.zeros_like(dk_ref)
    dv_ref[...] = jnp.zeros_like(dv_ref)

    def query_block(i, _):
        first = i * BQ
        q = rows(i * qn, qn, 0)
        cotan = rows(i * qn, qn, 1)
        qpos = first + lax.broadcasted_iota(jnp.int32, (1, BQ), 1)
        qstart = start_of(qpos)
        low = start_of(first) // BK
        high = (first + BQ - 1) // BK + 1
        last_start = start_of(first + BQ - 1)

        def scores(kb, carry, masked):
            top, total, delta = carry
            k = rows(kb * kn, kn, 2)
            v = rows(kb * kn, kn, 3)
            st = dot(k, q, NT)
            dpt = dot(v, cotan, NT)
            if masked:
                kpos = kb * BK + lax.broadcasted_iota(jnp.int32, (BK, BQ), 0)
                st = jnp.where((kpos >= qstart) & (kpos <= qpos), st, MASKED)
            newtop = jnp.maximum(top, jnp.max(st, axis=0, keepdims=True))
            p = jnp.exp2((st - newtop) * EXP2_SCALE)
            fade = jnp.exp2((top - newtop) * EXP2_SCALE)
            total = total * fade + jnp.sum(p, axis=0, keepdims=True)
            delta = delta * fade + jnp.sum(p * dpt, axis=0, keepdims=True)
            at = pl.ds(pl.multiple_of(kb * BK, BK), BK)
            p_ref[at, :] = p
            dp_ref[at, :] = dpt
            m_ref[pl.ds(kb, 1), :] = newtop
            return newtop, total, delta

        def step(kb, carry):
            plain = ((kb + 1) * BK - 1 <= first) & (kb * BK >= last_start)
            return lax.cond(plain, lambda c: scores(kb, c, False), lambda c: scores(kb, c, True), carry)

        zero = jnp.zeros((1, BQ), jnp.float32)
        top, total, delta = lax.fori_loop(low, high, step, (zero + LOWEST, zero, zero))
        inverse = 1.0 / total
        delta = delta * inverse

        def grads(kb, dq):
            k = rows(kb * kn, kn, 2)
            at = pl.ds(pl.multiple_of(kb * BK, BK), BK)
            factor = jnp.exp2((m_ref[pl.ds(kb, 1), :] - top) * EXP2_SCALE) * inverse
            w = p_ref[at, :] * factor
            ds = (w * (dp_ref[at, :] - delta)).astype(jnp.bfloat16)
            dv_ref[at, :] += dot(w.astype(jnp.bfloat16), cotan, NN)
            dk_ref[at, :] += dot(ds, q, NN)
            return dq + dot(ds, k, TN)

        dq = lax.fori_loop(low, high, grads, jnp.zeros((BQ, DH), jnp.float32))
        dq_ref[pl.ds(i * qn, qn)] = (dq * SCALE).astype(jnp.bfloat16).reshape(qn, 128, DH)
        return 0

    lax.fori_loop(0, seq // BQ, query_block, 0)

    def finish(b, _):
        at = pl.ds(pl.multiple_of(b * 128, 128), 128)
        dkv_ref[b, :128, :] = (dk_ref[at, :] * SCALE).astype(jnp.bfloat16)
        dkv_ref[b, 128:, :] = dv_ref[at, :].astype(jnp.bfloat16)
        return 0

    lax.fori_loop(0, blocks, finish, 0)

def attention(x):
    blocks = x.shape[0]
    seq = blocks * 128
    spec = pl.BlockSpec(memory_space=pltpu.VMEM)
    return pl.pallas_call(
        attention_kernel,
        out_shape=(
            jax.ShapeDtypeStruct((blocks, 128, DH), jnp.bfloat16),
            jax.ShapeDtypeStruct((blocks, 256, DH), jnp.bfloat16),
        ),
        in_specs=[spec],
        out_specs=(spec, spec),
        scratch_shapes=[
            pltpu.VMEM((seq, BQ), jnp.float32),
            pltpu.VMEM((seq, BQ), jnp.float32),
            pltpu.VMEM((max(8,seq // BK), BQ), jnp.float32),
            pltpu.VMEM((seq, DH), jnp.float32),
            pltpu.VMEM((seq, DH), jnp.float32),
        ],
        compiler_params=pltpu.CompilerParams(vmem_limit_bytes=40 * 1024 * 1024),
        name="attention",
    )(x)


def shards(hidden, queries, keyvals, out_grad, segment):
    seq, dp = lax.axis_size("seq"), lax.axis_size("dp")
    tokens, width = hidden.shape[1], hidden.shape[2]
    groups = HQ // HK

    def by_head(array):
        return jnp.transpose(array.reshape(tokens, HQ, DH), (1, 0, 2))

    kv = jnp.transpose(keyvals[0].reshape(tokens, 2 * HK, DH), (1, 0, 2))
    numbers = segment[0].astype(jnp.bfloat16)
    send = jnp.concatenate(
        [
            by_head(queries[0]),
            by_head(out_grad[0]),
            jnp.repeat(kv[:HK], groups, axis=0),
            jnp.repeat(kv[HK:], groups, axis=0),
            jnp.broadcast_to(numbers, (HQ, SEGMENT_ROWS, tokens)),
        ],
        axis=1,
    )
    mine = lax.all_to_all(send, "seq", split_axis=0, concat_axis=0, tiled=True)

    share = width // (seq * dp)
    columns = jnp.transpose(hidden[0].T.reshape(seq, dp, share, tokens), (1, 0, 2, 3))
    columns = columns.reshape(dp, seq * share, tokens)
    columns = lax.all_to_all(columns, "dp", split_axis=0, concat_axis=0, tiled=True)

    dq, dkv = attention(mine)
    dkv = lax.all_to_all(dkv, "seq", split_axis=0, concat_axis=0, tiled=True)
    dq = lax.all_to_all(dq, "seq", split_axis=0, concat_axis=0, tiled=True)
    query_grad = jnp.transpose(dq, (1, 0, 2)).reshape(tokens, HQ * DH)

    total = jnp.sum(dkv.reshape(HK, groups, 2, tokens, DH).astype(jnp.float32), axis=1)
    keyval_grad = jnp.transpose(total, (2, 1, 0, 3)).reshape(tokens, 2 * HK * DH)
    keyval_grad = keyval_grad.astype(jnp.bfloat16)

    every = lax.all_gather(keyval_grad, "dp", axis=0)
    partial = jnp.einsum("sdt,stc->dc", columns, every, preferred_element_type=jnp.float32)
    partial = partial.astype(jnp.bfloat16).reshape(seq, share, 2 * HK * DH)
    partial = lax.all_to_all(partial, "seq", split_axis=0, concat_axis=0, tiled=True)
    weight_grad = jnp.sum(partial.astype(jnp.float32), axis=0)
    return (query_grad[None], keyval_grad[None], weight_grad)


def solution(mesh):
    in_specs = (
        P("dp", "seq", None),
        P("dp", "seq", None),
        P("dp", "seq", None),
        P("dp", "seq", None),
        P("dp", "seq"),
    )
    out_specs = (P("dp", "seq", None), P("dp", "seq", None), P(("seq", "dp"), None))
    return jax.shard_map(shards, mesh=mesh, in_specs=in_specs, out_specs=out_specs, check_vma=False)
```

time: 1290 us -> 208 us (0.16)
  waiting for transfers between devices: 967 us -> 79.4 us
  local copies, waits for them, and re-layouts: 123 us -> 15.2 us
  blocking collectives: 95.5 us -> 49.2 us
  other arithmetic: 41.7 us -> 2.73 us
  Pallas kernels: 0 us -> 32.5 us
  starting transfers between devices: 0.12 us -> 25.9 us
  loops' own time: 21.2 us -> 0 us
  matrix products: 21.2 us -> 0.77 us
  between operations: 13.9 us -> 0.86 us
    unnamed x4 -> x0, waiting for transfers between devices: 640 us -> none
    reduce_scatter x1 -> x0, waiting for transfers between devices: 323 us -> none  [shards(): lax.psum_scatter(keyval_all.astype(jnp.bfloat16), 'seq', scatter_dimensio...]
    all_gather x1, blocking collectives: 95.5 us -> 14 us  [shards(): every = lax.all_gather(keyval_grad, 'dp', axis=0)]
    all_to_all x0 -> x4, waiting for transfers between devices: none -> 79.4 us  [the longest x1 61.5 us: shards(): mine = lax.all_to_all(send, 'seq', split_axis=0, concat_axis=0, tiled=True)]
    all_to_all x0 -> x1, blocking collectives: none -> 35.2 us  [shards(): dkv = lax.all_to_all(dkv, 'seq', split_axis=0, concat_axis=0, tiled=True)]
    pallas_call x0 -> x1, Pallas kernels: none -> 32.5 us  [attention(): pl.pallas_call(attention_kernel, out_shape=(jax.ShapeDtypeStruct((blocks,...]
    dynamic_update_slice x16 -> x0, local copies, waits for them, and re-layouts: 29.2 us -> none  [block(): keyval_all = lax.dynamic_update_slice(keyval_all, older + fresh, (first, 0))]
    all_to_all x0 -> x4, starting transfers between devices: none -> 25.9 us  [the longest x1 11 us: shards(): mine = lax.all_to_all(send, 'seq', split_axis=0, concat_axis=0, tiled=True)]
  transfers between devices with their start and end apart: 3 -> 4, of which waited for: 3 -> 3; matrix products, arithmetic and copies ran while one was open for 1% -> 4% of each run, Pallas kernels for 0% -> 16%
where the time goes in v1:
time: 208 us; the launch traced here: 207 us
  waiting for transfers between devices  79.4 us (38%)
  blocking collectives  49.2 us (24%)
  Pallas kernels  32.5 us (16%)
  starting transfers between devices  25.9 us (12%)
  local copies, waits for them, and re-layouts  15.2 us (7%)
  other arithmetic  2.73 us (1%)
    all_to_all x1, waiting for transfers between devices, shards(): mine = lax.all_to_all(send, 'seq', split_axis=0, concat_axis=0, tiled=True)  61.5 us
    all_to_all x1, blocking collectives, shards(): dkv = lax.all_to_all(dkv, 'seq', split_axis=0, concat_axis=0, tiled=True)  35.2 us
    pallas_call x1, Pallas kernels, attention(): pl.pallas_call(attention_kernel, out_shape=(jax.ShapeDtypeStruct((blocks,...  32.5 us
    all_to_all x1, waiting for transfers between devices, shards(): lax.all_to_all(partial, 'seq', split_axis=0, concat_axis=0, tiled=True)  17.5 us
    all_gather x1, blocking collectives, shards(): every = lax.all_gather(keyval_grad, 'dp', axis=0)  14 us
    all_to_all x1, starting transfers between devices, shards(): mine = lax.all_to_all(send, 'seq', split_axis=0, concat_axis=0, tiled=True)  11 us
    unnamed x19, local copies, waits for them, and re-layouts  9.27 us
    all_to_all x1, starting transfers between devices, shards(): lax.all_to_all(partial, 'seq', split_axis=0, concat_axis=0, tiled=True)  7.45 us
  transfers between devices with their start and end apart: 4, of which 3 were waited for; matrix products, arithmetic and copies ran while one was open for 4% of the time, Pallas kernels for 16%

profile of v1, /device:TPU:0, one launch (start us, length us, event | category | flops | bytes accessed | tf_op | source)
XLA Modules:
  0.0 206.5 jit_solution(11590785560177676513)
XLA Ops:
  0.6 1.7 copy.36
  2.4 0.7 copy.37
  3.0 1.2 bitcast_dynamic-update-slice_fusion.1
  4.9 0.7 copy.39
  5.8 1.2 bitcast_dynamic-update-slice_fusion
  7.2 1.2 constant_dynamic-update-slice_fusion.1
  8.6 1.2 constant_dynamic-update-slice_fusion
  9.9 0.7 broadcast_dynamic-update-slice_fusion
  10.6 11.0 %all-to-all-start = ((bf16[32,528,128]{2,1,0:T(8,128)(2,1)}), bf16[32,528,128]{2,1,0:T(8,128)(2,1)}, u32[]{:S(2)}, u32[]{:S(2)}) async-start(bf16[32,528,128]{2,1,0:T(8,128)(2,1)} %broadcast_dynamic-update-slice_fusion), calls=%async_computation | async-start | bytes 8650752 | tf_op jit(solution)/shard_map/all_to_all | solution.py:150
  22.2 1.2 copy.46
  23.4 61.5 %all-to-all-done.x_ref = bf16[32,528,128]{2,1,0:T(8,128)(2,1)} async-done(((bf16[32,528,128]{2,1,0:T(8,128)(2,1)}), bf16[32,528,128]{2,1,0:T(8,128)(2,1)}, u32[]{:S(2)}, u32[]{:S(2)}) %all-to-all-start) | async-done | bytes 4325408 | tf_op jit(solution)/shard_map/all_to_all | solution.py:150
  84.9 3.5 %all-to-all-start.3 = ((bf16[4,1024,128]{2,1,0:T(8,128)(2,1)}), bf16[4,1024,128]{2,1,0:T(8,128)(2,1)S(1)}, u32[]{:S(2)}, u32[]{:S(2)}) async-start(bf16[4,1024,128]{2,1,0:T(8,128)(2,1)} %bitcast.17), calls=%async_computation.3 | async-start | bytes 2097152 | tf_op jit(solution)/shard_map/all_to_all | solution.py:155
  88.5 32.5 %attention.1 = (bf16[32,128,128]{2,1,0:T(8,128)(2,1)}, bf16[32,256,128]{2,1,0:T(8,128)(2,1)S(1)}) custom-call(bf16[32,528,128]{2,1,0:T(8,128)(2,1)} %all-to-all-done.x_ref), custom_call_target="tpu_custom_call" | custom-call | tf_op jit(solution)/shard_map/attention/pallas_call | solution.py:110
  121.0 35.2 %all_to_all.25 = bf16[32,256,128]{2,1,0:T(8,128)(2,1)} all-to-all(bf16[32,256,128]{2,1,0:T(8,128)(2,1)S(1)} %get-tuple-element.6), channel_id=1, replica_groups=mesh['seq'=32,'dp'=4] {'seq'}, dimensions={0} | all-to-all | bytes 4194304 | tf_op jit(solution)/shard_map/all_to_all | solution.py:158
  156.1 3.9 %all-to-all-start.1 = ((bf16[32,128,128]{2,1,0:T(8,128)(2,1)}), bf16[32,128,128]{2,1,0:T(8,128)(2,1)S(1)}, u32[]{:S(2)}, u32[]{:S(2)}) async-start(bf16[32,128,128]{2,1,0:T(8,128)(2,1)} %get-tuple-element.5), calls=%async_computation.1 | async-start | bytes 2097152 | tf_op jit(solution)/shard_map/all_to_all | solution.py:159
  160.1 1.9 reduce
  162.3 14.0 %all_gather.4 = bf16[4,128,512]{2,1,0:T(8,128)(2,1)S(1)} all-gather(bf16[1,128,512]{2,1,0:T(8,128)(2,1)S(1)} %copy.50), channel_id=1, replica_groups=mesh['seq'=32,'dp'=4] {'dp'}, dimensions={0}, use_global_device_ids=true | all-gather | bytes 655360 | tf_op jit(solution)/shard_map/all_gather | solution.py:166
  176.3 0.8 fusion
  177.1 1.3 copy.48
  178.8 7.5 %all-to-all-start.4 = ((bf16[32,32,512]{2,1,0:T(8,128)(2,1)}), bf16[32,32,512]{2,1,0:T(8,128)(2,1)S(1)}, u32[]{:S(2)}, u32[]{:S(2)}) async-start(bf16[32,32,512]{2,1,0:T(8,128)(2,1)} %bitcast.20), calls=%async_computation.4 | async-start | bytes 2097152 | tf_op jit(solution)/shard_map/all_to_all | solution.py:169
  186.2 0.7 copy.42
  186.9 1.3 copy.49
  188.2 17.5 %all-to-all-done.4 = bf16[32,32,512]{2,1,0:T(8,128)(2,1)S(1)} async-done(((bf16[32,32,512]{2,1,0:T(8,128)(2,1)}), bf16[32,32,512]{2,1,0:T(8,128)(2,1)S(1)}, u32[]{:S(2)}, u32[]{:S(2)}) %all-to-all-start.4) | async-done | bytes 1048608 | tf_op jit(solution)/shard_map/all_to_all | solution.py:169
  205.8 0.8 convert_reduce_fusion
  (23 shorter events, 2.6 us)
Async XLA Ops:
  0.6 3.6 %copy-start = (bf16[1,128,4096]{2,1,0:T(8,128)(2,1)S(1)}, bf16[1,128,4096]{2,1,0:T(8,128)(2,1)}, u32[]{:S(2)}) copy-start(bf16[1,128,4096]{2,1,0:T(8,128)(2,1)} %param.8) | copy-start | bytes 3145732
  2.4 3.2 %copy-start.3 = (bf16[1,128,512]{2,1,0:T(8,128)(2,1)S(1)}, bf16[1,128,512]{2,1,0:T(8,128)(2,1)}, u32[]{:S(2)}) copy-start(bf16[1,128,512]{2,1,0:T(8,128)(2,1)} %param.7) | copy-start | bytes 393220
  2.4 3.4 %copy-start.4 = (s32[1,128]{1,0:T(1,128)S(1)}, s32[1,128]{1,0:T(1,128)}, u32[]{:S(2)}) copy-start(s32[1,128]{1,0:T(1,128)} %param.9) | copy-start | bytes 1540
  10.6 11.0 %copy-start.1 = (bf16[1,128,4096]{2,1,0:T(8,128)(2,1)S(1)}, bf16[1,128,4096]{2,1,0:T(8,128)(2,1)}, u32[]{:S(2)}) copy-start(bf16[1,128,4096]{2,1,0:T(8,128)(2,1)} %param.5) | copy-start | bytes 3145732
  10.6 74.4 %all-to-all-start = ((bf16[32,528,128]{2,1,0:T(8,128)(2,1)}), bf16[32,528,128]{2,1,0:T(8,128)(2,1)}, u32[]{:S(2)}, u32[]{:S(2)}) async-start(bf16[32,528,128]{2,1,0:T(8,128)(2,1)} %broadcast_dynamic-update-slice_fusion), calls=%async_computation | async-start | bytes 8650752 | tf_op jit(solution)/shard_map/all_to_all | solution.py:150
  84.9 36.0 %all-to-all-start.3 = ((bf16[4,1024,128]{2,1,0:T(8,128)(2,1)}), bf16[4,1024,128]{2,1,0:T(8,128)(2,1)S(1)}, u32[]{:S(2)}, u32[]{:S(2)}) async-start(bf16[4,1024,128]{2,1,0:T(8,128)(2,1)} %bitcast.17), calls=%async_computation.3 | async-start | bytes 2097152 | tf_op jit(solution)/shard_map/all_to_all | solution.py:155
  156.1 22.7 %all-to-all-start.1 = ((bf16[32,128,128]{2,1,0:T(8,128)(2,1)}), bf16[32,128,128]{2,1,0:T(8,128)(2,1)S(1)}, u32[]{:S(2)}, u32[]{:S(2)}) async-start(bf16[32,128,128]{2,1,0:T(8,128)(2,1)} %get-tuple-element.5), calls=%async_computation.1 | async-start | bytes 2097152 | tf_op jit(solution)/shard_map/all_to_all | solution.py:159
  162.3 24.6 %copy-start.2 = (bf16[1,128,512]{2,1,0:T(8,128)(2,1)}, bf16[1,128,512]{2,1,0:T(8,128)(2,1)S(1)}, u32[]{:S(2)}) copy-start(bf16[1,128,512]{2,1,0:T(8,128)(2,1)S(1)} %copy.50) | copy-start | bytes 393220
  178.8 27.0 %all-to-all-start.4 = ((bf16[32,32,512]{2,1,0:T(8,128)(2,1)}), bf16[32,32,512]{2,1,0:T(8,128)(2,1)S(1)}, u32[]{:S(2)}, u32[]{:S(2)}) async-start(bf16[32,32,512]{2,1,0:T(8,128)(2,1)} %bitcast.20), calls=%async_computation.4 | async-start | bytes 2097152 | tf_op jit(solution)/shard_map/all_to_all | solution.py:169

commit v2 on v1

v2 whole, which is shorter than its diff:
```python
import jax
import jax.numpy as jnp
from jax import lax
from jax.experimental import pallas as pl
from jax.experimental.pallas import tpu as pltpu
from jax.sharding import PartitionSpec as P

HQ = 32
HK = 2
DH = 128
SCALE = DH ** -0.5
EXP2_SCALE = SCALE * 1.4426950408889634
MASKED = -1e30
LOWEST = -1e29
SEGMENT_ROWS = 16
BQ = 512
UNIT = 512
CHUNKS = (4, 2, 1)
VMEM_LIMIT = 48 * 1024 * 1024
NT = (((1,), (1,)), ((), ()))
NN = (((1,), (0,)), ((), ()))
TN = (((0,), (0,)), ((), ()))


def dot(a, b, dims):
    return lax.dot_general(a, b, dims, preferred_element_type=jnp.float32)


def attention_kernel(x_ref, out_ref, p_ref, dp_ref, m_ref, dk_ref, dv_ref):
    blocks = x_ref.shape[0]
    seq = blocks * 128
    qn, un = BQ // 128, UNIT // 128

    def rows(first, count, slot):
        part = x_ref[pl.ds(first, count), slot * 128 : (slot + 1) * 128, :]
        return part.reshape(count * 128, DH)

    segments = x_ref[:, 512:513, :].astype(jnp.float32)
    count0 = jnp.sum(jnp.where(segments < 0.5, 1.0, 0.0)).astype(jnp.int32)
    count1 = jnp.sum(jnp.where(segments < 1.5, 1.0, 0.0)).astype(jnp.int32)

    def start_of(pos):
        return jnp.where(pos >= count1, count1, jnp.where(pos >= count0, count0, 0))

    dk_ref[...] = jnp.zeros_like(dk_ref)
    dv_ref[...] = jnp.zeros_like(dv_ref)

    def query_block(i, _):
        first = i * BQ
        q = rows(i * qn, qn, 0)
        cotan = rows(i * qn, qn, 1)
        qpos = first + lax.broadcasted_iota(jnp.int32, (1, BQ), 1)
        qstart = start_of(qpos)
        low = start_of(first) // UNIT
        high = (first + BQ - 1) // UNIT + 1

        def walk(body, state):
            at = low
            for size in CHUNKS:
                count = (high - at) // size

                def step(t, carry, size=size, at=at):
                    return body(at + t * size, size, carry)

                state = lax.fori_loop(0, count, step, state)
                at = at + count * size
            return state

        def scores(kb, size, carry):
            top, total, delta = carry
            k = rows(kb * un, size * un, 2)
            v = rows(kb * un, size * un, 3)
            st = dot(k, q, NT)
            dpt = dot(v, cotan, NT)
            at = pl.ds(pl.multiple_of(kb * UNIT, UNIT), size * UNIT)
            kpos = kb * UNIT + lax.broadcasted_iota(jnp.int32, (size * UNIT, BQ), 0)
            st = jnp.where((kpos >= qstart) & (kpos <= qpos), st, MASKED)
            newtop = jnp.maximum(top, jnp.max(st, axis=0, keepdims=True))
            p = jnp.exp2((st - newtop) * EXP2_SCALE)
            fade = jnp.exp2((top - newtop) * EXP2_SCALE)
            total = total * fade + jnp.sum(p, axis=0, keepdims=True)
            delta = delta * fade + jnp.sum(p * dpt, axis=0, keepdims=True)
            p_ref[at, :] = p
            dp_ref[at, :] = dpt
            m_ref[pl.ds(kb, 1), :] = newtop
            return newtop, total, delta

        zero = jnp.zeros((1, BQ), jnp.float32)
        top, total, delta = walk(scores, (zero + LOWEST, zero, zero))
        inverse = 1.0 / total
        delta = delta * inverse

        def grads(kb, size, dq):
            k = rows(kb * un, size * un, 2)
            at = pl.ds(pl.multiple_of(kb * UNIT, UNIT), size * UNIT)
            factor = jnp.exp2((m_ref[pl.ds(kb, 1), :] - top) * EXP2_SCALE) * inverse
            w = p_ref[at, :] * factor
            ds = (w * (dp_ref[at, :] - delta)).astype(jnp.bfloat16)
            dv_ref[at, :] += dot(w.astype(jnp.bfloat16), cotan, NN)
            dk_ref[at, :] += dot(ds, q, NN)
            return dq + dot(ds, k, TN)

        dq = walk(grads, jnp.zeros((BQ, DH), jnp.float32))
        out_ref[pl.ds(i * qn, qn), :128, :] = (
            (dq * SCALE).astype(jnp.bfloat16).reshape(qn, 128, DH)
        )
        return 0

    lax.fori_loop(0, seq // BQ, query_block, 0)

    def finish(b, _):
        at = pl.ds(pl.multiple_of(b * 128, 128), 128)
        out_ref[b, 128:256, :] = (dk_ref[at, :] * SCALE).astype(jnp.bfloat16)
        out_ref[b, 256:384, :] = dv_ref[at, :].astype(jnp.bfloat16)
        return 0

    lax.fori_loop(0, blocks, finish, 0)


def in_vmem(body, out_shape, inputs, scratch=(), name=None):
    spec = pl.BlockSpec(memory_space=pltpu.VMEM)
    many = isinstance(out_shape, tuple)
    return pl.pallas_call(
        body,
        out_shape=out_shape,
        in_specs=[spec] * len(inputs),
        out_specs=(spec,) * len(out_shape) if many else spec,
        scratch_shapes=list(scratch),
        compiler_params=pltpu.CompilerParams(vmem_limit_bytes=VMEM_LIMIT),
        name=name,
    )(*inputs)


def attention(x):
    blocks = x.shape[0]
    seq = blocks * 128
    scratch = [
        pltpu.VMEM((seq, BQ), jnp.float32),
        pltpu.VMEM((seq, BQ), jnp.float32),
        pltpu.VMEM((seq // UNIT, BQ), jnp.float32),
        pltpu.VMEM((seq, DH), jnp.float32),
        pltpu.VMEM((seq, DH), jnp.float32),
    ]
    out = jax.ShapeDtypeStruct((blocks, 384, DH), jnp.bfloat16)
    return in_vmem(attention_kernel, out, [x], scratch, "attention")


def pack_kernel(q_ref, g_ref, kv_ref, seg_ref, h_ref, send_ref, cols_ref):
    tokens = q_ref.shape[0]
    groups = HQ // HK
    dp, width = cols_ref.shape[0], cols_ref.shape[1]
    share = h_ref.shape[1] // (HQ * dp)
    numbers = jnp.broadcast_to(seg_ref[...].astype(jnp.bfloat16), (SEGMENT_ROWS, tokens))
    for h in range(HQ):
        at = slice(h * DH, (h + 1) * DH)
        k = (h // groups) * DH
        v = HK * DH + k
        send_ref[h, 0:128, :] = q_ref[:, at]
        send_ref[h, 128:256, :] = g_ref[:, at]
        send_ref[h, 256:384, :] = kv_ref[:, k : k + DH]
        send_ref[h, 384:512, :] = kv_ref[:, v : v + DH]
        send_ref[h, 512:528, :] = numbers
    span = share * dp
    for s in range(width // share):
        turned = h_ref[:, s * span : (s + 1) * span].T
        for r in range(dp):
            cols_ref[r, s * share : (s + 1) * share, :] = turned[r * share : (r + 1) * share]


def combine_kernel(part_ref, out_ref):
    groups = HQ // HK
    for g in range(HK):
        for kind in range(2):
            total = jnp.zeros((128, DH), jnp.float32)
            for h in range(g * groups, (g + 1) * groups):
                total += part_ref[h, (kind + 1) * 128 : (kind + 2) * 128, :].astype(jnp.float32)
            at = (kind * HK + g) * DH
            out_ref[:, at : at + DH] = total.astype(jnp.bfloat16)


def weight_kernel(cols_ref, kv_ref, out_ref):
    seq, share = out_ref.shape[0], out_ref.shape[1]
    total = dot(cols_ref[0], kv_ref[0], NN)
    for r in range(1, cols_ref.shape[0]):
        total += dot(cols_ref[r], kv_ref[r], NN)
    out_ref[...] = total.astype(jnp.bfloat16).reshape(seq, share, total.shape[1])


def unpack_kernel(part_ref, out_ref):
    for h in range(HQ):
        out_ref[:, h * DH : (h + 1) * DH] = part_ref[h, :128, :]


def total_kernel(part_ref, out_ref):
    total = part_ref[0].astype(jnp.float32)
    for s in range(1, part_ref.shape[0]):
        total += part_ref[s].astype(jnp.float32)
    out_ref[...] = total


def exchange(array, axis):
    return lax.all_to_all(array, axis, split_axis=0, concat_axis=0, tiled=True)


def shards(hidden, queries, keyvals, out_grad, segment):
    seq, dp = lax.axis_size("seq"), lax.axis_size("dp")
    tokens, width = hidden.shape[1], hidden.shape[2]
    share = width // (seq * dp)
    half = jnp.bfloat16
    shape = jax.ShapeDtypeStruct

    send, columns = in_vmem(
        pack_kernel,
        (shape((HQ, 4 * tokens + SEGMENT_ROWS, DH), half), shape((dp, seq * share, tokens), half)),
        [queries[0], out_grad[0], keyvals[0], segment, hidden[0]],
        name="pack",
    )
    mine = exchange(send, "seq")
    columns = exchange(columns, "dp")
    back = exchange(attention(mine), "seq")
    keyval_grad = in_vmem(
        combine_kernel, shape((tokens, 2 * HK * DH), half), [back], name="combine"
    )
    every = lax.all_gather(keyval_grad, "dp", axis=0)
    partial = in_vmem(
        weight_kernel, shape((seq, share, 2 * HK * DH), half), [columns, every], name="weight"
    )
    partial = exchange(partial, "seq")
    query_grad = in_vmem(unpack_kernel, shape((tokens, HQ * DH), half), [back], name="unpack")
    weight_grad = in_vmem(
        total_kernel, shape((share, 2 * HK * DH), jnp.float32), [partial], name="total"
    )
    return (query_grad[None], keyval_grad[None], weight_grad)


def solution(mesh):
    in_specs = (
        P("dp", "seq", None),
        P("dp", "seq", None),
        P("dp", "seq", None),
        P("dp", "seq", None),
        P("dp", "seq"),
    )
    out_specs = (P("dp", "seq", None), P("dp", "seq", None), P(("seq", "dp"), None))
    return jax.shard_map(shards, mesh=mesh, in_specs=in_specs, out_specs=out_specs, check_vma=False)
```

time: 208 us -> 205 us (0.986); the launches traced: 207 us -> 201 us
  blocking collectives: 49.2 us -> 127 us
  waiting for transfers between devices: 79.4 us -> 18.5 us
  starting transfers between devices: 25.9 us -> 8.92 us
  local copies, waits for them, and re-layouts: 15.2 us -> 8.23 us
  Pallas kernels: 32.5 us -> 38.1 us
  other arithmetic: 2.73 us -> 0 us
    all_to_all x1 -> x2, blocking collectives: 35.2 us -> 109 us  [exchange(): return lax.all_to_all(array, axis, split_axis=0, concat_axis=0, tiled=True)]
    all_to_all x4 -> x2, waiting for transfers between devices: 79.4 us -> 18.5 us  [exchange(): return lax.all_to_all(array, axis, split_axis=0, concat_axis=0, tiled=True)]
    all_to_all x4 -> x2, starting transfers between devices: 25.9 us -> 8.92 us  [exchange(): return lax.all_to_all(array, axis, split_axis=0, concat_axis=0, tiled=True)]
    pallas_call x1 -> x6, Pallas kernels: 32.5 us -> 38.1 us  [in_vmem(): pl.pallas_call(body, out_shape=out_shape, in_specs=[spec] * len(inputs),...]
    all_gather x1, blocking collectives: 14 us -> 17.6 us  [shards(): every = lax.all_gather(keyval_grad, 'dp', axis=0)]
    reduce_sum x2 -> x0, other arithmetic: 2.72 us -> none  [the longest x1 1.94 us: shards(): jnp.sum(dkv.reshape(HK, groups, 2, tokens, DH).astype(jnp.float32), axis=1)]
    unnamed x19 -> x16, local copies, waits for them, and re-layouts: 9.27 us -> 8.23 us
  transfers between devices with their start and end apart: 4 -> 2, of which waited for: 3 -> 1; matrix products, arithmetic and copies ran while one was open for 4% -> 0% of each run, Pallas kernels for 16% -> 1%
where the time goes in v2:
time: 205 us; the launch traced here: 201 us
  blocking collectives  127 us (62%)
  Pallas kernels  38.1 us (19%)
  waiting for transfers between devices  18.5 us (9%)
  starting transfers between devices  8.92 us (4%)
  local copies, waits for them, and re-layouts  8.23 us (4%)
    all_to_all x2, blocking collectives, exchange(): return lax.all_to_all(array, axis, split_axis=0, concat_axis=0, tiled=True)  109 us
    pallas_call x6, Pallas kernels, in_vmem(): pl.pallas_call(body, out_shape=out_shape, in_specs=[spec] * len(inputs),...  38.1 us
    all_to_all x2, waiting for transfers between devices, exchange(): return lax.all_to_all(array, axis, split_axis=0, concat_axis=0, tiled=True)  18.5 us
    all_gather x1, blocking collectives, shards(): every = lax.all_gather(keyval_grad, 'dp', axis=0)  17.6 us
    all_to_all x2, starting transfers between devices, exchange(): return lax.all_to_all(array, axis, split_axis=0, concat_axis=0, tiled=True)  8.92 us
    unnamed x16, local copies, waits for them, and re-layouts  8.23 us
  transfers between devices with their start and end apart: 2, of which 1 were waited for; matrix products, arithmetic and copies ran while one was open for 0% of the time, Pallas kernels for 1%

profile of v2, /device:TPU:0, one launch (start us, length us, event | category | flops | bytes accessed | tf_op | source)
XLA Modules:
  0.0 201.2 jit_solution(9559018209309442062)
XLA Ops:
  0.6 0.0 copy-start.2
  0.6 1.2 copy-done.2
  1.9 0.0 copy-start.3
  1.9 1.2 copy-done.3
  3.1 1.2 copy-done.4
  4.3 0.9 copy-done.6
  5.2 0.7 copy-done.7
  5.9 2.9 %pack.1 = (bf16[32,528,128]{2,1,0:T(8,128)(2,1)}, bf16[4,1024,128]{2,1,0:T(8,128)(2,1)S(1)}) custom-call(bf16[128,4096]{1,0:T(8,128)(2,1)S(1)} %bitcast.8, bf16[128,4096]{1,0:T(8,128)(2,1)S(1)} %bitcast.9, bf16[128,512]{1,0:T(8,128)(2,1)S(1)} %bitcast.11, s32[1,128]{1,0:T(1,128)S(1)} %copy-done.7, bf16[128,4096]{1,0:T(8,128)(2,1)S(1)} %bitcast.10), custom_call_target="tpu_custom_call" | custom-call | tf_op jit(solution)/shard_map/pack/pallas_call | solution.py:123
  8.7 1.0 copy-done.5
  9.7 65.0 %all_to_all.20.x_ref = bf16[32,528,128]{2,1,0:T(8,128)(2,1)} all-to-all(bf16[32,528,128]{2,1,0:T(8,128)(2,1)} %get-tuple-element.5), channel_id=1, replica_groups=mesh['seq'=32,'dp'=4] {'seq'}, dimensions={0} | all-to-all | bytes 8650752 | tf_op jit(solution)/shard_map/all_to_all | solution.py:202
  74.7 28.6 %attention.1 = bf16[32,384,128]{2,1,0:T(8,128)(2,1)S(1)} custom-call(bf16[32,528,128]{2,1,0:T(8,128)(2,1)} %all_to_all.20.x_ref), custom_call_target="tpu_custom_call" | custom-call | tf_op jit(solution)/shard_map/attention/pallas_call | solution.py:123
  103.3 44.2 %all_to_all.21.part_ref = bf16[32,384,128]{2,1,0:T(8,128)(2,1)S(1)} all-to-all(bf16[32,384,128]{2,1,0:T(8,128)(2,1)S(1)} %attention.1), channel_id=1, replica_groups=mesh['seq'=32,'dp'=4] {'seq'}, dimensions={0} | all-to-all | bytes 6291456 | tf_op jit(solution)/shard_map/all_to_all | solution.py:202
  147.5 4.2 %all-to-all-start.2 = ((bf16[4,1024,128]{2,1,0:T(8,128)(2,1)}), bf16[4,1024,128]{2,1,0:T(8,128)(2,1)}, u32[]{:S(2)}, u32[]{:S(2)}) async-start(bf16[4,1024,128]{2,1,0:T(8,128)(2,1)} %copy-done.5), calls=%async_computation.2 | async-start | bytes 2097152 | tf_op jit(solution)/shard_map/all_to_all | solution.py:202
  151.7 0.9 combine.1
  152.7 17.6 %all-gather = bf16[512,512]{1,0:T(8,128)(2,1)} all-gather(bf16[128,512]{1,0:T(8,128)(2,1)} %combine.1), channel_id=2, replica_groups=mesh['seq'=32,'dp'=4] {'dp'}, dimensions={0}, use_global_device_ids=true | all-gather | bytes 655360 | tf_op jit(solution)/shard_map/all_gather | solution.py:224
  170.3 0.0 all-to-all-done.2.cols_ref
  170.3 1.0 copy-done.1
  171.3 2.4 %weight.1 = bf16[32,32,512]{2,1,0:T(8,128)(2,1)S(1)} custom-call(bf16[4,1024,128]{2,1,0:T(8,128)(2,1)} %all-to-all-done.2.cols_ref, bf16[4,128,512]{2,1,0:T(8,128)(2,1)S(1)} %bitcast.7), custom_call_target="tpu_custom_call" | custom-call | tf_op jit(solution)/shard_map/weight/pallas_call | solution.py:123
  173.8 0.0 copy-start
  173.8 1.0 copy-done
  174.8 4.7 %all-to-all-start.3 = ((bf16[32,32,512]{2,1,0:T(8,128)(2,1)}), bf16[32,32,512]{2,1,0:T(8,128)(2,1)}, u32[]{:S(2)}, u32[]{:S(2)}) async-start(bf16[32,32,512]{2,1,0:T(8,128)(2,1)} %copy-done), calls=%async_computation.3 | async-start | bytes 2097152 | tf_op jit(solution)/shard_map/all_to_all | solution.py:202
  179.5 1.2 unpack.1
  180.7 18.5 %all-to-all-done.3.part_ref = bf16[32,32,512]{2,1,0:T(8,128)(2,1)} async-done(((bf16[32,32,512]{2,1,0:T(8,128)(2,1)}), bf16[32,32,512]{2,1,0:T(8,128)(2,1)}, u32[]{:S(2)}, u32[]{:S(2)}) %all-to-all-start.3) | async-done | bytes 1048608 | tf_op jit(solution)/shard_map/all_to_all | solution.py:202
  199.2 2.0 total.1
  (5 shorter events, 0.0 us)
Async XLA Ops:
  0.6 1.2 copy-start.2
  1.9 1.2 copy-start.3
  3.1 1.2 copy-start.4
  4.3 0.9 copy-start.6
  5.2 0.7 copy-start.7
  8.7 1.0 copy-start.5
  147.5 22.8 %all-to-all-start.2 = ((bf16[4,1024,128]{2,1,0:T(8,128)(2,1)}), bf16[4,1024,128]{2,1,0:T(8,128)(2,1)}, u32[]{:S(2)}, u32[]{:S(2)}) async-start(bf16[4,1024,128]{2,1,0:T(8,128)(2,1)} %copy-done.5), calls=%async_computation.2 | async-start | bytes 2097152 | tf_op jit(solution)/shard_map/all_to_all | solution.py:202
  170.3 1.0 copy-start.1
  173.8 1.0 copy-start
  174.8 24.4 %all-to-all-start.3 = ((bf16[32,32,512]{2,1,0:T(8,128)(2,1)}), bf16[32,32,512]{2,1,0:T(8,128)(2,1)}, u32[]{:S(2)}, u32[]{:S(2)}) async-start(bf16[32,32,512]{2,1,0:T(8,128)(2,1)} %copy-done), calls=%async_computation.3 | async-start | bytes 2097152 | tf_op jit(solution)/shard_map/all_to_all | solution.py:202

commit v3 on v2

v3 whole, which is shorter than its diff:
```python
import jax
import jax.numpy as jnp
from jax import lax
from jax.experimental import pallas as pl
from jax.experimental.pallas import tpu as pltpu
from jax.sharding import PartitionSpec as P

HQ = 32
HK = 2
DH = 128
SCALE = DH ** -0.5
EXP2_SCALE = SCALE * 1.4426950408889634
MASKED = -1e30
LOWEST = -1e29
SEGMENT_ROWS = 16
BQ = 512
UNIT = 512
CHUNKS = (4, 2, 1)
VMEM_LIMIT = 127 * 512 * 1024
NT = (((1,), (1,)), ((), ()))
NN = (((1,), (0,)), ((), ()))
TN = (((0,), (0,)), ((), ()))


def dot(a, b, dims):
    return lax.dot_general(a, b, dims, preferred_element_type=jnp.float32)


def attention_kernel(
    x_hbm, out_hbm, x_ref, out_ref, p_ref, dp_ref, m_ref, dk_ref, dv_ref, sems, out_sems
):
    blocks = x_ref.shape[0]
    seq = blocks * 128
    qn, un = BQ // 128, UNIT // 128
    steps = seq // BQ

    def arrival(i):
        at = pl.ds(i * qn, qn)
        return pltpu.make_async_copy(x_hbm.at[at, :512], x_ref.at[at, :512], sems.at[i])

    def departure(i):
        at = pl.ds(i * qn, qn)
        return pltpu.make_async_copy(
            out_ref.at[at, :128], out_hbm.at[at, :128], out_sems.at[i]
        )

    def final(i):
        at = pl.ds(i * qn, qn)
        return pltpu.make_async_copy(
            out_ref.at[at, 128:], out_hbm.at[at, 128:], out_sems.at[steps + i]
        )

    numbers = pltpu.make_async_copy(x_hbm.at[:, 512:], x_ref.at[:, 512:], sems.at[steps])
    numbers.start()
    for i in range(steps):
        arrival(i).start()
    dk_ref[...] = jnp.zeros_like(dk_ref)
    dv_ref[...] = jnp.zeros_like(dv_ref)
    numbers.wait()

    def rows(first, count, slot):
        part = x_ref[pl.ds(first, count), slot * 128 : (slot + 1) * 128, :]
        return part.reshape(count * 128, DH)

    segments = x_ref[:, 512:513, :].astype(jnp.float32)
    count0 = jnp.sum(jnp.where(segments < 0.5, 1.0, 0.0)).astype(jnp.int32)
    count1 = jnp.sum(jnp.where(segments < 1.5, 1.0, 0.0)).astype(jnp.int32)

    def start_of(pos):
        return jnp.where(pos >= count1, count1, jnp.where(pos >= count0, count0, 0))

    def query_block(i, _):
        arrival(i).wait()
        first = i * BQ
        q = rows(i * qn, qn, 0)
        cotan = rows(i * qn, qn, 1)
        qpos = first + lax.broadcasted_iota(jnp.int32, (1, BQ), 1)
        qstart = start_of(qpos)
        low = start_of(first) // UNIT
        high = (first + BQ - 1) // UNIT + 1

        def walk(body, state):
            at = low
            for size in CHUNKS:
                count = (high - at) // size

                def step(t, carry, size=size, at=at):
                    return body(at + t * size, size, carry)

                state = lax.fori_loop(0, count, step, state)
                at = at + count * size
            return state

        def scores(kb, size, carry):
            top, total, delta = carry
            k = rows(kb * un, size * un, 2)
            v = rows(kb * un, size * un, 3)
            st = dot(k, q, NT)
            dpt = dot(v, cotan, NT)
            at = pl.ds(pl.multiple_of(kb * UNIT, UNIT), size * UNIT)
            kpos = kb * UNIT + lax.broadcasted_iota(jnp.int32, (size * UNIT, BQ), 0)
            st = jnp.where((kpos >= qstart) & (kpos <= qpos), st, MASKED)
            newtop = jnp.maximum(top, jnp.max(st, axis=0, keepdims=True))
            p = jnp.exp2((st - newtop) * EXP2_SCALE)
            fade = jnp.exp2((top - newtop) * EXP2_SCALE)
            total = total * fade + jnp.sum(p, axis=0, keepdims=True)
            delta = delta * fade + jnp.sum(p * dpt, axis=0, keepdims=True)
            p_ref[at, :] = p
            dp_ref[at, :] = dpt
            m_ref[pl.ds(kb, 1), :] = newtop
            return newtop, total, delta

        zero = jnp.zeros((1, BQ), jnp.float32)
        top, total, delta = walk(scores, (zero + LOWEST, zero, zero))
        inverse = 1.0 / total
        delta = delta * inverse

        def grads(kb, size, dq):
            k = rows(kb * un, size * un, 2)
            at = pl.ds(pl.multiple_of(kb * UNIT, UNIT), size * UNIT)
            factor = jnp.exp2((m_ref[pl.ds(kb, 1), :] - top) * EXP2_SCALE) * inverse
            w = p_ref[at, :] * factor
            ds = (w * (dp_ref[at, :] - delta)).astype(jnp.bfloat16)
            dv_ref[at, :] += dot(w.astype(jnp.bfloat16), cotan, NN)
            dk_ref[at, :] += dot(ds, q, NN)
            return dq + dot(ds, k, TN)

        dq = walk(grads, jnp.zeros((BQ, DH), jnp.float32))
        out_ref[pl.ds(i * qn, qn), :128, :] = (
            (dq * SCALE).astype(jnp.bfloat16).reshape(qn, 128, DH)
        )
        departure(i).start()
        return 0

    lax.fori_loop(0, steps, query_block, 0)

    def finish(i, _):
        for b in range(qn):
            at = pl.ds(pl.multiple_of((i * qn + b) * 128, 128), 128)
            out_ref[i * qn + b, 128:256, :] = (dk_ref[at, :] * SCALE).astype(jnp.bfloat16)
            out_ref[i * qn + b, 256:384, :] = dv_ref[at, :].astype(jnp.bfloat16)
        final(i).start()
        return 0

    lax.fori_loop(0, steps, finish, 0)
    for i in range(steps):
        departure(i).wait()
        final(i).wait()


def local(body, out_shape, inputs, scratch, name):
    spec = pl.BlockSpec(memory_space=pltpu.HBM)
    many = isinstance(out_shape, tuple)
    return pl.pallas_call(
        body,
        out_shape=out_shape,
        in_specs=[spec] * len(inputs),
        out_specs=(spec,) * len(out_shape) if many else spec,
        scratch_shapes=scratch,
        compiler_params=pltpu.CompilerParams(vmem_limit_bytes=VMEM_LIMIT),
        name=name,
    )(*inputs)


def attention(x):
    blocks = x.shape[0]
    seq = blocks * 128
    return pl.pallas_call(
        attention_kernel,
        out_shape=jax.ShapeDtypeStruct((blocks, 384, DH), jnp.bfloat16),
        in_specs=[pl.BlockSpec(memory_space=pltpu.HBM)],
        out_specs=pl.BlockSpec(memory_space=pltpu.HBM),
        scratch_shapes=[
            pltpu.VMEM(x.shape, jnp.bfloat16),
            pltpu.VMEM((blocks, 384, DH), jnp.bfloat16),
            pltpu.VMEM((seq, BQ), jnp.float32),
            pltpu.VMEM((seq, BQ), jnp.float32),
            pltpu.VMEM((seq // UNIT, BQ), jnp.float32),
            pltpu.VMEM((seq, DH), jnp.float32),
            pltpu.VMEM((seq, DH), jnp.float32),
            pltpu.SemaphoreType.DMA((seq // BQ + 1,)),
            pltpu.SemaphoreType.DMA((2 * seq // BQ,)),
        ],
        compiler_params=pltpu.CompilerParams(vmem_limit_bytes=VMEM_LIMIT),
        cost_estimate=pl.CostEstimate(
            flops=10 * 1000**3, bytes_accessed=8 * 1000**2, transcendentals=8 * 1000**2
        ),
        name="attention",
    )(x)


def pack_kernel(
    q_hbm, g_hbm, kv_hbm, seg_hbm, h_hbm, send_hbm, cols_hbm, seg_ref, h_ref, number_ref, cols_ref, sems
):
    tokens = q_hbm.shape[0]
    groups = HQ // HK
    dp, width = cols_ref.shape[0], cols_ref.shape[1]
    share = h_ref.shape[1] // (HQ * dp)
    rest = [
        pltpu.make_async_copy(seg_hbm, seg_ref, sems.at[4]),
        pltpu.make_async_copy(h_hbm, h_ref, sems.at[5]),
    ]
    for copy in rest:
        copy.start()
    copies = []
    for h in range(HQ):
        k = (h // groups) * DH
        sources = [(q_hbm, h * DH), (g_hbm, h * DH), (kv_hbm, k), (kv_hbm, HK * DH + k)]
        for slot, (source, first) in enumerate(sources):
            target = send_hbm.at[h, pl.ds(slot * tokens, tokens)]
            copies.append(
                pltpu.make_async_copy(source.at[:, pl.ds(first, DH)], target, sems.at[slot])
            )
    for copy in copies:
        copy.start()
    rest[0].wait()
    numbers = jnp.broadcast_to(seg_ref[...].astype(jnp.bfloat16), (SEGMENT_ROWS, tokens))
    for h in range(HQ):
        number_ref[h] = numbers
    rest.append(pltpu.make_async_copy(number_ref, send_hbm.at[:, 4 * tokens :], sems.at[6]))
    rest[2].start()
    rest[1].wait()
    span = share * dp
    for s in range(width // share):
        turned = h_ref[:, s * span : (s + 1) * span].T
        for r in range(dp):
            cols_ref[r, s * share : (s + 1) * share, :] = turned[r * share : (r + 1) * share]
    rest.append(pltpu.make_async_copy(cols_ref, cols_hbm, sems.at[7]))
    rest[3].start()
    for slot in range(4):
        whole = send_hbm.at[:, pl.ds(slot * tokens, tokens)]
        pltpu.make_async_copy(whole, whole, sems.at[slot]).wait()
    for copy in rest[2:]:
        copy.wait()


def combine_kernel(part_hbm, out_hbm, part_ref, out_ref, sems):
    groups = HQ // HK
    pieces = sems.shape[0] - 1
    some = HQ // pieces
    tokens = out_ref.shape[0]
    arrivals = []
    for j in range(pieces):
        at = pl.ds(j * some, some)
        arrivals.append(
            pltpu.make_async_copy(part_hbm.at[at, tokens:], part_ref.at[at], sems.at[j])
        )
    for copy in arrivals:
        copy.start()
    for g in range(HK):
        totals = [jnp.zeros((tokens, DH), jnp.float32)] * 2
        for h in range(g * groups, (g + 1) * groups):
            if h % some == 0:
                arrivals[h // some].wait()
            for kind in range(2):
                at = slice(kind * tokens, (kind + 1) * tokens)
                totals[kind] += part_ref[h, at, :].astype(jnp.float32)
        for kind in range(2):
            at = (kind * HK + g) * DH
            out_ref[:, at : at + DH] = totals[kind].astype(jnp.bfloat16)
    copy = pltpu.make_async_copy(out_ref, out_hbm, sems.at[pieces])
    copy.start()
    copy.wait()


def weight_kernel(cols_hbm, kv_hbm, out_hbm, cols_ref, kv_ref, out_ref, sems):
    parts, depth, _ = cols_ref.shape
    seq, share = out_ref.shape[0], out_ref.shape[1]
    rows, some = depth // parts, seq // parts
    first = pltpu.make_async_copy(kv_hbm, kv_ref, sems.at[2 * parts])
    first.start()
    arrivals, departures = [], []
    for j in range(parts):
        at, to = pl.ds(j * rows, rows), pl.ds(j * some, some)
        arrivals.append(
            pltpu.make_async_copy(cols_hbm.at[:, at], cols_ref.at[:, at], sems.at[j])
        )
        departures.append(
            pltpu.make_async_copy(out_ref.at[to], out_hbm.at[to], sems.at[parts + j])
        )
    for copy in arrivals:
        copy.start()
    first.wait()
    for j in range(parts):
        arrivals[j].wait()
        at = slice(j * rows, (j + 1) * rows)
        total = dot(cols_ref[0, at], kv_ref[0], NN)
        for r in range(1, parts):
            total += dot(cols_ref[r, at], kv_ref[r], NN)
        out_ref[j * some : (j + 1) * some] = total.astype(jnp.bfloat16).reshape(
            some, share, total.shape[1]
        )
        departures[j].start()
    for copy in departures:
        copy.wait()


def unpack_kernel(part_hbm, out_hbm, sem):
    tokens = out_hbm.shape[0]
    copies = []
    for h in range(HQ):
        target = out_hbm.at[:, pl.ds(h * DH, DH)]
        copies.append(pltpu.make_async_copy(part_hbm.at[h, pl.ds(0, tokens)], target, sem))
    for copy in copies:
        copy.start()
    pltpu.make_async_copy(out_hbm, out_hbm, sem).wait()


def total_kernel(part_hbm, out_hbm, part_ref, out_ref, sems):
    seq = part_ref.shape[0]
    pieces = sems.shape[0] - 1
    some = seq // pieces
    arrivals = []
    for j in range(pieces):
        at = pl.ds(j * some, some)
        arrivals.append(pltpu.make_async_copy(part_hbm.at[at], part_ref.at[at], sems.at[j]))
    for copy in arrivals:
        copy.start()
    total = jnp.zeros(out_ref.shape, jnp.float32)
    for j in range(pieces):
        arrivals[j].wait()
        for s in range(j * some, (j + 1) * some):
            total += part_ref[s].astype(jnp.float32)
    out_ref[...] = total
    copy = pltpu.make_async_copy(out_ref, out_hbm, sems.at[pieces])
    copy.start()
    copy.wait()


def exchange(array, axis):
    return lax.all_to_all(array, axis, split_axis=0, concat_axis=0, tiled=True)


def shards(hidden, queries, keyvals, out_grad, segment):
    seq, dp = lax.axis_size("seq"), lax.axis_size("dp")
    tokens, width = hidden.shape[1], hidden.shape[2]
    share = width // (seq * dp)
    half = jnp.bfloat16
    shape = jax.ShapeDtypeStruct

    inputs = [queries[0], out_grad[0], keyvals[0], segment, hidden[0]]
    send, columns = local(
        pack_kernel,
        (shape((HQ, 4 * tokens + SEGMENT_ROWS, DH), half), shape((dp, seq * share, tokens), half)),
        inputs,
        [
            pltpu.VMEM(segment.shape, segment.dtype),
            pltpu.VMEM(hidden.shape[1:], hidden.dtype),
            pltpu.VMEM((HQ, SEGMENT_ROWS, tokens), half),
            pltpu.VMEM((dp, seq * share, tokens), half),
            pltpu.SemaphoreType.DMA((8,)),
        ],
        "pack",
    )
    mine, columns = lax.optimization_barrier((exchange(send, "seq"), columns))
    columns = exchange(columns, "dp")
    grads, columns = lax.optimization_barrier((attention(mine), columns))
    back = exchange(grads, "seq")
    keyval_grad = local(
        combine_kernel,
        shape((tokens, 2 * HK * DH), half),
        [back],
        [
            pltpu.VMEM((HQ, 2 * tokens, DH), half),
            pltpu.VMEM((tokens, 2 * HK * DH), half),
            pltpu.SemaphoreType.DMA((9,)),
        ],
        "combine",
    )
    every = lax.all_gather(keyval_grad, "dp", axis=0)
    result = (seq, share, 2 * HK * DH)
    partial = local(
        weight_kernel,
        shape(result, half),
        [columns, every],
        [
            pltpu.VMEM(columns.shape, half),
            pltpu.VMEM(every.shape, half),
            pltpu.VMEM(result, half),
            pltpu.SemaphoreType.DMA((2 * dp + 1,)),
        ],
        "weight",
    )
    partial = exchange(partial, "seq")
    query_grad = local(
        unpack_kernel,
        shape((tokens, HQ * DH), half),
        [back],
        [pltpu.SemaphoreType.DMA],
        "unpack",
    )
    weight_grad = local(
        total_kernel,
        shape(result[1:], jnp.float32),
        [partial],
        [
            pltpu.VMEM(result, half),
            pltpu.VMEM(result[1:], jnp.float32),
            pltpu.SemaphoreType.DMA((5,)),
        ],
        "total",
    )
    return (query_grad[None], keyval_grad[None], weight_grad)


def solution(mesh):
    in_specs = (
        P("dp", "seq", None),
        P("dp", "seq", None),
        P("dp", "seq", None),
        P("dp", "seq", None),
        P("dp", "seq"),
    )
    out_specs = (P("dp", "seq", None), P("dp", "seq", None), P(("seq", "dp"), None))
    return jax.shard_map(shards, mesh=mesh, in_specs=in_specs, out_specs=out_specs, check_vma=False)
```

time: 205 us -> 332 us (1.62); the launches traced: 201 us -> 334 us
  Pallas kernels: 38.1 us -> 197 us
  waiting for transfers between devices: 18.5 us -> 0.01 us
  local copies, waits for them, and re-layouts: 8.23 us -> 0 us
    pallas_call x6, Pallas kernels: 38.1 us -> 197 us  [the longest x5 169 us: local(): pl.pallas_call(body, out_shape=out_shape, in_specs=[spec] * len(inputs),...]
    all_to_all x2, waiting for transfers between devices: 18.5 us -> 0.01 us  [exchange(): return lax.all_to_all(array, axis, split_axis=0, concat_axis=0, tiled=True)]
    unnamed x16 -> x0, local copies, waits for them, and re-layouts: 8.23 us -> none
  transfers between devices with their start and end apart: 2 -> 2, of which waited for: 1 -> 0; matrix products, arithmetic and copies ran while one was open for 0% -> 0% of each run, Pallas kernels for 1% -> 18%
where the time goes in v3:
time: 332 us; the launch traced here: 334 us
  Pallas kernels  197 us (59%)
  blocking collectives  126 us (38%)
  starting transfers between devices  9.57 us (3%)
    pallas_call x5, Pallas kernels, local(): pl.pallas_call(body, out_shape=out_shape, in_specs=[spec] * len(inputs),...  169 us
    all_to_all x2, blocking collectives, exchange(): return lax.all_to_all(array, axis, split_axis=0, concat_axis=0, tiled=True)  107 us
    pallas_call x1, Pallas kernels, attention(): pl.pallas_call(attention_kernel, out_shape=jax.ShapeDtypeStruct((blocks,...  28.3 us
    all_gather x1, blocking collectives, shards(): every = lax.all_gather(keyval_grad, 'dp', axis=0)  19.8 us
    all_to_all x2, starting transfers between devices, exchange(): return lax.all_to_all(array, axis, split_axis=0, concat_axis=0, tiled=True)  9.57 us
  transfers between devices with their start and end apart: 2, of which 0 were waited for; matrix products, arithmetic and copies ran while one was open for 0% of the time, Pallas kernels for 18%

profile of v3, /device:TPU:0, one launch (start us, length us, event | category | flops | bytes accessed | tf_op | source)
XLA Modules:
  0.0 333.8 jit_solution(11793272471930987205)
XLA Ops:
  0.6 128.2 %pack.1 = (bf16[32,528,128]{2,1,0:T(8,128)(2,1)}, bf16[4,1024,128]{2,1,0:T(8,128)(2,1)}) custom-call(bf16[128,4096]{1,0:T(8,128)(2,1)} %bitcast.8, bf16[128,4096]{1,0:T(8,128)(2,1)} %bitcast.9, bf16[128,512]{1,0:T(8,128)(2,1)} %bitcast.13, s32[1,128]{1,0:T(1,128)} %seg_hbm.1, bf16[128,4096]{1,0:T(8,128)(2,1)} %bitcast.10), custom_call_target="tpu_custom_call" | custom-call | tf_op jit(solution)/shard_map/pack/pallas_call | solution.py:154
  128.9 65.0 %all_to_all.20.x_hbm = bf16[32,528,128]{2,1,0:T(8,128)(2,1)} all-to-all(bf16[32,528,128]{2,1,0:T(8,128)(2,1)} %get-tuple-element.9), channel_id=1, replica_groups=mesh['seq'=32,'dp'=4] {'seq'}, dimensions={0} | all-to-all | bytes 8650752 | tf_op jit(solution)/shard_map/all_to_all | solution.py:331
  193.9 4.2 %all-to-all-start.1 = ((bf16[4,1024,128]{2,1,0:T(8,128)(2,1)}), bf16[4,1024,128]{2,1,0:T(8,128)(2,1)}, u32[]{:S(2)}, u32[]{:S(2)}) async-start(bf16[4,1024,128]{2,1,0:T(8,128)(2,1)} %get-tuple-element.12), calls=%async_computation.1 | async-start | bytes 2097152 | tf_op jit(solution)/shard_map/all_to_all | solution.py:331
  198.1 28.3 %attention.1 = bf16[32,384,128]{2,1,0:T(8,128)(2,1)} custom-call(bf16[32,528,128]{2,1,0:T(8,128)(2,1)} %all_to_all.20.x_hbm), custom_call_target="tpu_custom_call" | custom-call | flops 10000000000 | bytes 8000000 | tf_op jit(solution)/shard_map/attention/pallas_call | solution.py:168
  226.5 0.0 all-to-all-done.1.cols_hbm
  226.5 41.6 %all_to_all.21.part_hbm = bf16[32,384,128]{2,1,0:T(8,128)(2,1)} all-to-all(bf16[32,384,128]{2,1,0:T(8,128)(2,1)} %attention.1), channel_id=1, replica_groups=mesh['seq'=32,'dp'=4] {'seq'}, dimensions={0} | all-to-all | bytes 6291456 | tf_op jit(solution)/shard_map/all_to_all | solution.py:331
  268.1 2.3 combine.1
  270.4 19.8 %all-gather = bf16[512,512]{1,0:T(8,128)(2,1)} all-gather(bf16[128,512]{1,0:T(8,128)(2,1)} %combine.1), channel_id=2, replica_groups=mesh['seq'=32,'dp'=4] {'dp'}, dimensions={0}, use_global_device_ids=true | all-gather | bytes 655360 | tf_op jit(solution)/shard_map/all_gather | solution.py:370
  290.1 3.6 %weight.1 = bf16[32,32,512]{2,1,0:T(8,128)(2,1)} custom-call(bf16[4,1024,128]{2,1,0:T(8,128)(2,1)} %all-to-all-done.1.cols_hbm, bf16[4,128,512]{2,1,0:T(8,128)(2,1)} %bitcast.7), custom_call_target="tpu_custom_call" | custom-call | tf_op jit(solution)/shard_map/weight/pallas_call | solution.py:154
  293.7 5.3 %all-to-all-start.3 = ((bf16[32,32,512]{2,1,0:T(8,128)(2,1)}), bf16[32,32,512]{2,1,0:T(8,128)(2,1)}, u32[]{:S(2)}, u32[]{:S(2)}) async-start(bf16[32,32,512]{2,1,0:T(8,128)(2,1)} %weight.1), calls=%async_computation.3 | async-start | bytes 2097152 | tf_op jit(solution)/shard_map/all_to_all | solution.py:331
  299.1 32.9 %unpack.1 = bf16[128,4096]{1,0:T(8,128)(2,1)} custom-call(bf16[32,384,128]{2,1,0:T(8,128)(2,1)} %all_to_all.21.part_hbm), custom_call_target="tpu_custom_call" | custom-call | tf_op jit(solution)/shard_map/unpack/pallas_call | solution.py:154
  331.9 0.0 all-to-all-done.3.part_hbm
  331.9 1.9 total.1
Async XLA Ops:
  193.9 32.6 %all-to-all-start.1 = ((bf16[4,1024,128]{2,1,0:T(8,128)(2,1)}), bf16[4,1024,128]{2,1,0:T(8,128)(2,1)}, u32[]{:S(2)}, u32[]{:S(2)}) async-start(bf16[4,1024,128]{2,1,0:T(8,128)(2,1)} %get-tuple-element.12), calls=%async_computation.1 | async-start | bytes 2097152 | tf_op jit(solution)/shard_map/all_to_all | solution.py:331
  293.7 38.2 %all-to-all-start.3 = ((bf16[32,32,512]{2,1,0:T(8,128)(2,1)}), bf16[32,32,512]{2,1,0:T(8,128)(2,1)}, u32[]{:S(2)}, u32[]{:S(2)}) async-start(bf16[32,32,512]{2,1,0:T(8,128)(2,1)} %weight.1), calls=%async_computation.3 | async-start | bytes 2097152 | tf_op jit(solution)/shard_map/all_to_all | solution.py:331

commit v4 on v3

--- a/solution.py
+++ b/solution.py
@@ -190,47 +190,48 @@
 
 
 def pack_kernel(
-    q_hbm, g_hbm, kv_hbm, seg_hbm, h_hbm, send_hbm, cols_hbm, seg_ref, h_ref, number_ref, cols_ref, sems
+    q_hbm, g_hbm, kv_hbm, seg_hbm, h_hbm, send_hbm, cols_hbm, *scratch
 ):
-    tokens = q_hbm.shape[0]
+    q_ref, g_ref, kv_ref, seg_ref, h_ref, send_ref, cols_ref, in_sems, out_sems = scratch
+    pairs = [(seg_hbm, seg_ref), (kv_hbm, kv_ref), (q_hbm, q_ref), (g_hbm, g_ref), (h_hbm, h_ref)]
+    arrivals = [pltpu.make_async_copy(*pair, in_sems.at[i]) for i, pair in enumerate(pairs)]
+    for copy in arrivals:
+        copy.start()
+    tokens = q_ref.shape[0]
     groups = HQ // HK
     dp, width = cols_ref.shape[0], cols_ref.shape[1]
     share = h_ref.shape[1] // (HQ * dp)
-    rest = [
-        pltpu.make_async_copy(seg_hbm, seg_ref, sems.at[4]),
-        pltpu.make_async_copy(h_hbm, h_ref, sems.at[5]),
-    ]
-    for copy in rest:
-        copy.start()
-    copies = []
+    bounds = [(2 * tokens, 4 * tokens + SEGMENT_ROWS), (0, tokens), (tokens, 2 * tokens)]
+    departures = []
+    for i, (first, last) in enumerate(bounds):
+        at = pl.ds(first, last - first)
+        departures.append(
+            pltpu.make_async_copy(send_ref.at[:, at], send_hbm.at[:, at], out_sems.at[i])
+        )
+    departures.append(pltpu.make_async_copy(cols_ref, cols_hbm, out_sems.at[3]))
+    arrivals[0].wait()
+    numbers = jnp.broadcast_to(seg_ref[...].astype(jnp.bfloat16), (SEGMENT_ROWS, tokens))
+    arrivals[1].wait()
     for h in range(HQ):
         k = (h // groups) * DH
-        sources = [(q_hbm, h * DH), (g_hbm, h * DH), (kv_hbm, k), (kv_hbm, HK * DH + k)]
-        for slot, (source, first) in enumerate(sources):
-            target = send_hbm.at[h, pl.ds(slot * tokens, tokens)]
-            copies.append(
-                pltpu.make_async_copy(source.at[:, pl.ds(first, DH)], target, sems.at[slot])
-            )
-    for copy in copies:
-        copy.start()
-    rest[0].wait()
-    numbers = jnp.broadcast_to(seg_ref[...].astype(jnp.bfloat16), (SEGMENT_ROWS, tokens))
-    for h in range(HQ):
-        number_ref[h] = numbers
-    rest.append(pltpu.make_async_copy(number_ref, send_hbm.at[:, 4 * tokens :], sems.at[6]))
-    rest[2].start()
-    rest[1].wait()
+        v = HK * DH + k
+        send_ref[h, 2 * tokens : 3 * tokens, :] = kv_ref[:, k : k + DH]
+        send_ref[h, 3 * tokens : 4 * tokens, :] = kv_ref[:, v : v + DH]
+        send_ref[h, 4 * tokens :, :] = numbers
+    departures[0].start()
+    for slot, ref in ((0, q_ref), (1, g_ref)):
+        arrivals[2 + slot].wait()
+        for h in range(HQ):
+            send_ref[h, slot * tokens : (slot + 1) * tokens, :] = ref[:, h * DH : (h + 1) * DH]
+        departures[1 + slot].start()
+    arrivals[4].wait()
     span = share * dp
     for s in range(width // share):
         turned = h_ref[:, s * span : (s + 1) * span].T
         for r in range(dp):
             cols_ref[r, s * share : (s + 1) * share, :] = turned[r * share : (r + 1) * share]
-    rest.append(pltpu.make_async_copy(cols_ref, cols_hbm, sems.at[7]))
-    rest[3].start()
-    for slot in range(4):
-        whole = send_hbm.at[:, pl.ds(slot * tokens, tokens)]
-        pltpu.make_async_copy(whole, whole, sems.at[slot]).wait()
-    for copy in rest[2:]:
+    departures[3].start()
+    for copy in departures:
         copy.wait()
 
 
@@ -295,15 +296,16 @@
         copy.wait()
 
 
-def unpack_kernel(part_hbm, out_hbm, sem):
-    tokens = out_hbm.shape[0]
-    copies = []
+def unpack_kernel(part_hbm, out_hbm, part_ref, out_ref, sems):
+    tokens = out_ref.shape[0]
+    copy = pltpu.make_async_copy(part_hbm.at[:, :tokens], part_ref, sems.at[0])
+    copy.start()
+    copy.wait()
     for h in range(HQ):
-        target = out_hbm.at[:, pl.ds(h * DH, DH)]
-        copies.append(pltpu.make_async_copy(part_hbm.at[h, pl.ds(0, tokens)], target, sem))
-    for copy in copies:
-        copy.start()
-    pltpu.make_async_copy(out_hbm, out_hbm, sem).wait()
+        out_ref[:, h * DH : (h + 1) * DH] = part_ref[h]
+    copy = pltpu.make_async_copy(out_ref, out_hbm, sems.at[1])
+    copy.start()
+    copy.wait()
 
 
 def total_kernel(part_hbm, out_hbm, part_ref, out_ref, sems):
@@ -344,11 +346,15 @@
         (shape((HQ, 4 * tokens + SEGMENT_ROWS, DH), half), shape((dp, seq * share, tokens), half)),
         inputs,
         [
+            pltpu.VMEM(queries.shape[1:], half),
+            pltpu.VMEM(out_grad.shape[1:], half),
+            pltpu.VMEM(keyvals.shape[1:], half),
             pltpu.VMEM(segment.shape, segment.dtype),
-            pltpu.VMEM(hidden.shape[1:], hidden.dtype),
-            pltpu.VMEM((HQ, SEGMENT_ROWS, tokens), half),
+            pltpu.VMEM(hidden.shape[1:], half),
+            pltpu.VMEM((HQ, 4 * tokens + SEGMENT_ROWS, DH), half),
             pltpu.VMEM((dp, seq * share, tokens), half),
-            pltpu.SemaphoreType.DMA((8,)),
+            pltpu.SemaphoreType.DMA((5,)),
+            pltpu.SemaphoreType.DMA((4,)),
         ],
         "pack",
     )
@@ -386,7 +392,11 @@
         unpack_kernel,
         shape((tokens, HQ * DH), half),
         [back],
-        [pltpu.SemaphoreType.DMA],
+        [
+            pltpu.VMEM((HQ, tokens, DH), half),
+            pltpu.VMEM((tokens, HQ * DH), half),
+            pltpu.SemaphoreType.DMA((2,)),
+        ],
         "unpack",
     )
     weight_grad = local(

time: 332 us -> 191 us (0.58)
  Pallas kernels: 197 us -> 42.2 us
  waiting for transfers between devices: 0.01 us -> 17 us
  blocking collectives: 126 us -> 121 us
    pallas_call x5, Pallas kernels: 169 us -> 13.9 us  [local(): pl.pallas_call(body, out_shape=out_shape, in_specs=[spec] * len(inputs),...]
    all_to_all x2, waiting for transfers between devices: 0.01 us -> 17 us  [exchange(): return lax.all_to_all(array, axis, split_axis=0, concat_axis=0, tiled=True)]
    all_gather x1, blocking collectives: 19.8 us -> 13.9 us  [shards(): every = lax.all_gather(keyval_grad, 'dp', axis=0)]
  transfers between devices with their start and end apart: 2 -> 2, of which waited for: 0 -> 1; matrix products, arithmetic and copies ran while one was open for 0% -> 0% of each run, Pallas kernels for 18% -> 16%
where the time goes in v4:
time: 191 us; the launch traced here: 190 us
  blocking collectives  121 us (63%)
  Pallas kernels  42.2 us (22%)
  waiting for transfers between devices  17 us (9%)
  starting transfers between devices  9.58 us (5%)
    all_to_all x2, blocking collectives, exchange(): return lax.all_to_all(array, axis, split_axis=0, concat_axis=0, tiled=True)  107 us
    pallas_call x1, Pallas kernels, attention(): pl.pallas_call(attention_kernel, out_shape=jax.ShapeDtypeStruct((blocks,...  28.3 us
    all_to_all x2, waiting for transfers between devices, exchange(): return lax.all_to_all(array, axis, split_axis=0, concat_axis=0, tiled=True)  17 us
    all_gather x1, blocking collectives, shards(): every = lax.all_gather(keyval_grad, 'dp', axis=0)  13.9 us
    pallas_call x5, Pallas kernels, local(): pl.pallas_call(body, out_shape=out_shape, in_specs=[spec] * len(inputs),...  13.9 us
    all_to_all x2, starting transfers between devices, exchange(): return lax.all_to_all(array, axis, split_axis=0, concat_axis=0, tiled=True)  9.58 us
  transfers between devices with their start and end apart: 2, of which 1 were waited for; matrix products, arithmetic and copies ran while one was open for 0% of the time, Pallas kernels for 16%

profile of v4, /device:TPU:0, one launch (start us, length us, event | category | flops | bytes accessed | tf_op | source)
XLA Modules:
  0.0 190.0 jit_solution(1144458422702749285)
XLA Ops:
  0.6 3.7 %pack.1 = (bf16[32,528,128]{2,1,0:T(8,128)(2,1)}, bf16[4,1024,128]{2,1,0:T(8,128)(2,1)}) custom-call(bf16[128,4096]{1,0:T(8,128)(2,1)} %bitcast.8, bf16[128,4096]{1,0:T(8,128)(2,1)} %bitcast.9, bf16[128,512]{1,0:T(8,128)(2,1)} %bitcast.13, s32[1,128]{1,0:T(1,128)} %seg_hbm.1, bf16[128,4096]{1,0:T(8,128)(2,1)} %bitcast.10), custom_call_target="tpu_custom_call" | custom-call | tf_op jit(solution)/shard_map/pack/pallas_call | solution.py:154
  4.3 65.0 %all_to_all.20.x_hbm = bf16[32,528,128]{2,1,0:T(8,128)(2,1)} all-to-all(bf16[32,528,128]{2,1,0:T(8,128)(2,1)} %get-tuple-element.9), channel_id=1, replica_groups=mesh['seq'=32,'dp'=4] {'seq'}, dimensions={0} | all-to-all | bytes 8650752 | tf_op jit(solution)/shard_map/all_to_all | solution.py:333
  69.3 4.2 %all-to-all-start.1 = ((bf16[4,1024,128]{2,1,0:T(8,128)(2,1)}), bf16[4,1024,128]{2,1,0:T(8,128)(2,1)}, u32[]{:S(2)}, u32[]{:S(2)}) async-start(bf16[4,1024,128]{2,1,0:T(8,128)(2,1)} %get-tuple-element.12), calls=%async_computation.1 | async-start | bytes 2097152 | tf_op jit(solution)/shard_map/all_to_all | solution.py:333
  73.6 28.3 %attention.1 = bf16[32,384,128]{2,1,0:T(8,128)(2,1)} custom-call(bf16[32,528,128]{2,1,0:T(8,128)(2,1)} %all_to_all.20.x_hbm), custom_call_target="tpu_custom_call" | custom-call | flops 10000000000 | bytes 8000000 | tf_op jit(solution)/shard_map/attention/pallas_call | solution.py:168
  101.9 0.0 all-to-all-done.1.cols_hbm
  101.9 41.6 %all_to_all.21.part_hbm = bf16[32,384,128]{2,1,0:T(8,128)(2,1)} all-to-all(bf16[32,384,128]{2,1,0:T(8,128)(2,1)} %attention.1), channel_id=1, replica_groups=mesh['seq'=32,'dp'=4] {'seq'}, dimensions={0} | all-to-all | bytes 6291456 | tf_op jit(solution)/shard_map/all_to_all | solution.py:333
  143.5 2.3 %combine.1 = bf16[128,512]{1,0:T(8,128)(2,1)} custom-call(bf16[32,384,128]{2,1,0:T(8,128)(2,1)} %all_to_all.21.part_hbm), custom_call_target="tpu_custom_call" | custom-call | tf_op jit(solution)/shard_map/combine/pallas_call | solution.py:154
  145.8 13.9 %all-gather = bf16[512,512]{1,0:T(8,128)(2,1)} all-gather(bf16[128,512]{1,0:T(8,128)(2,1)} %combine.1), channel_id=2, replica_groups=mesh['seq'=32,'dp'=4] {'dp'}, dimensions={0}, use_global_device_ids=true | all-gather | bytes 655360 | tf_op jit(solution)/shard_map/all_gather | solution.py:376
  159.7 3.6 %weight.1 = bf16[32,32,512]{2,1,0:T(8,128)(2,1)} custom-call(bf16[4,1024,128]{2,1,0:T(8,128)(2,1)} %all-to-all-done.1.cols_hbm, bf16[4,128,512]{2,1,0:T(8,128)(2,1)} %bitcast.7), custom_call_target="tpu_custom_call" | custom-call | tf_op jit(solution)/shard_map/weight/pallas_call | solution.py:154
  163.3 5.3 %all-to-all-start.3 = ((bf16[32,32,512]{2,1,0:T(8,128)(2,1)}), bf16[32,32,512]{2,1,0:T(8,128)(2,1)}, u32[]{:S(2)}, u32[]{:S(2)}) async-start(bf16[32,32,512]{2,1,0:T(8,128)(2,1)} %weight.1), calls=%async_computation.3 | async-start | bytes 2097152 | tf_op jit(solution)/shard_map/all_to_all | solution.py:333
  168.7 2.5 %unpack.1 = bf16[128,4096]{1,0:T(8,128)(2,1)} custom-call(bf16[32,384,128]{2,1,0:T(8,128)(2,1)} %all_to_all.21.part_hbm), custom_call_target="tpu_custom_call" | custom-call | tf_op jit(solution)/shard_map/unpack/pallas_call | solution.py:154
  171.2 17.0 %all-to-all-done.3.part_hbm = bf16[32,32,512]{2,1,0:T(8,128)(2,1)} async-done(((bf16[32,32,512]{2,1,0:T(8,128)(2,1)}), bf16[32,32,512]{2,1,0:T(8,128)(2,1)}, u32[]{:S(2)}, u32[]{:S(2)}) %all-to-all-start.3) | async-done | bytes 1048608 | tf_op jit(solution)/shard_map/all_to_all | solution.py:333
  188.1 1.9 total.1
Async XLA Ops:
  69.3 32.6 %all-to-all-start.1 = ((bf16[4,1024,128]{2,1,0:T(8,128)(2,1)}), bf16[4,1024,128]{2,1,0:T(8,128)(2,1)}, u32[]{:S(2)}, u32[]{:S(2)}) async-start(bf16[4,1024,128]{2,1,0:T(8,128)(2,1)} %get-tuple-element.12), calls=%async_computation.1 | async-start | bytes 2097152 | tf_op jit(solution)/shard_map/all_to_all | solution.py:333
  163.3 24.8 %all-to-all-start.3 = ((bf16[32,32,512]{2,1,0:T(8,128)(2,1)}), bf16[32,32,512]{2,1,0:T(8,128)(2,1)}, u32[]{:S(2)}, u32[]{:S(2)}) async-start(bf16[32,32,512]{2,1,0:T(8,128)(2,1)} %weight.1), calls=%async_computation.3 | async-start | bytes 2097152 | tf_op jit(solution)/shard_map/all_to_all | solution.py:333

commit v5 on v4

--- a/solution.py
+++ b/solution.py
@@ -14,12 +14,12 @@
 LOWEST = -1e29
 SEGMENT_ROWS = 16
 BQ = 512
-UNIT = 512
+UNIT = 256
 CHUNKS = (4, 2, 1)
 VMEM_LIMIT = 127 * 512 * 1024
+SMALL_LIMIT = 20 * 1024 * 1024
 NT = (((1,), (1,)), ((), ()))
 NN = (((1,), (0,)), ((), ()))
-TN = (((0,), (0,)), ((), ()))
 
 
 def dot(a, b, dims):
@@ -27,7 +27,7 @@
 
 
 def attention_kernel(
-    x_hbm, out_hbm, x_ref, out_ref, p_ref, dp_ref, m_ref, dk_ref, dv_ref, sems, out_sems
+    x_hbm, out_hbm, x_ref, out_ref, p_ref, dp_ref, m_ref, dk_ref, dv_ref, kt_ref, sems, out_sems
 ):
     blocks = x_ref.shape[0]
     seq = blocks * 128
@@ -74,6 +74,9 @@
         first = i * BQ
         q = rows(i * qn, qn, 0)
         cotan = rows(i * qn, qn, 1)
+        for b in range(qn):
+            at = pl.ds(pl.multiple_of(first + b * 128, 128), 128)
+            kt_ref[:, at] = x_ref[i * qn + b, 256:384, :].T
         qpos = first + lax.broadcasted_iota(jnp.int32, (1, BQ), 1)
         qstart = start_of(qpos)
         low = start_of(first) // UNIT
@@ -116,16 +119,15 @@
         delta = delta * inverse
 
         def grads(kb, size, dq):
-            k = rows(kb * un, size * un, 2)
             at = pl.ds(pl.multiple_of(kb * UNIT, UNIT), size * UNIT)
             factor = jnp.exp2((m_ref[pl.ds(kb, 1), :] - top) * EXP2_SCALE) * inverse
             w = p_ref[at, :] * factor
             ds = (w * (dp_ref[at, :] - delta)).astype(jnp.bfloat16)
             dv_ref[at, :] += dot(w.astype(jnp.bfloat16), cotan, NN)
             dk_ref[at, :] += dot(ds, q, NN)
-            return dq + dot(ds, k, TN)
-
-        dq = walk(grads, jnp.zeros((BQ, DH), jnp.float32))
+            return dq + dot(kt_ref[:, at], ds, NN)
+
+        dq = walk(grads, jnp.zeros((DH, BQ), jnp.float32)).T
         out_ref[pl.ds(i * qn, qn), :128, :] = (
             (dq * SCALE).astype(jnp.bfloat16).reshape(qn, 128, DH)
         )
@@ -178,6 +180,7 @@
             pltpu.VMEM((seq // UNIT, BQ), jnp.float32),
             pltpu.VMEM((seq, DH), jnp.float32),
             pltpu.VMEM((seq, DH), jnp.float32),
+            pltpu.VMEM((DH, seq), jnp.bfloat16),
             pltpu.SemaphoreType.DMA((seq // BQ + 1,)),
             pltpu.SemaphoreType.DMA((2 * seq // BQ,)),
         ],
@@ -189,9 +192,9 @@
     )(x)
 
 
-def pack_kernel(
-    q_hbm, g_hbm, kv_hbm, seg_hbm, h_hbm, send_hbm, cols_hbm, *scratch
-):
+def pack_kernel(q_hbm, g_hbm, kv_hbm, seg_hbm, h_hbm, send_hbm, *rest):
+    cols_hbm, scratch = rest[:-9], rest[-9:]
+    mine = lax.axis_index("dp")
     q_ref, g_ref, kv_ref, seg_ref, h_ref, send_ref, cols_ref, in_sems, out_sems = scratch
     pairs = [(seg_hbm, seg_ref), (kv_hbm, kv_ref), (q_hbm, q_ref), (g_hbm, g_ref), (h_hbm, h_ref)]
     arrivals = [pltpu.make_async_copy(*pair, in_sems.at[i]) for i, pair in enumerate(pairs)]
@@ -208,7 +211,8 @@
         departures.append(
             pltpu.make_async_copy(send_ref.at[:, at], send_hbm.at[:, at], out_sems.at[i])
         )
-    departures.append(pltpu.make_async_copy(cols_ref, cols_hbm, out_sems.at[3]))
+    for k, target in enumerate(cols_hbm):
+        departures.append(pltpu.make_async_copy(cols_ref.at[k], target, out_sems.at[3 + k]))
     arrivals[0].wait()
     numbers = jnp.broadcast_to(seg_ref[...].astype(jnp.bfloat16), (SEGMENT_ROWS, tokens))
     arrivals[1].wait()
@@ -229,8 +233,10 @@
     for s in range(width // share):
         turned = h_ref[:, s * span : (s + 1) * span].T
         for r in range(dp):
-            cols_ref[r, s * share : (s + 1) * share, :] = turned[r * share : (r + 1) * share]
-    departures[3].start()
+            part = turned[r * share : (r + 1) * share]
+            cols_ref[jnp.bitwise_xor(mine, r), s * share : (s + 1) * share, :] = part
+    for copy in departures[3:]:
+        copy.start()
     for copy in departures:
         copy.wait()
 
@@ -264,30 +270,22 @@
     copy.wait()
 
 
-def weight_kernel(cols_hbm, kv_hbm, out_hbm, cols_ref, kv_ref, out_ref, sems):
-    parts, depth, _ = cols_ref.shape
+def weight_kernel(*refs):
+    *cols_ref, kv_ref, out_hbm, out_ref, sems = refs
+    mine = lax.axis_index("dp")
     seq, share = out_ref.shape[0], out_ref.shape[1]
-    rows, some = depth // parts, seq // parts
-    first = pltpu.make_async_copy(kv_hbm, kv_ref, sems.at[2 * parts])
-    first.start()
-    arrivals, departures = [], []
-    for j in range(parts):
-        at, to = pl.ds(j * rows, rows), pl.ds(j * some, some)
-        arrivals.append(
-            pltpu.make_async_copy(cols_hbm.at[:, at], cols_ref.at[:, at], sems.at[j])
-        )
+    pieces = sems.shape[0]
+    some = seq // pieces
+    departures = []
+    for j in range(pieces):
+        to = pl.ds(j * some, some)
         departures.append(
-            pltpu.make_async_copy(out_ref.at[to], out_hbm.at[to], sems.at[parts + j])
-        )
-    for copy in arrivals:
-        copy.start()
-    first.wait()
-    for j in range(parts):
-        arrivals[j].wait()
-        at = slice(j * rows, (j + 1) * rows)
-        total = dot(cols_ref[0, at], kv_ref[0], NN)
-        for r in range(1, parts):
-            total += dot(cols_ref[r, at], kv_ref[r], NN)
+            pltpu.make_async_copy(out_ref.at[to], out_hbm.at[to], sems.at[j])
+        )
+        at = slice(j * some * share, (j + 1) * some * share)
+        total = dot(cols_ref[0][at], kv_ref[mine], NN)
+        for r in range(1, len(cols_ref)):
+            total += dot(cols_ref[r][at], kv_ref[jnp.bitwise_xor(mine, r)], NN)
         out_ref[j * some : (j + 1) * some] = total.astype(jnp.bfloat16).reshape(
             some, share, total.shape[1]
         )
@@ -341,9 +339,10 @@
     shape = jax.ShapeDtypeStruct
 
     inputs = [queries[0], out_grad[0], keyvals[0], segment, hidden[0]]
-    send, columns = local(
+    column = shape((seq * share, tokens), half)
+    send, *columns = local(
         pack_kernel,
-        (shape((HQ, 4 * tokens + SEGMENT_ROWS, DH), half), shape((dp, seq * share, tokens), half)),
+        (shape((HQ, 4 * tokens + SEGMENT_ROWS, DH), half),) + (column,) * dp,
         inputs,
         [
             pltpu.VMEM(queries.shape[1:], half),
@@ -354,12 +353,13 @@
             pltpu.VMEM((HQ, 4 * tokens + SEGMENT_ROWS, DH), half),
             pltpu.VMEM((dp, seq * share, tokens), half),
             pltpu.SemaphoreType.DMA((5,)),
-            pltpu.SemaphoreType.DMA((4,)),
+            pltpu.SemaphoreType.DMA((3 + dp,)),
         ],
         "pack",
     )
     mine, columns = lax.optimization_barrier((exchange(send, "seq"), columns))
-    columns = exchange(columns, "dp")
+    for k in range(1, dp):
+        columns[k] = lax.ppermute(columns[k], "dp", [(r, r ^ k) for r in range(dp)])
     grads, columns = lax.optimization_barrier((attention(mine), columns))
     back = exchange(grads, "seq")
     keyval_grad = local(
@@ -375,18 +375,15 @@
     )
     every = lax.all_gather(keyval_grad, "dp", axis=0)
     result = (seq, share, 2 * HK * DH)
-    partial = local(
+    partial = pl.pallas_call(
         weight_kernel,
-        shape(result, half),
-        [columns, every],
-        [
-            pltpu.VMEM(columns.shape, half),
-            pltpu.VMEM(every.shape, half),
-            pltpu.VMEM(result, half),
-            pltpu.SemaphoreType.DMA((2 * dp + 1,)),
-        ],
-        "weight",
-    )
+        out_shape=shape(result, half),
+        in_specs=[pl.BlockSpec(memory_space=pltpu.VMEM)] * (dp + 1),
+        out_specs=pl.BlockSpec(memory_space=pltpu.HBM),
+        scratch_shapes=[pltpu.VMEM(result, half), pltpu.SemaphoreType.DMA((4,))],
+        compiler_params=pltpu.CompilerParams(vmem_limit_bytes=SMALL_LIMIT),
+        name="weight",
+    )(*columns, every)
     partial = exchange(partial, "seq")
     query_grad = local(
         unpack_kernel,

time: 191 us -> 187 us (0.979)
  starting transfers between devices: 9.58 us -> 6.54 us
    all_to_all x2 -> x1, starting transfers between devices: 9.58 us -> 4.68 us  [exchange(): return lax.all_to_all(array, axis, split_axis=0, concat_axis=0, tiled=True)]
    pallas_call x5 -> x4, Pallas kernels: 13.9 us -> 10.3 us  [local(): pl.pallas_call(body, out_shape=out_shape, in_specs=[spec] * len(inputs),...]
    pallas_call x0 -> x1, Pallas kernels: none -> 3.06 us  [shards(): pl.pallas_call(weight_kernel, out_shape=shape(result, half), in_specs=[pl...]
    all_to_all x2 -> x1, waiting for transfers between devices: 17 us -> 17.2 us  [exchange(): return lax.all_to_all(array, axis, split_axis=0, concat_axis=0, tiled=True)]
  transfers between devices with their start and end apart: 2 -> 4, of which waited for: 1 -> 1; matrix products, arithmetic and copies ran while one was open for 0% -> 0% of each run, Pallas kernels for 16% -> 17%
where the time goes in v5:
time: 187 us
  blocking collectives  120 us (64%)
  Pallas kernels  42.4 us (23%)
  waiting for transfers between devices  17.2 us (9%)
  starting transfers between devices  6.54 us (3%)
    all_to_all x2, blocking collectives, exchange(): return lax.all_to_all(array, axis, split_axis=0, concat_axis=0, tiled=True)  108 us
    pallas_call x1, Pallas kernels, attention(): pl.pallas_call(attention_kernel, out_shape=jax.ShapeDtypeStruct((blocks,...  29 us
    all_to_all x1, waiting for transfers between devices, exchange(): return lax.all_to_all(array, axis, split_axis=0, concat_axis=0, tiled=True)  17.2 us
    all_gather x1, blocking collectives, shards(): every = lax.all_gather(keyval_grad, 'dp', axis=0)  12.1 us
    pallas_call x4, Pallas kernels, local(): pl.pallas_call(body, out_shape=out_shape, in_specs=[spec] * len(inputs),...  10.3 us
    all_to_all x1, starting transfers between devices, exchange(): return lax.all_to_all(array, axis, split_axis=0, concat_axis=0, tiled=True)  4.68 us
  transfers between devices with their start and end apart: 4, of which 1 were waited for; matrix products, arithmetic and copies ran while one was open for 0% of the time, Pallas kernels for 17%

profile of v5, /device:TPU:0, one launch (start us, length us, event | category | flops | bytes accessed | tf_op | source)
XLA Modules:
  0.0 186.5 jit_solution(3678778158279409680)
XLA Ops:
  0.6 3.7 %pack.1 = (bf16[32,528,128]{2,1,0:T(8,128)(2,1)}, bf16[1024,128]{1,0:T(8,128)(2,1)}, bf16[1024,128]{1,0:T(8,128)(2,1)}, bf16[1024,128]{1,0:T(8,128)(2,1)}, bf16[1024,128]{1,0:T(8,128)(2,1)}) custom-call(bf16[128,4096]{1,0:T(8,128)(2,1)} %bitcast.8, bf16[128,4096]{1,0:T(8,128)(2,1)} %bitcast.9, bf16[128,512]{1,0:T(8,128)(2,1)} %bitcast.13, s32[1,128]{1,0:T(1,128)} %seg_hbm.1, ...), custom_call_target="tpu_custom_call" | custom-call | tf_op jit(solution)/shard_map/pack/pallas_call | solution.py:156
  4.3 65.0 %all_to_all.15.x_hbm = bf16[32,528,128]{2,1,0:T(8,128)(2,1)} all-to-all(bf16[32,528,128]{2,1,0:T(8,128)(2,1)} %get-tuple-element.18), channel_id=1, replica_groups=mesh['seq'=32,'dp'=4] {'seq'}, dimensions={0} | all-to-all | bytes 8650752 | tf_op jit(solution)/shard_map/all_to_all | solution.py:331
  69.3 0.0 collective-permute-start
  69.3 1.0 collective-permute-start.1
  70.4 0.8 collective-permute-start.2
  71.2 29.0 %attention.1 = bf16[32,384,128]{2,1,0:T(8,128)(2,1)} custom-call(bf16[32,528,128]{2,1,0:T(8,128)(2,1)} %all_to_all.15.x_hbm), custom_call_target="tpu_custom_call" | custom-call | flops 10000000000 | bytes 8000000 | tf_op jit(solution)/shard_map/attention/pallas_call | solution.py:170
  100.2 0.0 copy-start
  100.2 0.0 collective-permute-done.refs_1_
  100.2 0.0 collective-permute-done.1.refs_2_
  100.2 0.0 collective-permute-done.2.refs_3_
  100.2 42.5 %all_to_all.16.part_hbm = bf16[32,384,128]{2,1,0:T(8,128)(2,1)} all-to-all(bf16[32,384,128]{2,1,0:T(8,128)(2,1)} %attention.1), channel_id=1, replica_groups=mesh['seq'=32,'dp'=4] {'seq'}, dimensions={0} | all-to-all | bytes 6291456 | tf_op jit(solution)/shard_map/all_to_all | solution.py:331
  142.7 2.3 %combine.1 = bf16[128,512]{1,0:T(8,128)(2,1)} custom-call(bf16[32,384,128]{2,1,0:T(8,128)(2,1)} %all_to_all.16.part_hbm), custom_call_target="tpu_custom_call" | custom-call | tf_op jit(solution)/shard_map/combine/pallas_call | solution.py:156
  145.0 12.1 %all-gather = bf16[512,512]{1,0:T(8,128)(2,1)S(1)} all-gather(bf16[128,512]{1,0:T(8,128)(2,1)} %combine.1), channel_id=2, replica_groups=mesh['seq'=32,'dp'=4] {'dp'}, dimensions={0}, use_global_device_ids=true | all-gather | bytes 655360 | tf_op jit(solution)/shard_map/all_gather | solution.py:376
  157.1 0.0 copy-done
  157.1 3.1 %weight.1 = bf16[32,32,512]{2,1,0:T(8,128)(2,1)} custom-call(bf16[1024,128]{1,0:T(8,128)(2,1)S(1)} %copy-done, bf16[1024,128]{1,0:T(8,128)(2,1)} %collective-permute-done.refs_1_, bf16[1024,128]{1,0:T(8,128)(2,1)} %collective-permute-done.1.refs_2_, bf16[1024,128]{1,0:T(8,128)(2,1)} %collective-permute-done.2.refs_3_, bf16[4,128,512]{2,1,0:T(8,128)(2,1)S(1)} %bitcast.7), custom_call_target="tpu_custom_call" | custom-call | tf_op jit(solution)/shard_map/weight/pallas_call | solution.py:378
  160.2 4.7 %all-to-all-start.2 = ((bf16[32,32,512]{2,1,0:T(8,128)(2,1)}), bf16[32,32,512]{2,1,0:T(8,128)(2,1)}, u32[]{:S(2)}, u32[]{:S(2)}) async-start(bf16[32,32,512]{2,1,0:T(8,128)(2,1)} %weight.1), calls=%async_computation.2 | async-start | bytes 2097152 | tf_op jit(solution)/shard_map/all_to_all | solution.py:331
  164.9 2.5 %unpack.1 = bf16[128,4096]{1,0:T(8,128)(2,1)} custom-call(bf16[32,384,128]{2,1,0:T(8,128)(2,1)} %all_to_all.16.part_hbm), custom_call_target="tpu_custom_call" | custom-call | tf_op jit(solution)/shard_map/unpack/pallas_call | solution.py:156
  167.4 17.2 %all-to-all-done.2.part_hbm = bf16[32,32,512]{2,1,0:T(8,128)(2,1)} async-done(((bf16[32,32,512]{2,1,0:T(8,128)(2,1)}), bf16[32,32,512]{2,1,0:T(8,128)(2,1)}, u32[]{:S(2)}, u32[]{:S(2)}) %all-to-all-start.2) | async-done | bytes 1048608 | tf_op jit(solution)/shard_map/all_to_all | solution.py:331
  184.6 1.9 %total.1 = f32[32,512]{1,0:T(8,128)} custom-call(bf16[32,32,512]{2,1,0:T(8,128)(2,1)} %all-to-all-done.2.part_hbm), custom_call_target="tpu_custom_call" | custom-call | tf_op jit(solution)/shard_map/total/pallas_call | solution.py:156
Async XLA Ops:
  69.3 30.9 %collective-permute-start = (bf16[1024,128]{1,0:T(8,128)(2,1)}, bf16[1024,128]{1,0:T(8,128)(2,1)}, u32[]{:S(2)}, u32[]{:S(2)}) collective-permute-start(bf16[1024,128]{1,0:T(8,128)(2,1)} %get-tuple-element.25), channel_id=1, source_target_pairs={{0,1},{1,0},{2,3},{3,2},{4,5},{5,4},{6,7},{7,6},{8,9},{9,8},{10,11... | collective-permute-start | bytes 786440 | tf_op jit(solution)/shard_map/ppermute | solution.py:362
  69.3 30.9 %collective-permute-start.1 = (bf16[1024,128]{1,0:T(8,128)(2,1)}, bf16[1024,128]{1,0:T(8,128)(2,1)}, u32[]{:S(2)}, u32[]{:S(2)}) collective-permute-start(bf16[1024,128]{1,0:T(8,128)(2,1)} %get-tuple-element.26), channel_id=1, source_target_pairs={{0,2},{1,3},{2,0},{3,1},{4,6},{5,7},{6,4},{7,5},{8,10},{9,11},{10,... | collective-permute-start | bytes 786440 | tf_op jit(solution)/shard_map/ppermute | solution.py:362
  70.4 29.9 %collective-permute-start.2 = (bf16[1024,128]{1,0:T(8,128)(2,1)}, bf16[1024,128]{1,0:T(8,128)(2,1)}, u32[]{:S(2)}, u32[]{:S(2)}) collective-permute-start(bf16[1024,128]{1,0:T(8,128)(2,1)} %get-tuple-element.27), channel_id=1, source_target_pairs={{0,3},{1,2},{2,1},{3,0},{4,7},{5,6},{6,5},{7,4},{8,11},{9,10},{10,... | collective-permute-start | bytes 786440 | tf_op jit(solution)/shard_map/ppermute | solution.py:362
  100.2 56.9 %copy-start = (bf16[1024,128]{1,0:T(8,128)(2,1)S(1)}, bf16[1024,128]{1,0:T(8,128)(2,1)}, u32[]{:S(2)}) copy-start(bf16[1024,128]{1,0:T(8,128)(2,1)} %get-tuple-element.29.refs_0_) | copy-start | bytes 786436
  160.2 24.4 %all-to-all-start.2 = ((bf16[32,32,512]{2,1,0:T(8,128)(2,1)}), bf16[32,32,512]{2,1,0:T(8,128)(2,1)}, u32[]{:S(2)}, u32[]{:S(2)}) async-start(bf16[32,32,512]{2,1,0:T(8,128)(2,1)} %weight.1), calls=%async_computation.2 | async-start | bytes 2097152 | tf_op jit(solution)/shard_map/all_to_all | solution.py:331

commit v6 on v5

v6 whole, which is shorter than its diff:
```python
import jax
import jax.numpy as jnp
from jax import lax
from jax.experimental import pallas as pl
from jax.experimental.pallas import tpu as pltpu
from jax.sharding import PartitionSpec as P

HQ = 32
HK = 2
DH = 128
SCALE = DH ** -0.5
EXP2_SCALE = SCALE * 1.4426950408889634
MASKED = -1e30
LOWEST = -1e29
SEGMENT_ROWS = 16
BQ = 512
UNIT = 256
CHUNKS = (8, 4, 2, 1)
PLANES = 8
VMEM_LIMIT = 127 * 512 * 1024
SMALL_LIMIT = 20 * 1024 * 1024
NT = (((1,), (1,)), ((), ()))
NN = (((1,), (0,)), ((), ()))


def dot(a, b, dims):
    return lax.dot_general(a, b, dims, preferred_element_type=jnp.float32)


def attention_kernel(*refs):
    kv_hbm, q_hbm = refs[0], refs[1:5]
    dkv_hbm, dq_hbm = refs[5], refs[6:10]
    x_ref, seg_ref, q_ref, dq_ref, dkv_ref = refs[10:15]
    p_ref, dp_ref, m_ref, dk_ref, dv_ref, kt_ref, sems, out_sems = refs[15:]
    planes, lines = kv_hbm.shape[0], kv_hbm.shape[1]
    blocks = planes * lines
    seq = blocks * 128
    un = UNIT // 128
    mine = lax.axis_index("seq")
    line, plane = mine // planes, mine % planes

    arrivals = []
    for j in range(lines):
        at = pl.ds(j * planes, planes)
        arrivals.append(
            pltpu.make_async_copy(kv_hbm.at[:, j, 256:], seg_ref.at[at], sems.at[j])
        )
    for j in range(lines):
        at = pl.ds(j * planes, planes)
        arrivals.append(
            pltpu.make_async_copy(kv_hbm.at[:, j, :256], x_ref.at[at], sems.at[lines + j])
        )
    for j in range(lines):
        arrivals.append(pltpu.make_async_copy(q_hbm[j], q_ref.at[j], sems.at[2 * lines + j]))
    for copy in arrivals:
        copy.start()

    def departure(j):
        return pltpu.make_async_copy(dq_ref.at[j], dq_hbm[j], out_sems.at[j])

    def final(j):
        return pltpu.make_async_copy(dkv_ref.at[:, j], dkv_hbm.at[:, j], out_sems.at[lines + j])

    dk_ref[...] = jnp.zeros_like(dk_ref)
    dv_ref[...] = jnp.zeros_like(dv_ref)
    for copy in arrivals:
        copy.wait()

    def rows(first, count, slot):
        part = x_ref[pl.ds(first, count), slot * 128 : (slot + 1) * 128, :]
        return part.reshape(count * 128, DH)

    def turn(b, _):
        kt_ref[:, pl.ds(pl.multiple_of(b * 128, 128), 128)] = x_ref[b, :128, :].T
        return 0

    lax.fori_loop(0, blocks, turn, 0)
    segments = seg_ref[:, 0:1, :].astype(jnp.float32)
    count0 = jnp.sum(jnp.where(segments < 0.5, 1.0, 0.0)).astype(jnp.int32)
    count1 = jnp.sum(jnp.where(segments < 1.5, 1.0, 0.0)).astype(jnp.int32)

    def start_of(pos):
        return jnp.where(pos >= count1, count1, jnp.where(pos >= count0, count0, 0))

    heads = dq_ref.shape[1]
    some = BQ // 128
    turns = heads // some

    def query_block(i, _):
        j, part = i // turns, i % turns
        first = (jnp.bitwise_xor(line, j) * planes + plane) * 128
        q = q_ref[j, pl.ds(part * some, some)].reshape(BQ, DH)
        cotan = q_ref[j, pl.ds(heads + part * some, some)].reshape(BQ, DH)
        qpos = first + lax.broadcasted_iota(jnp.int32, (1, BQ), 1) % 128
        qstart = start_of(qpos)
        low = start_of(first) // UNIT
        high = (first + 127) // UNIT + 1

        def walk(body, state):
            at = low
            for size in CHUNKS:
                count = (high - at) // size

                def step(t, carry, size=size, at=at):
                    return body(at + t * size, size, carry)

                state = lax.fori_loop(0, count, step, state)
                at = at + count * size
            return state

        def scores(kb, size, carry):
            top, total, delta = carry
            k = rows(kb * un, size * un, 0)
            v = rows(kb * un, size * un, 1)
            st = dot(k, q, NT)
            dpt = dot(v, cotan, NT)
            at = pl.ds(pl.multiple_of(kb * UNIT, UNIT), size * UNIT)
            kpos = kb * UNIT + lax.broadcasted_iota(jnp.int32, (size * UNIT, BQ), 0)
            st = jnp.where((kpos >= qstart) & (kpos <= qpos), st, MASKED)
            newtop = jnp.maximum(top, jnp.max(st, axis=0, keepdims=True))
            p = jnp.exp2((st - newtop) * EXP2_SCALE)
            fade = jnp.exp2((top - newtop) * EXP2_SCALE)
            total = total * fade + jnp.sum(p, axis=0, keepdims=True)
            delta = delta * fade + jnp.sum(p * dpt, axis=0, keepdims=True)
            p_ref[at, :] = p
            dp_ref[at, :] = dpt
            m_ref[pl.ds(kb, 1), :] = newtop
            return newtop, total, delta

        zero = jnp.zeros((1, BQ), jnp.float32)
        top, total, delta = walk(scores, (zero + LOWEST, zero, zero))
        inverse = 1.0 / total
        delta = delta * inverse

        def grads(kb, size, dq):
            at = pl.ds(pl.multiple_of(kb * UNIT, UNIT), size * UNIT)
            factor = jnp.exp2((m_ref[pl.ds(kb, 1), :] - top) * EXP2_SCALE) * inverse
            w = p_ref[at, :] * factor
            ds = (w * (dp_ref[at, :] - delta)).astype(jnp.bfloat16)
            dv_ref[at, :] += dot(w.astype(jnp.bfloat16), cotan, NN)
            dk_ref[at, :] += dot(ds, q, NN)
            return dq + dot(kt_ref[:, at], ds, NN)

        dq = walk(grads, jnp.zeros((DH, BQ), jnp.float32)).T
        dq_ref[j, pl.ds(part * some, some)] = (
            (dq * SCALE).astype(jnp.bfloat16).reshape(some, 128, DH)
        )
        for k in range(lines):
            pl.when(i == (k + 1) * turns - 1)(departure(k).start)
        return 0

    lax.fori_loop(0, lines * turns, query_block, 0)

    def finish(b, _):
        at = pl.ds(pl.multiple_of(b * 128, 128), 128)
        dkv_ref[b % planes, b // planes, :128, :] = (dk_ref[at, :] * SCALE).astype(jnp.bfloat16)
        dkv_ref[b % planes, b // planes, 128:, :] = dv_ref[at, :].astype(jnp.bfloat16)
        return 0

    for j in range(lines):
        lax.fori_loop(j * planes, (j + 1) * planes, finish, 0)
        final(j).start()
    for j in range(lines):
        departure(j).wait()
        final(j).wait()


def local(body, out_shape, inputs, scratch, name):
    spec = pl.BlockSpec(memory_space=pltpu.HBM)
    many = isinstance(out_shape, tuple)
    return pl.pallas_call(
        body,
        out_shape=out_shape,
        in_specs=[spec] * len(inputs),
        out_specs=(spec,) * len(out_shape) if many else spec,
        scratch_shapes=scratch,
        compiler_params=pltpu.CompilerParams(vmem_limit_bytes=VMEM_LIMIT),
        name=name,
    )(*inputs)


def attention(kv, parts):
    planes, lines = kv.shape[0], kv.shape[1]
    blocks = planes * lines
    seq = blocks * 128
    heads = parts[0].shape[0] // 2
    half = jnp.bfloat16
    shape = jax.ShapeDtypeStruct
    spec = pl.BlockSpec(memory_space=pltpu.HBM)
    return pl.pallas_call(
        attention_kernel,
        out_shape=(shape((planes, lines, 256, DH), half),)
        + (shape((heads, 128, DH), half),) * lines,
        in_specs=[spec] * (1 + lines),
        out_specs=(spec,) * (1 + lines),
        scratch_shapes=[
            pltpu.VMEM((blocks, 256, DH), half),
            pltpu.VMEM((blocks, SEGMENT_ROWS, 128), half),
            pltpu.VMEM((lines, 2 * heads, 128, DH), half),
            pltpu.VMEM((lines, heads, 128, DH), half),
            pltpu.VMEM((planes, lines, 256, DH), half),
            pltpu.VMEM((seq, BQ), jnp.float32),
            pltpu.VMEM((seq, BQ), jnp.float32),
            pltpu.VMEM((max(8, seq // UNIT), BQ), jnp.float32),
            pltpu.VMEM((seq, DH), jnp.float32),
            pltpu.VMEM((seq, DH), jnp.float32),
            pltpu.VMEM((DH, seq), half),
            pltpu.SemaphoreType.DMA((3 * lines,)),
            pltpu.SemaphoreType.DMA((2 * lines,)),
        ],
        compiler_params=pltpu.CompilerParams(vmem_limit_bytes=VMEM_LIMIT),
        cost_estimate=pl.CostEstimate(
            flops=10 * 1000**3, bytes_accessed=8 * 1000**2, transcendentals=8 * 1000**2
        ),
        name="attention",
    )(kv, *parts)


def pack_kernel(q_hbm, g_hbm, kv_hbm, seg_hbm, h_hbm, *rest):
    kv_out, q_out, cols_out = rest[0], rest[1:5], rest[5:9]
    q_ref, g_ref, kv_ref, seg_ref, h_ref, kv_send, q_send, cols_ref, in_sems, out_sems = rest[9:]
    line, core = lax.axis_index("seq") // PLANES, lax.axis_index("dp")
    pairs = [(seg_hbm, seg_ref), (kv_hbm, kv_ref), (q_hbm, q_ref), (g_hbm, g_ref), (h_hbm, h_ref)]
    arrivals = [pltpu.make_async_copy(*pair, in_sems.at[i]) for i, pair in enumerate(pairs)]
    for copy in arrivals:
        copy.start()
    tokens = q_ref.shape[0]
    lines, heads = q_send.shape[0], q_send.shape[1] // 2
    dp, width = cols_ref.shape[0], cols_ref.shape[1]
    share = h_ref.shape[1] // (HQ * dp)
    departures = [pltpu.make_async_copy(kv_send, kv_out, out_sems.at[0])]
    for k in range(lines):
        departures.append(pltpu.make_async_copy(q_send.at[k], q_out[k], out_sems.at[1 + k]))
    for k in range(dp):
        sem = out_sems.at[1 + lines + k]
        departures.append(pltpu.make_async_copy(cols_ref.at[k], cols_out[k], sem))
    arrivals[0].wait()
    numbers = jnp.broadcast_to(seg_ref[...].astype(jnp.bfloat16), (SEGMENT_ROWS, tokens))
    arrivals[1].wait()
    for j in range(lines):
        k = (j * heads // (HQ // HK)) * DH
        v = HK * DH + k
        kv_send[j, :tokens, :] = kv_ref[:, k : k + DH]
        kv_send[j, tokens : 2 * tokens, :] = kv_ref[:, v : v + DH]
        kv_send[j, 2 * tokens :, :] = numbers
    departures[0].start()
    for kind, ref in ((0, q_ref), (1, g_ref)):
        arrivals[2 + kind].wait()
        for h in range(HQ):
            to = jnp.bitwise_xor(line, h // heads)
            q_send[to, kind * heads + h % heads] = ref[:, h * DH : (h + 1) * DH]
    for copy in departures[1 : 1 + lines]:
        copy.start()
    arrivals[4].wait()
    span = share * dp
    for s in range(width // share):
        turned = h_ref[:, s * span : (s + 1) * span].T
        for r in range(dp):
            part = turned[r * share : (r + 1) * share]
            cols_ref[jnp.bitwise_xor(core, r), s * share : (s + 1) * share, :] = part
    for copy in departures[1 + lines :]:
        copy.start()
    for copy in departures:
        copy.wait()


def gather_kernel(part_hbm, out_hbm, part_ref, out_ref, sems):
    planes, lines = part_ref.shape[0], part_ref.shape[1]
    arrivals = [
        pltpu.make_async_copy(part_hbm.at[w], part_ref.at[w], sems.at[w]) for w in range(planes)
    ]
    for copy in arrivals:
        copy.start()
    for copy in arrivals:
        copy.wait()
    for j in range(lines):
        total = part_ref[0, j].astype(jnp.float32)
        for w in range(1, planes):
            total += part_ref[w, j].astype(jnp.float32)
        out_ref[j] = total.astype(jnp.bfloat16)
    copy = pltpu.make_async_copy(out_ref, out_hbm, sems.at[planes])
    copy.start()
    copy.wait()


def combine_kernel(part_ref, out_ref):
    tokens = out_ref.shape[0]
    each = part_ref.shape[0] // HK
    for g in range(HK):
        for kind in range(2):
            rows = slice(kind * tokens, (kind + 1) * tokens)
            total = part_ref[g * each, rows, :].astype(jnp.float32)
            for j in range(g * each + 1, (g + 1) * each):
                total += part_ref[j, rows, :].astype(jnp.float32)
            at = (kind * HK + g) * DH
            out_ref[:, at : at + DH] = total.astype(jnp.bfloat16)


def weight_kernel(*refs):
    *cols_ref, kv_ref, out_hbm, out_ref, sems = refs
    mine = lax.axis_index("dp")
    seq, share = out_ref.shape[0], out_ref.shape[1]
    pieces = sems.shape[0]
    some = seq // pieces
    departures = []
    for j in range(pieces):
        to = pl.ds(j * some, some)
        departures.append(
            pltpu.make_async_copy(out_ref.at[to], out_hbm.at[to], sems.at[j])
        )
        at = slice(j * some * share, (j + 1) * some * share)
        total = dot(cols_ref[0][at], kv_ref[mine], NN)
        for r in range(1, len(cols_ref)):
            total += dot(cols_ref[r][at], kv_ref[jnp.bitwise_xor(mine, r)], NN)
        out_ref[j * some : (j + 1) * some] = total.astype(jnp.bfloat16).reshape(
            some, share, total.shape[1]
        )
        departures[j].start()
    for copy in departures:
        copy.wait()


def unpack_kernel(*refs):
    part_hbm, out_hbm, part_ref, out_ref, sems = refs[:-4], *refs[-4:]
    line = lax.axis_index("seq") // PLANES
    heads = part_ref.shape[1]
    arrivals = [
        pltpu.make_async_copy(part, part_ref.at[k], sems.at[k]) for k, part in enumerate(part_hbm)
    ]
    for copy in arrivals:
        copy.start()
    for k, copy in enumerate(arrivals):
        copy.wait()
        first = jnp.bitwise_xor(line, k) * heads
        for h in range(heads):
            at = pl.ds(pl.multiple_of((first + h) * DH, DH), DH)
            out_ref[:, at] = part_ref[k, h]
    copy = pltpu.make_async_copy(out_ref, out_hbm, sems.at[len(part_hbm)])
    copy.start()
    copy.wait()


def total_kernel(part_hbm, out_hbm, part_ref, out_ref, sems):
    seq = part_ref.shape[0]
    pieces = sems.shape[0] - 1
    some = seq // pieces
    arrivals = []
    for j in range(pieces):
        at = pl.ds(j * some, some)
        arrivals.append(pltpu.make_async_copy(part_hbm.at[at], part_ref.at[at], sems.at[j]))
    for copy in arrivals:
        copy.start()
    total = jnp.zeros(out_ref.shape, jnp.float32)
    for j in range(pieces):
        arrivals[j].wait()
        for s in range(j * some, (j + 1) * some):
            total += part_ref[s].astype(jnp.float32)
    out_ref[...] = total
    copy = pltpu.make_async_copy(out_ref, out_hbm, sems.at[pieces])
    copy.start()
    copy.wait()


def exchange(array, axis, groups=None):
    return lax.all_to_all(
        array, axis, split_axis=0, concat_axis=0, axis_index_groups=groups, tiled=True
    )


def shards(hidden, queries, keyvals, out_grad, segment):
    seq, dp = lax.axis_size("seq"), lax.axis_size("dp")
    tokens, width = hidden.shape[1], hidden.shape[2]
    share = width // (seq * dp)
    lines = seq // PLANES
    heads = HQ // lines
    half = jnp.bfloat16
    shape = jax.ShapeDtypeStruct
    along = [[j * PLANES + w for j in range(lines)] for w in range(PLANES)]
    across = [[j * PLANES + w for w in range(PLANES)] for j in range(lines)]

    def partners(k):
        return [(p, (p // PLANES ^ k) * PLANES + p % PLANES) for p in range(seq)]

    inputs = [queries[0], out_grad[0], keyvals[0], segment, hidden[0]]
    shared = (lines, 2 * tokens + SEGMENT_ROWS, DH)
    kv, *parts = local(
        pack_kernel,
        (shape(shared, half),)
        + (shape((2 * heads, tokens, DH), half),) * lines
        + (shape((seq * share, tokens), half),) * dp,
        inputs,
        [
            pltpu.VMEM(queries.shape[1:], half),
            pltpu.VMEM(out_grad.shape[1:], half),
            pltpu.VMEM(keyvals.shape[1:], half),
            pltpu.VMEM(segment.shape, segment.dtype),
            pltpu.VMEM(hidden.shape[1:], half),
            pltpu.VMEM(shared, half),
            pltpu.VMEM((lines, 2 * heads, tokens, DH), half),
            pltpu.VMEM((dp, seq * share, tokens), half),
            pltpu.SemaphoreType.DMA((5,)),
            pltpu.SemaphoreType.DMA((1 + lines + dp,)),
        ],
        "pack",
    )
    parts, columns = parts[:lines], parts[lines:]
    kv, parts = lax.optimization_barrier((exchange(kv, "seq", along), parts))
    for k in range(1, lines):
        parts[k] = lax.ppermute(parts[k], "seq", partners(k))
    kv = jnp.broadcast_to(kv[None], (PLANES,) + shared)
    kv = exchange(kv, "seq", across)
    kv, parts, columns = lax.optimization_barrier((kv, parts, columns))
    for k in range(1, dp):
        columns[k] = lax.ppermute(columns[k], "dp", [(r, r ^ k) for r in range(dp)])
    dkv, *dq = attention(kv, parts)
    dkv, dq, columns = lax.optimization_barrier((dkv, dq, columns))
    for k in range(1, lines):
        dq[k] = lax.ppermute(dq[k], "seq", partners(k))
    dkv, dq = lax.optimization_barrier((exchange(dkv, "seq", across), dq))
    dkv = local(
        gather_kernel,
        shape((lines, 2 * tokens, DH), half),
        [dkv],
        [
            pltpu.VMEM(dkv.shape, half),
            pltpu.VMEM(dkv.shape[1:], half),
            pltpu.SemaphoreType.DMA((PLANES + 1,)),
        ],
        "gather",
    )
    dkv = exchange(dkv, "seq", along)
    keyval_grad = pl.pallas_call(
        combine_kernel,
        out_shape=shape((tokens, 2 * HK * DH), half),
        in_specs=[pl.BlockSpec(memory_space=pltpu.VMEM)],
        out_specs=pl.BlockSpec(memory_space=pltpu.VMEM),
        compiler_params=pltpu.CompilerParams(vmem_limit_bytes=SMALL_LIMIT),
        name="combine",
    )(dkv)
    every = lax.all_gather(keyval_grad, "dp", axis=0)
    result = (seq, share, 2 * HK * DH)
    partial = pl.pallas_call(
        weight_kernel,
        out_shape=shape(result, half),
        in_specs=[pl.BlockSpec(memory_space=pltpu.VMEM)] * (dp + 1),
        out_specs=pl.BlockSpec(memory_space=pltpu.HBM),
        scratch_shapes=[pltpu.VMEM(result, half), pltpu.SemaphoreType.DMA((4,))],
        compiler_params=pltpu.CompilerParams(vmem_limit_bytes=SMALL_LIMIT),
        name="weight",
    )(*columns, every)
    partial = exchange(partial, "seq")
    query_grad = local(
        unpack_kernel,
        shape((tokens, HQ * DH), half),
        dq,
        [
            pltpu.VMEM((lines, heads, tokens, DH), half),
            pltpu.VMEM((tokens, HQ * DH), half),
            pltpu.SemaphoreType.DMA((lines + 1,)),
        ],
        "unpack",
    )
    weight_grad = local(
        total_kernel,
        shape(result[1:], jnp.float32),
        [partial],
        [
            pltpu.VMEM(result, half),
            pltpu.VMEM(result[1:], jnp.float32),
            pltpu.SemaphoreType.DMA((5,)),
        ],
        "total",
    )
    return (query_grad[None], keyval_grad[None], weight_grad)


def solution(mesh):
    in_specs = (
        P("dp", "seq", None),
        P("dp", "seq", None),
        P("dp", "seq", None),
        P("dp", "seq", None),
        P("dp", "seq"),
    )
    out_specs = (P("dp", "seq", None), P("dp", "seq", None), P(("seq", "dp"), None))
    return jax.shard_map(shards, mesh=mesh, in_specs=in_specs, out_specs=out_specs, check_vma=False)
```

time: 187 us -> 182 us (0.973)
  blocking collectives: 120 us -> 28.5 us
  waiting for transfers between devices: 17.2 us -> 69.3 us
  starting transfers between devices: 6.54 us -> 37.8 us
  local copies, waits for them, and re-layouts: 0.01 us -> 5.49 us
  Pallas kernels: 42.4 us -> 39.8 us
    all_to_all x2, blocking collectives: 108 us -> 21.3 us  [exchange(): lax.all_to_all(array, axis, split_axis=0, concat_axis=0, axis_index_group...]
    ppermute x0 -> x6, waiting for transfers between devices: none -> 34.5 us  [the longest x3 21 us: shards(): parts[k] = lax.ppermute(parts[k], 'seq', partners(k))]
    all_to_all x1 -> x3, starting transfers between devices: 4.68 us -> 26.5 us  [exchange(): lax.all_to_all(array, axis, split_axis=0, concat_axis=0, axis_index_group...]
    all_to_all x1 -> x3, waiting for transfers between devices: 17.2 us -> 34.9 us  [exchange(): lax.all_to_all(array, axis, split_axis=0, concat_axis=0, axis_index_group...]
    ppermute x0 -> x6, starting transfers between devices: none -> 9.46 us  [the longest x3 4.76 us: shards(): dq[k] = lax.ppermute(dq[k], 'seq', partners(k))]
    all_gather x1, blocking collectives: 12.1 us -> 7.16 us  [shards(): every = lax.all_gather(keyval_grad, 'dp', axis=0)]
    unnamed x2 -> x22, local copies, waits for them, and re-layouts: 0.01 us -> 3.82 us
    pallas_call x1 -> x2, Pallas kernels: 29 us -> 26.5 us  [the longest x1 25.8 us: attention(): pl.pallas_call(attention_kernel, out_shape=(shape((planes, lines, 256, DH...]
  transfers between devices with their start and end apart: 4 -> 12, of which waited for: 1 -> 9; matrix products, arithmetic and copies ran while one was open for 0% -> 0% of each run, Pallas kernels for 17% -> 15%
where the time goes in v6:
time: 182 us
  waiting for transfers between devices  69.3 us (38%)
  Pallas kernels  39.8 us (22%)
  starting transfers between devices  37.8 us (21%)
  blocking collectives  28.5 us (16%)
  local copies, waits for them, and re-layouts  5.49 us (3%)
    all_to_all x3, waiting for transfers between devices, exchange(): lax.all_to_all(array, axis, split_axis=0, concat_axis=0, axis_index_group...  34.9 us
    all_to_all x3, starting transfers between devices, exchange(): lax.all_to_all(array, axis, split_axis=0, concat_axis=0, axis_index_group...  26.5 us
    pallas_call x1, Pallas kernels, attention(): pl.pallas_call(attention_kernel, out_shape=(shape((planes, lines, 256, DH...  25.8 us
    all_to_all x2, blocking collectives, exchange(): lax.all_to_all(array, axis, split_axis=0, concat_axis=0, axis_index_group...  21.3 us
    ppermute x3, waiting for transfers between devices, shards(): parts[k] = lax.ppermute(parts[k], 'seq', partners(k))  21 us
    ppermute x3, waiting for transfers between devices, shards(): dq[k] = lax.ppermute(dq[k], 'seq', partners(k))  13.4 us
    pallas_call x4, Pallas kernels, local(): pl.pallas_call(body, out_shape=out_shape, in_specs=[spec] * len(inputs),...  10.3 us
    all_gather x1, blocking collectives, shards(): every = lax.all_gather(keyval_grad, 'dp', axis=0)  7.16 us
  transfers between devices with their start and end apart: 12, of which 9 were waited for; matrix products, arithmetic and copies ran while one was open for 0% of the time, Pallas kernels for 15%

profile of v6, /device:TPU:0, one launch (start us, length us, event | category | flops | bytes accessed | tf_op | source)
XLA Modules:
  0.0 181.7 jit_solution(3468743592967137513)
XLA Ops:
  0.6 3.6 %pack.1 = (bf16[4,272,128]{2,1,0:T(8,128)(2,1)}, bf16[16,128,128]{2,1,0:T(8,128)(2,1)}, bf16[16,128,128]{2,1,0:T(8,128)(2,1)}, bf16[16,128,128]{2,1,0:T(8,128)(2...) custom-call(bf16[128,4096]{1,0:T(8,128)(2,1)} %bitcast.8, ...), custom_call_target="tpu_custom_call" | custom-call | tf_op jit(solution)/shard_map/pack/pallas_call | solution.py:171
  4.2 11.2 %all_to_all.25 = bf16[4,272,128]{2,1,0:T(8,128)(2,1)S(1)} all-to-all(bf16[4,272,128]{2,1,0:T(8,128)(2,1)} %get-tuple-element.45), channel_id=1, replica_groups={{0,32,64,96},{4,36,68,100},{8,40,72,104},{12,44,76,108},{16,48,80,112},..., dimensions={0} | all-to-all | bytes 557056 | tf_op jit(solution)/shard_map/all_to_all | solution.py:365
  17.1 7.9 %all-to-all-start.1 = ((bf16[8,4,272,128]{3,2,1,0:T(8,128)(2,1)}), bf16[8,4,272,128]{3,2,1,0:T(8,128)(2,1)S(1)}, u32[]{:S(2)}, u32[]{:S(2)}) async-start(bf16[8,4,272,128]{3,2,1,0:T(8,128)(2,1)} %broadcast_in_dim.12), calls=%async_computation.1 | async-start | bytes 4456448 | tf_op jit(solution)/shard_map/all_to_all | solution.py:365
  25.6 2.1 %collective-permute-start.1 = (bf16[16,128,128]{2,1,0:T(8,128)(2,1)S(1)}, bf16[16,128,128]{2,1,0:T(8,128)(2,1)S(1)}, u32[]{:S(2)}, u32[]{:S(2)}) collective-permute-start(bf16[16,128,128]{2,1,0:T(8,128)(2,1)S(1)} %copy-done.7), channel_id=1, source_target_pairs={{0,64},{4,68},{8,72},{12,76},{16,80},{20,84},{24,88},{28,92},{32,9... | collective-permute-start | bytes 1572872 | tf_op jit(solution)/shard_map/ppermute | solution.py:409
  27.7 2.1 %collective-permute-start.2 = (bf16[16,128,128]{2,1,0:T(8,128)(2,1)S(1)}, bf16[16,128,128]{2,1,0:T(8,128)(2,1)}, u32[]{:S(2)}, u32[]{:S(2)}) collective-permute-start(bf16[16,128,128]{2,1,0:T(8,128)(2,1)S(1)} %copy-done.6), channel_id=1, source_target_pairs={{0,96},{4,100},{8,104},{12,108},{16,112},{20,116},{24,120},{28,124... | collective-permute-start | bytes 1572872 | tf_op jit(solution)/shard_map/ppermute | solution.py:409
  29.7 10.4 %collective-permute-done.refs_2_ = bf16[16,128,128]{2,1,0:T(8,128)(2,1)S(1)} collective-permute-done((bf16[16,128,128]{2,1,0:T(8,128)(2,1)}, bf16[16,128,128]{2,1,0:T(8,128)(2,1)S(1)}, u32[]{:S(2)}, u32[]{:S(2)}) %collective-permute-start) | collective-permute-done | bytes 524320 | tf_op jit(solution)/shard_map/ppermute | solution.py:409
  40.1 9.0 %collective-permute-done.1.refs_3_ = bf16[16,128,128]{2,1,0:T(8,128)(2,1)S(1)} collective-permute-done((bf16[16,128,128]{2,1,0:T(8,128)(2,1)S(1)}, bf16[16,128,128]{2,1,0:T(8,128)(2,1)S(1)}, u32[]{:S(2)}, u32[]{:S(2)}) %collective-permute-start.1) | collective-permute-done | bytes 524320 | tf_op jit(solution)/shard_map/ppermute | solution.py:409
  49.9 1.7 collective-permute-done.2.refs_4_
  51.6 3.9 %all-to-all-done.1.refs_0_ = bf16[8,4,272,128]{3,2,1,0:T(8,128)(2,1)S(1)} async-done(((bf16[8,4,272,128]{3,2,1,0:T(8,128)(2,1)}), bf16[8,4,272,128]{3,2,1,0:T(8,128)(2,1)S(1)}, u32[]{:S(2)}, u32[]{:S(2)}) %all-to-all-start.1) | async-done | bytes 2228256 | tf_op jit(solution)/shard_map/all_to_all | solution.py:365
  58.7 25.8 %attention.1 = (bf16[8,4,256,128]{3,2,1,0:T(8,128)(2,1)}, bf16[8,128,128]{2,1,0:T(8,128)(2,1)}, bf16[8,128,128]{2,1,0:T(8,128)(2,1)}, bf16[8,128,128]{2,1,0:T(8,128)(2,1)}, bf16[8,128,128]{2,1,0:T(8,128)(2,1)}) custom-call(bf16[8,4,272,128]{3,2,1,0:T(8,128)(2,1)} %copy-done.3, bf16[16,128,128]{2,1,0:T(8,128)(2,1)} %get-tuple-element.60.refs_1_, ...), custom_call_target="tpu_custom_call" | custom-call | flops 10000000000 | bytes 8000000 | tf_op jit(solution)/shard_map/attention/pallas_call | solution.py:190
  85.3 12.1 %all-to-all-start.2 = ((bf16[8,4,256,128]{3,2,1,0:T(8,128)(2,1)}), bf16[8,4,256,128]{3,2,1,0:T(8,128)(2,1)}, u32[]{:S(2)}, u32[]{:S(2)}) async-start(bf16[8,4,256,128]{3,2,1,0:T(8,128)(2,1)} %get-tuple-element.73), calls=%async_computation.2 | async-start | bytes 4194304 | tf_op jit(solution)/shard_map/all_to_all | solution.py:365
  97.5 3.5 %collective-permute-start.7 = (bf16[8,128,128]{2,1,0:T(8,128)(2,1)S(1)}, bf16[8,128,128]{2,1,0:T(8,128)(2,1)}, u32[]{:S(2)}, u32[]{:S(2)}) collective-permute-start(bf16[8,128,128]{2,1,0:T(8,128)(2,1)S(1)} %copy-done.9), channel_id=1, source_target_pairs={{0,64},{4,68},{8,72},{12,76},{16,80},{20,84},{24,88},{28,92},{32,9... | collective-permute-start | bytes 786440 | tf_op jit(solution)/shard_map/ppermute | solution.py:418
  102.2 4.6 %collective-permute-done.6.refs_1_ = bf16[8,128,128]{2,1,0:T(8,128)(2,1)} collective-permute-done((bf16[8,128,128]{2,1,0:T(8,128)(2,1)S(1)}, bf16[8,128,128]{2,1,0:T(8,128)(2,1)}, u32[]{:S(2)}, u32[]{:S(2)}) %collective-permute-start.6) | collective-permute-done | bytes 262176 | tf_op jit(solution)/shard_map/ppermute | solution.py:418
  106.7 6.3 %collective-permute-done.7.refs_2_ = bf16[8,128,128]{2,1,0:T(8,128)(2,1)} collective-permute-done((bf16[8,128,128]{2,1,0:T(8,128)(2,1)S(1)}, bf16[8,128,128]{2,1,0:T(8,128)(2,1)}, u32[]{:S(2)}, u32[]{:S(2)}) %collective-permute-start.7) | collective-permute-done | bytes 262176 | tf_op jit(solution)/shard_map/ppermute | solution.py:418
  113.0 2.6 %collective-permute-done.8.refs_3_ = bf16[8,128,128]{2,1,0:T(8,128)(2,1)} collective-permute-done((bf16[8,128,128]{2,1,0:T(8,128)(2,1)S(1)}, bf16[8,128,128]{2,1,0:T(8,128)(2,1)}, u32[]{:S(2)}, u32[]{:S(2)}) %collective-permute-start.8) | collective-permute-done | bytes 262176 | tf_op jit(solution)/shard_map/ppermute | solution.py:418
  115.6 13.7 %all-to-all-done.2.part_hbm = bf16[8,4,256,128]{3,2,1,0:T(8,128)(2,1)} async-done(((bf16[8,4,256,128]{3,2,1,0:T(8,128)(2,1)}), bf16[8,4,256,128]{3,2,1,0:T(8,128)(2,1)}, u32[]{:S(2)}, u32[]{:S(2)}) %all-to-all-start.2) | async-done | bytes 2097184 | tf_op jit(solution)/shard_map/all_to_all | solution.py:365
  129.3 2.5 %gather.1 = bf16[4,256,128]{2,1,0:T(8,128)(2,1)} custom-call(bf16[8,4,256,128]{3,2,1,0:T(8,128)(2,1)} %all-to-all-done.2.part_hbm), custom_call_target="tpu_custom_call" | custom-call | tf_op jit(solution)/shard_map/gather/pallas_call | solution.py:171
  131.9 10.1 %all_to_all.26.part_ref = bf16[4,256,128]{2,1,0:T(8,128)(2,1)S(1)} all-to-all(bf16[4,256,128]{2,1,0:T(8,128)(2,1)} %gather.1), channel_id=1, replica_groups={{0,32,64,96},{4,36,68,100},{8,40,72,104},{12,44,76,108},{16,48,80,112},..., dimensions={0} | all-to-all | bytes 524288 | tf_op jit(solution)/shard_map/all_to_all | solution.py:365
  142.6 7.2 %all-gather = bf16[512,512]{1,0:T(8,128)(2,1)S(1)} all-gather(bf16[128,512]{1,0:T(8,128)(2,1)} %combine.1), channel_id=2, replica_groups=mesh['seq'=32,'dp'=4] {'dp'}, dimensions={0}, use_global_device_ids=true | all-gather | bytes 655360 | tf_op jit(solution)/shard_map/all_gather | solution.py:440
  150.7 3.0 %weight.1 = bf16[32,32,512]{2,1,0:T(8,128)(2,1)} custom-call(bf16[1024,128]{1,0:T(8,128)(2,1)S(1)} %copy-done, bf16[1024,128]{1,0:T(8,128)(2,1)S(1)} %copy-done.2, bf16[1024,128]{1,0:T(8,128)(2,1)} %collective-permute-done.4.refs_2_, bf16[1024,128]{1,0:T(8,128)(2,1)} %collective-permute-done.5.refs_3_, bf16[4,128,512]{2,1,0:T(8,128)(2,1)S(1)} %bitcast.7), custom_call_target="tpu_custom_call" | custom-call | tf_op jit(solution)/shard_map/weight/pallas_call | solution.py:442
  153.8 6.5 %all-to-all-start.4 = ((bf16[32,32,512]{2,1,0:T(8,128)(2,1)}), bf16[32,32,512]{2,1,0:T(8,128)(2,1)}, u32[]{:S(2)}, u32[]{:S(2)}) async-start(bf16[32,32,512]{2,1,0:T(8,128)(2,1)} %weight.1), calls=%async_computation.4 | async-start | bytes 2097152 | tf_op jit(solution)/shard_map/all_to_all | solution.py:365
  160.3 2.3 %unpack.1 = bf16[128,4096]{1,0:T(8,128)(2,1)} custom-call(bf16[8,128,128]{2,1,0:T(8,128)(2,1)} %get-tuple-element.78.refs_0_, bf16[8,128,128]{2,1,0:T(8,128)(2,1)} %collective-permute-done.6.refs_1_, bf16[8,128,128]{2,1,0:T(8,128)(2,1)} %collective-permute-done.7.refs_2_, bf16[8,128,128]{2,1,0:T(8,128)(2,1)} %collective-permute-done.8.refs_3_), custom_call_target="tpu_custom_call" | custom-call | tf_op jit(solution)/shard_map/unpack/pallas_call | solution.py:171
  162.6 17.2 %all-to-all-done.4.part_hbm = bf16[32,32,512]{2,1,0:T(8,128)(2,1)} async-done(((bf16[32,32,512]{2,1,0:T(8,128)(2,1)}), bf16[32,32,512]{2,1,0:T(8,128)(2,1)}, u32[]{:S(2)}, u32[]{:S(2)}) %all-to-all-start.4) | async-done | bytes 1048608 | tf_op jit(solution)/shard_map/all_to_all | solution.py:365
  179.8 1.9 %total.1 = f32[32,512]{1,0:T(8,128)} custom-call(bf16[32,32,512]{2,1,0:T(8,128)(2,1)} %all-to-all-done.4.part_hbm), custom_call_target="tpu_custom_call" | custom-call | tf_op jit(solution)/shard_map/total/pallas_call | solution.py:171
  (33 shorter events, 9.9 us)
Async XLA Ops:
  17.1 8.5 %copy-start.7 = (bf16[16,128,128]{2,1,0:T(8,128)(2,1)S(1)}, bf16[16,128,128]{2,1,0:T(8,128)(2,1)}, u32[]{:S(2)}) copy-start(bf16[16,128,128]{2,1,0:T(8,128)(2,1)} %get-tuple-element.53) | copy-start | bytes 1572868
  17.1 10.6 %copy-start.6 = (bf16[16,128,128]{2,1,0:T(8,128)(2,1)S(1)}, bf16[16,128,128]{2,1,0:T(8,128)(2,1)}, u32[]{:S(2)}) copy-start(bf16[16,128,128]{2,1,0:T(8,128)(2,1)} %get-tuple-element.54) | copy-start | bytes 1572868
  17.1 38.4 %all-to-all-start.1 = ((bf16[8,4,272,128]{3,2,1,0:T(8,128)(2,1)}), bf16[8,4,272,128]{3,2,1,0:T(8,128)(2,1)S(1)}, u32[]{:S(2)}, u32[]{:S(2)}) async-start(bf16[8,4,272,128]{3,2,1,0:T(8,128)(2,1)} %broadcast_in_dim.12), calls=%async_computation.1 | async-start | bytes 4456448 | tf_op jit(solution)/shard_map/all_to_all | solution.py:365
  25.0 15.1 %collective-permute-start = (bf16[16,128,128]{2,1,0:T(8,128)(2,1)}, bf16[16,128,128]{2,1,0:T(8,128)(2,1)S(1)}, u32[]{:S(2)}, u32[]{:S(2)}) collective-permute-start(bf16[16,128,128]{2,1,0:T(8,128)(2,1)} %get-tuple-element.52), channel_id=1, source_target_pairs={{0,32},{4,36},{8,40},{12,44},{16,48},{20,52},{24,56},{28,60},{32,0... | collective-permute-start | bytes 1572872 | tf_op jit(solution)/shard_map/ppermute | solution.py:409
  25.6 23.5 %collective-permute-start.1 = (bf16[16,128,128]{2,1,0:T(8,128)(2,1)S(1)}, bf16[16,128,128]{2,1,0:T(8,128)(2,1)S(1)}, u32[]{:S(2)}, u32[]{:S(2)}) collective-permute-start(bf16[16,128,128]{2,1,0:T(8,128)(2,1)S(1)} %copy-done.7), channel_id=1, source_target_pairs={{0,64},{4,68},{8,72},{12,76},{16,80},{20,84},{24,88},{28,92},{32,9... | collective-permute-start | bytes 1572872 | tf_op jit(solution)/shard_map/ppermute | solution.py:409
  27.7 23.9 %collective-permute-start.2 = (bf16[16,128,128]{2,1,0:T(8,128)(2,1)S(1)}, bf16[16,128,128]{2,1,0:T(8,128)(2,1)}, u32[]{:S(2)}, u32[]{:S(2)}) collective-permute-start(bf16[16,128,128]{2,1,0:T(8,128)(2,1)S(1)} %copy-done.6), channel_id=1, source_target_pairs={{0,96},{4,100},{8,104},{12,108},{16,112},{20,116},{24,120},{28,124... | collective-permute-start | bytes 1572872 | tf_op jit(solution)/shard_map/ppermute | solution.py:409
  40.1 9.0 %copy-start.4 = (bf16[16,128,128]{2,1,0:T(8,128)(2,1)}, bf16[16,128,128]{2,1,0:T(8,128)(2,1)S(1)}, u32[]{:S(2)}) copy-start(bf16[16,128,128]{2,1,0:T(8,128)(2,1)S(1)} %collective-permute-done.refs_2_) | copy-start | bytes 1572868
  49.1 0.8 copy-start.5
  55.5 1.4 copy-start.3
  56.9 27.7 %collective-permute-start.3 = (bf16[1024,128]{1,0:T(8,128)(2,1)}, bf16[1024,128]{1,0:T(8,128)(2,1)S(1)}, u32[]{:S(2)}, u32[]{:S(2)}) collective-permute-start(bf16[1024,128]{1,0:T(8,128)(2,1)} %get-tuple-element.70), channel_id=1, source_target_pairs={{0,1},{1,0},{2,3},{3,2},{4,5},{5,4},{6,7},{7,6},{8,9},{9,8},{10,11... | collective-permute-start | bytes 786440 | tf_op jit(solution)/shard_map/ppermute | solution.py:414
  56.9 27.7 %collective-permute-start.4 = (bf16[1024,128]{1,0:T(8,128)(2,1)}, bf16[1024,128]{1,0:T(8,128)(2,1)}, u32[]{:S(2)}, u32[]{:S(2)}) collective-permute-start(bf16[1024,128]{1,0:T(8,128)(2,1)} %get-tuple-element.71), channel_id=1, source_target_pairs={{0,2},{1,3},{2,0},{3,1},{4,6},{5,7},{6,4},{7,5},{8,10},{9,11},{10,... | collective-permute-start | bytes 786440 | tf_op jit(solution)/shard_map/ppermute | solution.py:414
  57.9 26.7 %collective-permute-start.5 = (bf16[1024,128]{1,0:T(8,128)(2,1)}, bf16[1024,128]{1,0:T(8,128)(2,1)}, u32[]{:S(2)}, u32[]{:S(2)}) collective-permute-start(bf16[1024,128]{1,0:T(8,128)(2,1)} %get-tuple-element.72), channel_id=1, source_target_pairs={{0,3},{1,2},{2,1},{3,0},{4,7},{5,6},{6,5},{7,4},{8,11},{9,10},{10,... | collective-permute-start | bytes 786440 | tf_op jit(solution)/shard_map/ppermute | solution.py:414
  84.5 12.8 %copy-start.10 = (bf16[8,128,128]{2,1,0:T(8,128)(2,1)S(1)}, bf16[8,128,128]{2,1,0:T(8,128)(2,1)}, u32[]{:S(2)}) copy-start(bf16[8,128,128]{2,1,0:T(8,128)(2,1)} %get-tuple-element.75) | copy-start | bytes 786436
  84.5 12.9 %copy-start.9 = (bf16[8,128,128]{2,1,0:T(8,128)(2,1)S(1)}, bf16[8,128,128]{2,1,0:T(8,128)(2,1)}, u32[]{:S(2)}) copy-start(bf16[8,128,128]{2,1,0:T(8,128)(2,1)} %get-tuple-element.76) | copy-start | bytes 786436
  84.6 16.4 %copy-start.8 = (bf16[8,128,128]{2,1,0:T(8,128)(2,1)S(1)}, bf16[8,128,128]{2,1,0:T(8,128)(2,1)}, u32[]{:S(2)}) copy-start(bf16[8,128,128]{2,1,0:T(8,128)(2,1)} %get-tuple-element.77) | copy-start | bytes 786436
  84.6 0.7 copy-start.1
  85.3 44.0 %all-to-all-start.2 = ((bf16[8,4,256,128]{3,2,1,0:T(8,128)(2,1)}), bf16[8,4,256,128]{3,2,1,0:T(8,128)(2,1)}, u32[]{:S(2)}, u32[]{:S(2)}) async-start(bf16[8,4,256,128]{3,2,1,0:T(8,128)(2,1)} %get-tuple-element.73), calls=%async_computation.2 | async-start | bytes 4194304 | tf_op jit(solution)/shard_map/all_to_all | solution.py:365
  97.4 52.4 %copy-start = (bf16[1024,128]{1,0:T(8,128)(2,1)S(1)}, bf16[1024,128]{1,0:T(8,128)(2,1)}, u32[]{:S(2)}) copy-start(bf16[1024,128]{1,0:T(8,128)(2,1)} %get-tuple-element.83.refs_0_) | copy-start | bytes 786436
  97.4 9.4 %collective-permute-start.6 = (bf16[8,128,128]{2,1,0:T(8,128)(2,1)S(1)}, bf16[8,128,128]{2,1,0:T(8,128)(2,1)}, u32[]{:S(2)}, u32[]{:S(2)}) collective-permute-start(bf16[8,128,128]{2,1,0:T(8,128)(2,1)S(1)} %copy-done.10), channel_id=1, source_target_pairs={{0,32},{4,36},{8,40},{12,44},{16,48},{20,52},{24,56},{28,60},{32,0... | collective-permute-start | bytes 786440 | tf_op jit(solution)/shard_map/ppermute | solution.py:418
  97.5 15.5 %collective-permute-start.7 = (bf16[8,128,128]{2,1,0:T(8,128)(2,1)S(1)}, bf16[8,128,128]{2,1,0:T(8,128)(2,1)}, u32[]{:S(2)}, u32[]{:S(2)}) collective-permute-start(bf16[8,128,128]{2,1,0:T(8,128)(2,1)S(1)} %copy-done.9), channel_id=1, source_target_pairs={{0,64},{4,68},{8,72},{12,76},{16,80},{20,84},{24,88},{28,92},{32,9... | collective-permute-start | bytes 786440 | tf_op jit(solution)/shard_map/ppermute | solution.py:418
  101.0 14.6 %collective-permute-start.8 = (bf16[8,128,128]{2,1,0:T(8,128)(2,1)S(1)}, bf16[8,128,128]{2,1,0:T(8,128)(2,1)}, u32[]{:S(2)}, u32[]{:S(2)}) collective-permute-start(bf16[8,128,128]{2,1,0:T(8,128)(2,1)S(1)} %copy-done.8), channel_id=1, source_target_pairs={{0,96},{4,100},{8,104},{12,108},{16,112},{20,116},{24,120},{28,124... | collective-permute-start | bytes 786440 | tf_op jit(solution)/shard_map/ppermute | solution.py:418
  149.8 1.0 copy-start.2
  153.8 26.0 %all-to-all-start.4 = ((bf16[32,32,512]{2,1,0:T(8,128)(2,1)}), bf16[32,32,512]{2,1,0:T(8,128)(2,1)}, u32[]{:S(2)}, u32[]{:S(2)}) async-start(bf16[32,32,512]{2,1,0:T(8,128)(2,1)} %weight.1), calls=%async_computation.4 | async-start | bytes 2097152 | tf_op jit(solution)/shard_map/all_to_all | solution.py:365

commit v7 on v6

--- a/solution.py
+++ b/solution.py
@@ -13,12 +13,13 @@
 MASKED = -1e30
 LOWEST = -1e29
 SEGMENT_ROWS = 16
-BQ = 512
+BQ = 1024
 UNIT = 256
-CHUNKS = (8, 4, 2, 1)
+CHUNKS = (4, 2, 1)
 PLANES = 8
 VMEM_LIMIT = 127 * 512 * 1024
 SMALL_LIMIT = 20 * 1024 * 1024
+ATTENTION_LIMIT = 59 * 1024 * 1024
 NT = (((1,), (1,)), ((), ()))
 NN = (((1,), (0,)), ((), ()))
 
@@ -109,14 +110,24 @@
             return state
 
         def scores(kb, size, carry):
+            plain = ((kb + size) * UNIT <= first) & (kb * UNIT >= start_of(first + 127))
+            return lax.cond(
+                plain,
+                lambda c: score_part(kb, size, c, False),
+                lambda c: score_part(kb, size, c, True),
+                carry,
+            )
+
+        def score_part(kb, size, carry, masked):
             top, total, delta = carry
             k = rows(kb * un, size * un, 0)
             v = rows(kb * un, size * un, 1)
             st = dot(k, q, NT)
             dpt = dot(v, cotan, NT)
             at = pl.ds(pl.multiple_of(kb * UNIT, UNIT), size * UNIT)
-            kpos = kb * UNIT + lax.broadcasted_iota(jnp.int32, (size * UNIT, BQ), 0)
-            st = jnp.where((kpos >= qstart) & (kpos <= qpos), st, MASKED)
+            if masked:
+                kpos = kb * UNIT + lax.broadcasted_iota(jnp.int32, (size * UNIT, BQ), 0)
+                st = jnp.where((kpos >= qstart) & (kpos <= qpos), st, MASKED)
             newtop = jnp.maximum(top, jnp.max(st, axis=0, keepdims=True))
             p = jnp.exp2((st - newtop) * EXP2_SCALE)
             fade = jnp.exp2((top - newtop) * EXP2_SCALE)
@@ -208,7 +219,7 @@
             pltpu.SemaphoreType.DMA((3 * lines,)),
             pltpu.SemaphoreType.DMA((2 * lines,)),
         ],
-        compiler_params=pltpu.CompilerParams(vmem_limit_bytes=VMEM_LIMIT),
+        compiler_params=pltpu.CompilerParams(vmem_limit_bytes=ATTENTION_LIMIT),
         cost_estimate=pl.CostEstimate(
             flops=10 * 1000**3, bytes_accessed=8 * 1000**2, transcendentals=8 * 1000**2
         ),
@@ -297,21 +308,36 @@
 
 
 def weight_kernel(*refs):
-    *cols_ref, kv_ref, out_hbm, out_ref, sems = refs
+    cols_hbm, (kv_hbm, out_hbm, cols_ref, kv_ref, out_ref, sems) = refs[:-6], refs[-6:]
     mine = lax.axis_index("dp")
+    dp = len(cols_hbm)
     seq, share = out_ref.shape[0], out_ref.shape[1]
-    pieces = sems.shape[0]
+    pieces = 4
     some = seq // pieces
-    departures = []
+    rows = some * share
+    first = pltpu.make_async_copy(kv_hbm, kv_ref, sems.at[0])
+    first.start()
+    arrivals, departures = [], []
     for j in range(pieces):
-        to = pl.ds(j * some, some)
-        departures.append(
-            pltpu.make_async_copy(out_ref.at[to], out_hbm.at[to], sems.at[j])
-        )
-        at = slice(j * some * share, (j + 1) * some * share)
-        total = dot(cols_ref[0][at], kv_ref[mine], NN)
-        for r in range(1, len(cols_ref)):
-            total += dot(cols_ref[r][at], kv_ref[jnp.bitwise_xor(mine, r)], NN)
+        at, to = pl.ds(j * rows, rows), pl.ds(j * some, some)
+        for r in range(dp):
+            sem = sems.at[1 + j * dp + r]
+            arrivals.append(
+                pltpu.make_async_copy(cols_hbm[r].at[at], cols_ref.at[r, at], sem)
+            )
+        sem = sems.at[1 + pieces * dp + j]
+        departures.append(pltpu.make_async_copy(out_ref.at[to], out_hbm.at[to], sem))
+    for copy in arrivals:
+        copy.start()
+    first.wait()
+    for j in range(pieces):
+        total = None
+        for r in range(dp):
+            arrivals[j * dp + r].wait()
+            part = dot(
+                cols_ref[r, j * rows : (j + 1) * rows], kv_ref[jnp.bitwise_xor(mine, r)], NN
+            )
+            total = part if total is None else total + part
         out_ref[j * some : (j + 1) * some] = total.astype(jnp.bfloat16).reshape(
             some, share, total.shape[1]
         )
@@ -439,15 +465,18 @@
     )(dkv)
     every = lax.all_gather(keyval_grad, "dp", axis=0)
     result = (seq, share, 2 * HK * DH)
-    partial = pl.pallas_call(
+    partial = local(
         weight_kernel,
-        out_shape=shape(result, half),
-        in_specs=[pl.BlockSpec(memory_space=pltpu.VMEM)] * (dp + 1),
-        out_specs=pl.BlockSpec(memory_space=pltpu.HBM),
-        scratch_shapes=[pltpu.VMEM(result, half), pltpu.SemaphoreType.DMA((4,))],
-        compiler_params=pltpu.CompilerParams(vmem_limit_bytes=SMALL_LIMIT),
-        name="weight",
-    )(*columns, every)
+        shape(result, half),
+        [*columns, every],
+        [
+            pltpu.VMEM((dp, seq * share, tokens), half),
+            pltpu.VMEM(every.shape, half),
+            pltpu.VMEM(result, half),
+            pltpu.SemaphoreType.DMA((1 + 4 * dp + 4,)),
+        ],
+        "weight",
+    )
     partial = exchange(partial, "seq")
     query_grad = local(
         unpack_kernel,

time: 182 us -> 177 us (0.973)
  blocking collectives: 28.5 us -> 32.4 us
  local copies, waits for them, and re-layouts: 5.49 us -> 2.52 us
  Pallas kernels: 39.8 us -> 37 us
  starting transfers between devices: 37.8 us -> 35.1 us
    all_gather x1, blocking collectives: 7.16 us -> 11.2 us  [shards(): every = lax.all_gather(keyval_grad, 'dp', axis=0)]
    pallas_call x4 -> x5, Pallas kernels: 10.3 us -> 14.1 us  [local(): pl.pallas_call(body, out_shape=out_shape, in_specs=[spec] * len(inputs),...]
    pallas_call x1, Pallas kernels: 25.8 us -> 22.2 us  [attention(): pl.pallas_call(attention_kernel, out_shape=(shape((planes, lines, 256, DH...]
    pallas_call x1 -> x0, Pallas kernels: 3 us -> none  [shards(): pl.pallas_call(weight_kernel, out_shape=shape(result, half), in_specs=[pl...]
    unnamed x22 -> x16, local copies, waits for them, and re-layouts: 3.82 us -> 0.83 us
    all_to_all x3, starting transfers between devices: 26.5 us -> 23.8 us  [exchange(): lax.all_to_all(array, axis, split_axis=0, concat_axis=0, axis_index_group...]
  transfers between devices with their start and end apart: 12 -> 12, of which waited for: 9 -> 9; matrix products, arithmetic and copies ran while one was open for 0% -> 0% of each run, Pallas kernels for 15% -> 14%
where the time goes in v7:
time: 177 us
  waiting for transfers between devices  69.4 us (39%)
  Pallas kernels  37 us (21%)
  starting transfers between devices  35.1 us (20%)
  blocking collectives  32.4 us (18%)
  local copies, waits for them, and re-layouts  2.52 us (1%)
    all_to_all x3, waiting for transfers between devices, exchange(): lax.all_to_all(array, axis, split_axis=0, concat_axis=0, axis_index_group...  34.9 us
    all_to_all x3, starting transfers between devices, exchange(): lax.all_to_all(array, axis, split_axis=0, concat_axis=0, axis_index_group...  23.8 us
    pallas_call x1, Pallas kernels, attention(): pl.pallas_call(attention_kernel, out_shape=(shape((planes, lines, 256, DH...  22.2 us
    all_to_all x2, blocking collectives, exchange(): lax.all_to_all(array, axis, split_axis=0, concat_axis=0, axis_index_group...  21.3 us
    ppermute x3, waiting for transfers between devices, shards(): parts[k] = lax.ppermute(parts[k], 'seq', partners(k))  21 us
    pallas_call x5, Pallas kernels, local(): pl.pallas_call(body, out_shape=out_shape, in_specs=[spec] * len(inputs),...  14.1 us
    ppermute x3, waiting for transfers between devices, shards(): dq[k] = lax.ppermute(dq[k], 'seq', partners(k))  13.5 us
    all_gather x1, blocking collectives, shards(): every = lax.all_gather(keyval_grad, 'dp', axis=0)  11.2 us
  transfers between devices with their start and end apart: 12, of which 9 were waited for; matrix products, arithmetic and copies ran while one was open for 0% of the time, Pallas kernels for 14%

profile of v7, /device:TPU:0, one launch (start us, length us, event | category | flops | bytes accessed | tf_op | source)
XLA Modules:
  0.0 177.5 jit_solution(16680338493269578659)
XLA Ops:
  0.6 3.6 %pack.1 = (bf16[4,272,128]{2,1,0:T(8,128)(2,1)}, bf16[16,128,128]{2,1,0:T(8,128)(2,1)}, bf16[16,128,128]{2,1,0:T(8,128)(2,1)}, bf16[16,128,128]{2,1,0:T(8,128)(2...) custom-call(bf16[128,4096]{1,0:T(8,128)(2,1)} %bitcast.8, ...), custom_call_target="tpu_custom_call" | custom-call | tf_op jit(solution)/shard_map/pack/pallas_call | solution.py:182
  4.2 11.2 %all_to_all.25 = bf16[4,272,128]{2,1,0:T(8,128)(2,1)S(1)} all-to-all(bf16[4,272,128]{2,1,0:T(8,128)(2,1)} %get-tuple-element.45), channel_id=1, replica_groups={{0,32,64,96},{4,36,68,100},{8,40,72,104},{12,44,76,108},{16,48,80,112},..., dimensions={0} | all-to-all | bytes 557056 | tf_op jit(solution)/shard_map/all_to_all | solution.py:391
  15.5 1.7 broadcast_in_dim.12
  17.1 7.9 %all-to-all-start.1 = ((bf16[8,4,272,128]{3,2,1,0:T(8,128)(2,1)}), bf16[8,4,272,128]{3,2,1,0:T(8,128)(2,1)S(1)}, u32[]{:S(2)}, u32[]{:S(2)}) async-start(bf16[8,4,272,128]{3,2,1,0:T(8,128)(2,1)} %broadcast_in_dim.12), calls=%async_computation.1 | async-start | bytes 4456448 | tf_op jit(solution)/shard_map/all_to_all | solution.py:391
  25.6 2.1 %collective-permute-start.1 = (bf16[16,128,128]{2,1,0:T(8,128)(2,1)}, bf16[16,128,128]{2,1,0:T(8,128)(2,1)S(1)}, u32[]{:S(2)}, u32[]{:S(2)}) collective-permute-start(bf16[16,128,128]{2,1,0:T(8,128)(2,1)} %get-tuple-element.53), channel_id=1, source_target_pairs={{0,64},{4,68},{8,72},{12,76},{16,80},{20,84},{24,88},{28,92},{32,9... | collective-permute-start | bytes 1572872 | tf_op jit(solution)/shard_map/ppermute | solution.py:435
  27.7 2.1 %collective-permute-start.2 = (bf16[16,128,128]{2,1,0:T(8,128)(2,1)S(1)}, bf16[16,128,128]{2,1,0:T(8,128)(2,1)}, u32[]{:S(2)}, u32[]{:S(2)}) collective-permute-start(bf16[16,128,128]{2,1,0:T(8,128)(2,1)S(1)} %copy-done.4), channel_id=1, source_target_pairs={{0,96},{4,100},{8,104},{12,108},{16,112},{20,116},{24,120},{28,124... | collective-permute-start | bytes 1572872 | tf_op jit(solution)/shard_map/ppermute | solution.py:435
  29.8 10.4 %collective-permute-done.refs_2_ = bf16[16,128,128]{2,1,0:T(8,128)(2,1)S(1)} collective-permute-done((bf16[16,128,128]{2,1,0:T(8,128)(2,1)}, bf16[16,128,128]{2,1,0:T(8,128)(2,1)S(1)}, u32[]{:S(2)}, u32[]{:S(2)}) %collective-permute-start) | collective-permute-done | bytes 524320 | tf_op jit(solution)/shard_map/ppermute | solution.py:435
  40.1 9.0 %collective-permute-done.1.refs_3_ = bf16[16,128,128]{2,1,0:T(8,128)(2,1)S(1)} collective-permute-done((bf16[16,128,128]{2,1,0:T(8,128)(2,1)}, bf16[16,128,128]{2,1,0:T(8,128)(2,1)S(1)}, u32[]{:S(2)}, u32[]{:S(2)}) %collective-permute-start.1) | collective-permute-done | bytes 524320 | tf_op jit(solution)/shard_map/ppermute | solution.py:435
  51.6 3.9 %all-to-all-done.1.refs_0_ = bf16[8,4,272,128]{3,2,1,0:T(8,128)(2,1)S(1)} async-done(((bf16[8,4,272,128]{3,2,1,0:T(8,128)(2,1)}), bf16[8,4,272,128]{3,2,1,0:T(8,128)(2,1)S(1)}, u32[]{:S(2)}, u32[]{:S(2)}) %all-to-all-start.1) | async-done | bytes 2228256 | tf_op jit(solution)/shard_map/all_to_all | solution.py:391
  57.4 22.2 %attention.1 = (bf16[8,4,256,128]{3,2,1,0:T(8,128)(2,1)}, bf16[8,128,128]{2,1,0:T(8,128)(2,1)}, bf16[8,128,128]{2,1,0:T(8,128)(2,1)}, bf16[8,128,128]{2,1,0:T(8,128)(2,1)}, bf16[8,128,128]{2,1,0:T(8,128)(2,1)}) custom-call(bf16[8,4,272,128]{3,2,1,0:T(8,128)(2,1)} %copy-done, bf16[16,128,128]{2,1,0:T(8,128)(2,1)} %get-tuple-element.60.refs_1_, ...), custom_call_target="tpu_custom_call" | custom-call | flops 10000000000 | bytes 8000000 | tf_op jit(solution)/shard_map/attention/pallas_call | solution.py:201
  79.7 10.4 %all-to-all-start.2 = ((bf16[8,4,256,128]{3,2,1,0:T(8,128)(2,1)}), bf16[8,4,256,128]{3,2,1,0:T(8,128)(2,1)}, u32[]{:S(2)}, u32[]{:S(2)}) async-start(bf16[8,4,256,128]{3,2,1,0:T(8,128)(2,1)} %get-tuple-element.73), calls=%async_computation.2 | async-start | bytes 4194304 | tf_op jit(solution)/shard_map/all_to_all | solution.py:391
  90.3 3.3 %collective-permute-start.7 = (bf16[8,128,128]{2,1,0:T(8,128)(2,1)S(1)}, bf16[8,128,128]{2,1,0:T(8,128)(2,1)}, u32[]{:S(2)}, u32[]{:S(2)}) collective-permute-start(bf16[8,128,128]{2,1,0:T(8,128)(2,1)S(1)} %copy-done.6), channel_id=1, source_target_pairs={{0,64},{4,68},{8,72},{12,76},{16,80},{20,84},{24,88},{28,92},{32,9... | collective-permute-start | bytes 786440 | tf_op jit(solution)/shard_map/ppermute | solution.py:444
  94.8 4.6 %collective-permute-done.6.refs_1_ = bf16[8,128,128]{2,1,0:T(8,128)(2,1)} collective-permute-done((bf16[8,128,128]{2,1,0:T(8,128)(2,1)S(1)}, bf16[8,128,128]{2,1,0:T(8,128)(2,1)}, u32[]{:S(2)}, u32[]{:S(2)}) %collective-permute-start.6) | collective-permute-done | bytes 262176 | tf_op jit(solution)/shard_map/ppermute | solution.py:444
  99.4 6.4 %collective-permute-done.7.refs_2_ = bf16[8,128,128]{2,1,0:T(8,128)(2,1)} collective-permute-done((bf16[8,128,128]{2,1,0:T(8,128)(2,1)S(1)}, bf16[8,128,128]{2,1,0:T(8,128)(2,1)}, u32[]{:S(2)}, u32[]{:S(2)}) %collective-permute-start.7) | collective-permute-done | bytes 262176 | tf_op jit(solution)/shard_map/ppermute | solution.py:444
  105.8 2.6 %collective-permute-done.8.refs_3_ = bf16[8,128,128]{2,1,0:T(8,128)(2,1)} collective-permute-done((bf16[8,128,128]{2,1,0:T(8,128)(2,1)S(1)}, bf16[8,128,128]{2,1,0:T(8,128)(2,1)}, u32[]{:S(2)}, u32[]{:S(2)}) %collective-permute-start.8) | collective-permute-done | bytes 262176 | tf_op jit(solution)/shard_map/ppermute | solution.py:444
  108.4 13.8 %all-to-all-done.2.part_hbm = bf16[8,4,256,128]{3,2,1,0:T(8,128)(2,1)} async-done(((bf16[8,4,256,128]{3,2,1,0:T(8,128)(2,1)}), bf16[8,4,256,128]{3,2,1,0:T(8,128)(2,1)}, u32[]{:S(2)}, u32[]{:S(2)}) %all-to-all-start.2) | async-done | bytes 2097184 | tf_op jit(solution)/shard_map/all_to_all | solution.py:391
  122.1 2.5 %gather.1 = bf16[4,256,128]{2,1,0:T(8,128)(2,1)} custom-call(bf16[8,4,256,128]{3,2,1,0:T(8,128)(2,1)} %all-to-all-done.2.part_hbm), custom_call_target="tpu_custom_call" | custom-call | tf_op jit(solution)/shard_map/gather/pallas_call | solution.py:182
  124.7 10.1 %all_to_all.26.part_ref = bf16[4,256,128]{2,1,0:T(8,128)(2,1)S(1)} all-to-all(bf16[4,256,128]{2,1,0:T(8,128)(2,1)} %gather.1), channel_id=1, replica_groups={{0,32,64,96},{4,36,68,100},{8,40,72,104},{12,44,76,108},{16,48,80,112},..., dimensions={0} | all-to-all | bytes 524288 | tf_op jit(solution)/shard_map/all_to_all | solution.py:391
  135.5 11.2 %all-gather = bf16[512,512]{1,0:T(8,128)(2,1)} all-gather(bf16[128,512]{1,0:T(8,128)(2,1)} %combine.1), channel_id=2, replica_groups=mesh['seq'=32,'dp'=4] {'dp'}, dimensions={0}, use_global_device_ids=true | all-gather | bytes 655360 | tf_op jit(solution)/shard_map/all_gather | solution.py:466
  146.6 3.8 %weight.1 = bf16[32,32,512]{2,1,0:T(8,128)(2,1)} custom-call(bf16[1024,128]{1,0:T(8,128)(2,1)} %get-tuple-element.83.refs_0_, bf16[1024,128]{1,0:T(8,128)(2,1)} %copy-done.1, bf16[1024,128]{1,0:T(8,128)(2,1)} %collective-permute-done.4.refs_2_, bf16[1024,128]{1,0:T(8,128)(2,1)} %collective-permute-done.5.refs_3_, bf16[4,128,512]{2,1,0:T(8,128)(2,1)} %bitcast.7), custom_call_target="tpu_custom_call" | custom-call | tf_op jit(solution)/shard_map/weight/pallas_call | solution.py:182
  150.5 5.5 %all-to-all-start.4 = ((bf16[32,32,512]{2,1,0:T(8,128)(2,1)}), bf16[32,32,512]{2,1,0:T(8,128)(2,1)}, u32[]{:S(2)}, u32[]{:S(2)}) async-start(bf16[32,32,512]{2,1,0:T(8,128)(2,1)} %weight.1), calls=%async_computation.4 | async-start | bytes 2097152 | tf_op jit(solution)/shard_map/all_to_all | solution.py:391
  155.9 2.3 %unpack.1 = bf16[128,4096]{1,0:T(8,128)(2,1)} custom-call(bf16[8,128,128]{2,1,0:T(8,128)(2,1)} %get-tuple-element.78.refs_0_, bf16[8,128,128]{2,1,0:T(8,128)(2,1)} %collective-permute-done.6.refs_1_, bf16[8,128,128]{2,1,0:T(8,128)(2,1)} %collective-permute-done.7.refs_2_, bf16[8,128,128]{2,1,0:T(8,128)(2,1)} %collective-permute-done.8.refs_3_), custom_call_target="tpu_custom_call" | custom-call | tf_op jit(solution)/shard_map/unpack/pallas_call | solution.py:182
  158.2 17.2 %all-to-all-done.4.part_hbm = bf16[32,32,512]{2,1,0:T(8,128)(2,1)} async-done(((bf16[32,32,512]{2,1,0:T(8,128)(2,1)}), bf16[32,32,512]{2,1,0:T(8,128)(2,1)}, u32[]{:S(2)}, u32[]{:S(2)}) %all-to-all-start.4) | async-done | bytes 1048608 | tf_op jit(solution)/shard_map/all_to_all | solution.py:391
  175.4 1.9 %total.1 = f32[32,512]{1,0:T(8,128)} custom-call(bf16[32,32,512]{2,1,0:T(8,128)(2,1)} %all-to-all-done.4.part_hbm), custom_call_target="tpu_custom_call" | custom-call | tf_op jit(solution)/shard_map/total/pallas_call | solution.py:182
  (27 shorter events, 7.1 us)
Async XLA Ops:
  17.1 10.6 %copy-start.4 = (bf16[16,128,128]{2,1,0:T(8,128)(2,1)S(1)}, bf16[16,128,128]{2,1,0:T(8,128)(2,1)}, u32[]{:S(2)}) copy-start(bf16[16,128,128]{2,1,0:T(8,128)(2,1)} %get-tuple-element.54) | copy-start | bytes 1572868
  17.1 38.4 %all-to-all-start.1 = ((bf16[8,4,272,128]{3,2,1,0:T(8,128)(2,1)}), bf16[8,4,272,128]{3,2,1,0:T(8,128)(2,1)S(1)}, u32[]{:S(2)}, u32[]{:S(2)}) async-start(bf16[8,4,272,128]{3,2,1,0:T(8,128)(2,1)} %broadcast_in_dim.12), calls=%async_computation.1 | async-start | bytes 4456448 | tf_op jit(solution)/shard_map/all_to_all | solution.py:391
  25.1 15.1 %collective-permute-start = (bf16[16,128,128]{2,1,0:T(8,128)(2,1)}, bf16[16,128,128]{2,1,0:T(8,128)(2,1)S(1)}, u32[]{:S(2)}, u32[]{:S(2)}) collective-permute-start(bf16[16,128,128]{2,1,0:T(8,128)(2,1)} %get-tuple-element.52), channel_id=1, source_target_pairs={{0,32},{4,36},{8,40},{12,44},{16,48},{20,52},{24,56},{28,60},{32,0... | collective-permute-start | bytes 1572872 | tf_op jit(solution)/shard_map/ppermute | solution.py:435
  25.6 23.5 %collective-permute-start.1 = (bf16[16,128,128]{2,1,0:T(8,128)(2,1)}, bf16[16,128,128]{2,1,0:T(8,128)(2,1)S(1)}, u32[]{:S(2)}, u32[]{:S(2)}) collective-permute-start(bf16[16,128,128]{2,1,0:T(8,128)(2,1)} %get-tuple-element.53), channel_id=1, source_target_pairs={{0,64},{4,68},{8,72},{12,76},{16,80},{20,84},{24,88},{28,92},{32,9... | collective-permute-start | bytes 1572872 | tf_op jit(solution)/shard_map/ppermute | solution.py:435
  27.7 23.9 %collective-permute-start.2 = (bf16[16,128,128]{2,1,0:T(8,128)(2,1)S(1)}, bf16[16,128,128]{2,1,0:T(8,128)(2,1)}, u32[]{:S(2)}, u32[]{:S(2)}) collective-permute-start(bf16[16,128,128]{2,1,0:T(8,128)(2,1)S(1)} %copy-done.4), channel_id=1, source_target_pairs={{0,96},{4,100},{8,104},{12,108},{16,112},{20,116},{24,120},{28,124... | collective-permute-start | bytes 1572872 | tf_op jit(solution)/shard_map/ppermute | solution.py:435
  40.1 17.3 %copy-start.2 = (bf16[16,128,128]{2,1,0:T(8,128)(2,1)}, bf16[16,128,128]{2,1,0:T(8,128)(2,1)S(1)}, u32[]{:S(2)}) copy-start(bf16[16,128,128]{2,1,0:T(8,128)(2,1)S(1)} %collective-permute-done.refs_2_) | copy-start | bytes 1572868
  49.1 0.8 copy-start.3
  55.5 1.9 %copy-start = (bf16[8,4,272,128]{3,2,1,0:T(8,128)(2,1)}, bf16[8,4,272,128]{3,2,1,0:T(8,128)(2,1)S(1)}, u32[]{:S(2)}) copy-start(bf16[8,4,272,128]{3,2,1,0:T(8,128)(2,1)S(1)} %all-to-all-done.1.refs_0_) | copy-start | bytes 6684676
  55.5 24.1 %collective-permute-start.3 = (bf16[1024,128]{1,0:T(8,128)(2,1)}, bf16[1024,128]{1,0:T(8,128)(2,1)S(1)}, u32[]{:S(2)}, u32[]{:S(2)}) collective-permute-start(bf16[1024,128]{1,0:T(8,128)(2,1)} %get-tuple-element.70), channel_id=1, source_target_pairs={{0,1},{1,0},{2,3},{3,2},{4,5},{5,4},{6,7},{7,6},{8,9},{9,8},{10,11... | collective-permute-start | bytes 786440 | tf_op jit(solution)/shard_map/ppermute | solution.py:440
  55.5 24.1 %collective-permute-start.4 = (bf16[1024,128]{1,0:T(8,128)(2,1)}, bf16[1024,128]{1,0:T(8,128)(2,1)}, u32[]{:S(2)}, u32[]{:S(2)}) collective-permute-start(bf16[1024,128]{1,0:T(8,128)(2,1)} %get-tuple-element.71), channel_id=1, source_target_pairs={{0,2},{1,3},{2,0},{3,1},{4,6},{5,7},{6,4},{7,5},{8,10},{9,11},{10,... | collective-permute-start | bytes 786440 | tf_op jit(solution)/shard_map/ppermute | solution.py:440
  56.5 23.1 %collective-permute-start.5 = (bf16[1024,128]{1,0:T(8,128)(2,1)}, bf16[1024,128]{1,0:T(8,128)(2,1)}, u32[]{:S(2)}, u32[]{:S(2)}) collective-permute-start(bf16[1024,128]{1,0:T(8,128)(2,1)} %get-tuple-element.72), channel_id=1, source_target_pairs={{0,3},{1,2},{2,1},{3,0},{4,7},{5,6},{6,5},{7,4},{8,11},{9,10},{10,... | collective-permute-start | bytes 786440 | tf_op jit(solution)/shard_map/ppermute | solution.py:440
  79.6 10.5 %copy-start.7 = (bf16[8,128,128]{2,1,0:T(8,128)(2,1)S(1)}, bf16[8,128,128]{2,1,0:T(8,128)(2,1)}, u32[]{:S(2)}) copy-start(bf16[8,128,128]{2,1,0:T(8,128)(2,1)} %get-tuple-element.75) | copy-start | bytes 786436
  79.6 10.7 %copy-start.6 = (bf16[8,128,128]{2,1,0:T(8,128)(2,1)S(1)}, bf16[8,128,128]{2,1,0:T(8,128)(2,1)}, u32[]{:S(2)}) copy-start(bf16[8,128,128]{2,1,0:T(8,128)(2,1)} %get-tuple-element.76) | copy-start | bytes 786436
  79.6 14.0 %copy-start.5 = (bf16[8,128,128]{2,1,0:T(8,128)(2,1)S(1)}, bf16[8,128,128]{2,1,0:T(8,128)(2,1)}, u32[]{:S(2)}) copy-start(bf16[8,128,128]{2,1,0:T(8,128)(2,1)} %get-tuple-element.77) | copy-start | bytes 786436
  79.6 45.1 %copy-start.1 = (bf16[1024,128]{1,0:T(8,128)(2,1)}, bf16[1024,128]{1,0:T(8,128)(2,1)S(1)}, u32[]{:S(2)}) copy-start(bf16[1024,128]{1,0:T(8,128)(2,1)S(1)} %collective-permute-done.3.refs_1_) | copy-start | bytes 786436
  79.7 42.5 %all-to-all-start.2 = ((bf16[8,4,256,128]{3,2,1,0:T(8,128)(2,1)}), bf16[8,4,256,128]{3,2,1,0:T(8,128)(2,1)}, u32[]{:S(2)}, u32[]{:S(2)}) async-start(bf16[8,4,256,128]{3,2,1,0:T(8,128)(2,1)} %get-tuple-element.73), calls=%async_computation.2 | async-start | bytes 4194304 | tf_op jit(solution)/shard_map/all_to_all | solution.py:391
  90.1 9.3 %collective-permute-start.6 = (bf16[8,128,128]{2,1,0:T(8,128)(2,1)S(1)}, bf16[8,128,128]{2,1,0:T(8,128)(2,1)}, u32[]{:S(2)}, u32[]{:S(2)}) collective-permute-start(bf16[8,128,128]{2,1,0:T(8,128)(2,1)S(1)} %copy-done.7), channel_id=1, source_target_pairs={{0,32},{4,36},{8,40},{12,44},{16,48},{20,52},{24,56},{28,60},{32,0... | collective-permute-start | bytes 786440 | tf_op jit(solution)/shard_map/ppermute | solution.py:444
  90.3 15.5 %collective-permute-start.7 = (bf16[8,128,128]{2,1,0:T(8,128)(2,1)S(1)}, bf16[8,128,128]{2,1,0:T(8,128)(2,1)}, u32[]{:S(2)}, u32[]{:S(2)}) collective-permute-start(bf16[8,128,128]{2,1,0:T(8,128)(2,1)S(1)} %copy-done.6), channel_id=1, source_target_pairs={{0,64},{4,68},{8,72},{12,76},{16,80},{20,84},{24,88},{28,92},{32,9... | collective-permute-start | bytes 786440 | tf_op jit(solution)/shard_map/ppermute | solution.py:444
  93.7 14.7 %collective-permute-start.8 = (bf16[8,128,128]{2,1,0:T(8,128)(2,1)S(1)}, bf16[8,128,128]{2,1,0:T(8,128)(2,1)}, u32[]{:S(2)}, u32[]{:S(2)}) collective-permute-start(bf16[8,128,128]{2,1,0:T(8,128)(2,1)S(1)} %copy-done.5), channel_id=1, source_target_pairs={{0,96},{4,100},{8,104},{12,108},{16,112},{20,116},{24,120},{28,124... | collective-permute-start | bytes 786440 | tf_op jit(solution)/shard_map/ppermute | solution.py:444
  150.5 25.0 %all-to-all-start.4 = ((bf16[32,32,512]{2,1,0:T(8,128)(2,1)}), bf16[32,32,512]{2,1,0:T(8,128)(2,1)}, u32[]{:S(2)}, u32[]{:S(2)}) async-start(bf16[32,32,512]{2,1,0:T(8,128)(2,1)} %weight.1), calls=%async_computation.4 | async-start | bytes 2097152 | tf_op jit(solution)/shard_map/all_to_all | solution.py:391

commit v8 on v7

--- a/solution.py
+++ b/solution.py
@@ -64,7 +64,7 @@
 
     dk_ref[...] = jnp.zeros_like(dk_ref)
     dv_ref[...] = jnp.zeros_like(dv_ref)
-    for copy in arrivals:
+    for copy in arrivals[: 2 * lines]:
         copy.wait()
 
     def rows(first, count, slot):
@@ -89,6 +89,8 @@
 
     def query_block(i, _):
         j, part = i // turns, i % turns
+        for k in range(lines):
+            pl.when(i == k * turns)(arrivals[2 * lines + k].wait)
         first = (jnp.bitwise_xor(line, j) * planes + plane) * 128
         q = q_ref[j, pl.ds(part * some, some)].reshape(BQ, DH)
         cotan = q_ref[j, pl.ds(heads + part * some, some)].reshape(BQ, DH)
@@ -227,49 +229,59 @@
     )(kv, *parts)
 
 
-def pack_kernel(q_hbm, g_hbm, kv_hbm, seg_hbm, h_hbm, *rest):
-    kv_out, q_out, cols_out = rest[0], rest[1:5], rest[5:9]
-    q_ref, g_ref, kv_ref, seg_ref, h_ref, kv_send, q_send, cols_ref, in_sems, out_sems = rest[9:]
+def share_kernel(kv_hbm, seg_hbm, out_hbm, kv_ref, seg_ref, out_ref, sems):
+    pairs = [(seg_hbm, seg_ref), (kv_hbm, kv_ref)]
+    arrivals = [pltpu.make_async_copy(*pair, sems.at[i]) for i, pair in enumerate(pairs)]
+    for copy in arrivals:
+        copy.start()
+    tokens = kv_ref.shape[0]
+    lines = out_ref.shape[0]
+    arrivals[0].wait()
+    numbers = jnp.broadcast_to(seg_ref[...].astype(jnp.bfloat16), (SEGMENT_ROWS, tokens))
+    arrivals[1].wait()
+    for j in range(lines):
+        k = (j * HK // lines) * DH
+        v = HK * DH + k
+        out_ref[j, :tokens, :] = kv_ref[:, k : k + DH]
+        out_ref[j, tokens : 2 * tokens, :] = kv_ref[:, v : v + DH]
+        out_ref[j, 2 * tokens :, :] = numbers
+    copy = pltpu.make_async_copy(out_ref, out_hbm, sems.at[2])
+    copy.start()
+    copy.wait()
+
+
+def pack_kernel(q_hbm, g_hbm, h_hbm, *rest):
+    q_out, cols_out = rest[:4], rest[4:8]
+    q_ref, g_ref, h_ref, q_send, cols_ref, in_sems, out_sems = rest[8:]
     line, core = lax.axis_index("seq") // PLANES, lax.axis_index("dp")
-    pairs = [(seg_hbm, seg_ref), (kv_hbm, kv_ref), (q_hbm, q_ref), (g_hbm, g_ref), (h_hbm, h_ref)]
+    pairs = [(q_hbm, q_ref), (g_hbm, g_ref), (h_hbm, h_ref)]
     arrivals = [pltpu.make_async_copy(*pair, in_sems.at[i]) for i, pair in enumerate(pairs)]
     for copy in arrivals:
         copy.start()
-    tokens = q_ref.shape[0]
     lines, heads = q_send.shape[0], q_send.shape[1] // 2
     dp, width = cols_ref.shape[0], cols_ref.shape[1]
     share = h_ref.shape[1] // (HQ * dp)
-    departures = [pltpu.make_async_copy(kv_send, kv_out, out_sems.at[0])]
+    departures = []
     for k in range(lines):
-        departures.append(pltpu.make_async_copy(q_send.at[k], q_out[k], out_sems.at[1 + k]))
+        departures.append(pltpu.make_async_copy(q_send.at[k], q_out[k], out_sems.at[k]))
     for k in range(dp):
-        sem = out_sems.at[1 + lines + k]
+        sem = out_sems.at[lines + k]
         departures.append(pltpu.make_async_copy(cols_ref.at[k], cols_out[k], sem))
-    arrivals[0].wait()
-    numbers = jnp.broadcast_to(seg_ref[...].astype(jnp.bfloat16), (SEGMENT_ROWS, tokens))
-    arrivals[1].wait()
-    for j in range(lines):
-        k = (j * heads // (HQ // HK)) * DH
-        v = HK * DH + k
-        kv_send[j, :tokens, :] = kv_ref[:, k : k + DH]
-        kv_send[j, tokens : 2 * tokens, :] = kv_ref[:, v : v + DH]
-        kv_send[j, 2 * tokens :, :] = numbers
-    departures[0].start()
     for kind, ref in ((0, q_ref), (1, g_ref)):
-        arrivals[2 + kind].wait()
+        arrivals[kind].wait()
         for h in range(HQ):
             to = jnp.bitwise_xor(line, h // heads)
             q_send[to, kind * heads + h % heads] = ref[:, h * DH : (h + 1) * DH]
-    for copy in departures[1 : 1 + lines]:
-        copy.start()
-    arrivals[4].wait()
+    for copy in departures[:lines]:
+        copy.start()
+    arrivals[2].wait()
     span = share * dp
     for s in range(width // share):
         turned = h_ref[:, s * span : (s + 1) * span].T
         for r in range(dp):
             part = turned[r * share : (r + 1) * share]
             cols_ref[jnp.bitwise_xor(core, r), s * share : (s + 1) * share, :] = part
-    for copy in departures[1 + lines :]:
+    for copy in departures[lines:]:
         copy.start()
     for copy in departures:
         copy.wait()
@@ -278,20 +290,23 @@
 def gather_kernel(part_hbm, out_hbm, part_ref, out_ref, sems):
     planes, lines = part_ref.shape[0], part_ref.shape[1]
     arrivals = [
-        pltpu.make_async_copy(part_hbm.at[w], part_ref.at[w], sems.at[w]) for w in range(planes)
+        pltpu.make_async_copy(part_hbm.at[:, j], part_ref.at[:, j], sems.at[j])
+        for j in range(lines)
     ]
     for copy in arrivals:
         copy.start()
-    for copy in arrivals:
-        copy.wait()
-    for j in range(lines):
+    departures = []
+    for j in range(lines):
+        arrivals[j].wait()
         total = part_ref[0, j].astype(jnp.float32)
         for w in range(1, planes):
             total += part_ref[w, j].astype(jnp.float32)
         out_ref[j] = total.astype(jnp.bfloat16)
-    copy = pltpu.make_async_copy(out_ref, out_hbm, sems.at[planes])
-    copy.start()
-    copy.wait()
+        sem = sems.at[lines + j]
+        departures.append(pltpu.make_async_copy(out_ref.at[j], out_hbm.at[j], sem))
+        departures[j].start()
+    for copy in departures:
+        copy.wait()
 
 
 def combine_kernel(part_ref, out_ref):
@@ -407,29 +422,36 @@
     def partners(k):
         return [(p, (p // PLANES ^ k) * PLANES + p % PLANES) for p in range(seq)]
 
-    inputs = [queries[0], out_grad[0], keyvals[0], segment, hidden[0]]
     shared = (lines, 2 * tokens + SEGMENT_ROWS, DH)
-    kv, *parts = local(
+    kv = local(
+        share_kernel,
+        shape(shared, half),
+        [keyvals[0], segment],
+        [
+            pltpu.VMEM(keyvals.shape[1:], half),
+            pltpu.VMEM(segment.shape, segment.dtype),
+            pltpu.VMEM(shared, half),
+            pltpu.SemaphoreType.DMA((3,)),
+        ],
+        "share",
+    )
+    parts = local(
         pack_kernel,
-        (shape(shared, half),)
-        + (shape((2 * heads, tokens, DH), half),) * lines
+        (shape((2 * heads, tokens, DH), half),) * lines
         + (shape((seq * share, tokens), half),) * dp,
-        inputs,
+        [queries[0], out_grad[0], hidden[0]],
         [
             pltpu.VMEM(queries.shape[1:], half),
             pltpu.VMEM(out_grad.shape[1:], half),
-            pltpu.VMEM(keyvals.shape[1:], half),
-            pltpu.VMEM(segment.shape, segment.dtype),
             pltpu.VMEM(hidden.shape[1:], half),
-            pltpu.VMEM(shared, half),
             pltpu.VMEM((lines, 2 * heads, tokens, DH), half),
             pltpu.VMEM((dp, seq * share, tokens), half),
-            pltpu.SemaphoreType.DMA((5,)),
-            pltpu.SemaphoreType.DMA((1 + lines + dp,)),
+            pltpu.SemaphoreType.DMA((3,)),
+            pltpu.SemaphoreType.DMA((lines + dp,)),
         ],
         "pack",
     )
-    parts, columns = parts[:lines], parts[lines:]
+    parts, columns = list(parts[:lines]), list(parts[lines:])
     kv, parts = lax.optimization_barrier((exchange(kv, "seq", along), parts))
     for k in range(1, lines):
         parts[k] = lax.ppermute(parts[k], "seq", partners(k))
@@ -450,7 +472,7 @@
         [
             pltpu.VMEM(dkv.shape, half),
             pltpu.VMEM(dkv.shape[1:], half),
-            pltpu.SemaphoreType.DMA((PLANES + 1,)),
+            pltpu.SemaphoreType.DMA((2 * lines,)),
         ],
         "gather",
     )

time: 177 us -> 174 us (0.983); the launches traced: 177 us -> 172 us
  blocking collectives: 32.4 us -> 18.8 us
  starting transfers between devices: 35.1 us -> 40 us
  waiting for transfers between devices: 69.4 us -> 71.8 us
    all_to_all x2 -> x1, blocking collectives: 21.3 us -> 11.6 us  [exchange(): lax.all_to_all(array, axis, split_axis=0, concat_axis=0, axis_index_group...]
    all_to_all x3 -> x4, starting transfers between devices: 23.8 us -> 28.7 us  [exchange(): lax.all_to_all(array, axis, split_axis=0, concat_axis=0, axis_index_group...]
    all_gather x1, blocking collectives: 11.2 us -> 7.15 us  [shards(): every = lax.all_gather(keyval_grad, 'dp', axis=0)]
    pallas_call x5 -> x6, Pallas kernels: 14.1 us -> 15.4 us  [local(): pl.pallas_call(body, out_shape=out_shape, in_specs=[spec] * len(inputs),...]
    all_to_all x3 -> x4, waiting for transfers between devices: 34.9 us -> 35.8 us  [exchange(): lax.all_to_all(array, axis, split_axis=0, concat_axis=0, axis_index_group...]
  transfers between devices with their start and end apart: 12 -> 13, of which waited for: 9 -> 10; matrix products, arithmetic and copies ran while one was open for 0% -> 0% of each run, Pallas kernels for 14% -> 16%
where the time goes in v8:
time: 174 us; the launch traced here: 172 us
  waiting for transfers between devices  71.8 us (41%)
  starting transfers between devices  40 us (23%)
  Pallas kernels  37.7 us (22%)
  blocking collectives  18.8 us (11%)
  local copies, waits for them, and re-layouts  2.5 us (1%)
    all_to_all x4, waiting for transfers between devices, exchange(): lax.all_to_all(array, axis, split_axis=0, concat_axis=0, axis_index_group...  35.8 us
    all_to_all x4, starting transfers between devices, exchange(): lax.all_to_all(array, axis, split_axis=0, concat_axis=0, axis_index_group...  28.7 us
    pallas_call x1, Pallas kernels, attention(): pl.pallas_call(attention_kernel, out_shape=(shape((planes, lines, 256, DH...  21.6 us
    ppermute x3, waiting for transfers between devices, shards(): parts[k] = lax.ppermute(parts[k], 'seq', partners(k))  21 us
    pallas_call x6, Pallas kernels, local(): pl.pallas_call(body, out_shape=out_shape, in_specs=[spec] * len(inputs),...  15.4 us
    ppermute x3, waiting for transfers between devices, shards(): dq[k] = lax.ppermute(dq[k], 'seq', partners(k))  14.9 us
    all_to_all x1, blocking collectives, exchange(): lax.all_to_all(array, axis, split_axis=0, concat_axis=0, axis_index_group...  11.6 us
    all_gather x1, blocking collectives, shards(): every = lax.all_gather(keyval_grad, 'dp', axis=0)  7.15 us
  transfers between devices with their start and end apart: 13, of which 10 were waited for; matrix products, arithmetic and copies ran while one was open for 0% of the time, Pallas kernels for 16%

profile of v8, /device:TPU:0, one launch (start us, length us, event | category | flops | bytes accessed | tf_op | source)
XLA Modules:
  0.0 171.7 jit_solution(13577491777492610256)
XLA Ops:
  2.3 4.4 %all-to-all-start = ((bf16[4,272,128]{2,1,0:T(8,128)(2,1)}), bf16[4,272,128]{2,1,0:T(8,128)(2,1)S(1)}, u32[]{:S(2)}, u32[]{:S(2)}) async-start(bf16[4,272,128]{2,1,0:T(8,128)(2,1)} %share.1), calls=%async_computation | async-start | bytes 557056 | tf_op jit(solution)/shard_map/all_to_all | solution.py:406
  6.7 3.5 %pack.1 = (bf16[16,128,128]{2,1,0:T(8,128)(2,1)}, bf16[16,128,128]{2,1,0:T(8,128)(2,1)}, bf16[16,128,128]{2,1,0:T(8,128)(2,1)}, bf16[16,128,128]{2,1,0:T(8,128)(...) custom-call(bf16[128,4096]{1,0:T(8,128)(2,1)} %bitcast.8, ...), custom_call_target="tpu_custom_call" | custom-call | tf_op jit(solution)/shard_map/pack/pallas_call | solution.py:184
  10.2 3.4 %all-to-all-done = bf16[4,272,128]{2,1,0:T(8,128)(2,1)S(1)} async-done(((bf16[4,272,128]{2,1,0:T(8,128)(2,1)}), bf16[4,272,128]{2,1,0:T(8,128)(2,1)S(1)}, u32[]{:S(2)}, u32[]{:S(2)}) %all-to-all-start) | async-done | bytes 278560 | tf_op jit(solution)/shard_map/all_to_all | solution.py:406
  15.2 7.9 %all-to-all-start.1 = ((bf16[8,4,272,128]{3,2,1,0:T(8,128)(2,1)}), bf16[8,4,272,128]{3,2,1,0:T(8,128)(2,1)S(1)}, u32[]{:S(2)}, u32[]{:S(2)}) async-start(bf16[8,4,272,128]{3,2,1,0:T(8,128)(2,1)} %broadcast_in_dim.12), calls=%async_computation.1 | async-start | bytes 4456448 | tf_op jit(solution)/shard_map/all_to_all | solution.py:406
  23.7 2.1 %collective-permute-start.1 = (bf16[16,128,128]{2,1,0:T(8,128)(2,1)}, bf16[16,128,128]{2,1,0:T(8,128)(2,1)S(1)}, u32[]{:S(2)}, u32[]{:S(2)}) collective-permute-start(bf16[16,128,128]{2,1,0:T(8,128)(2,1)} %get-tuple-element.51), channel_id=1, source_target_pairs={{0,64},{4,68},{8,72},{12,76},{16,80},{20,84},{24,88},{28,92},{32,9... | collective-permute-start | bytes 1572872 | tf_op jit(solution)/shard_map/ppermute | solution.py:457
  25.8 2.1 %collective-permute-start.2 = (bf16[16,128,128]{2,1,0:T(8,128)(2,1)S(1)}, bf16[16,128,128]{2,1,0:T(8,128)(2,1)}, u32[]{:S(2)}, u32[]{:S(2)}) collective-permute-start(bf16[16,128,128]{2,1,0:T(8,128)(2,1)S(1)} %copy-done.4), channel_id=1, source_target_pairs={{0,96},{4,100},{8,104},{12,108},{16,112},{20,116},{24,120},{28,124... | collective-permute-start | bytes 1572872 | tf_op jit(solution)/shard_map/ppermute | solution.py:457
  27.9 10.4 %collective-permute-done.refs_2_ = bf16[16,128,128]{2,1,0:T(8,128)(2,1)S(1)} collective-permute-done((bf16[16,128,128]{2,1,0:T(8,128)(2,1)}, bf16[16,128,128]{2,1,0:T(8,128)(2,1)S(1)}, u32[]{:S(2)}, u32[]{:S(2)}) %collective-permute-start) | collective-permute-done | bytes 524320 | tf_op jit(solution)/shard_map/ppermute | solution.py:457
  38.2 9.0 %collective-permute-done.1.refs_3_ = bf16[16,128,128]{2,1,0:T(8,128)(2,1)S(1)} collective-permute-done((bf16[16,128,128]{2,1,0:T(8,128)(2,1)}, bf16[16,128,128]{2,1,0:T(8,128)(2,1)S(1)}, u32[]{:S(2)}, u32[]{:S(2)}) %collective-permute-start.1) | collective-permute-done | bytes 524320 | tf_op jit(solution)/shard_map/ppermute | solution.py:457
  49.7 4.0 %all-to-all-done.1.refs_0_ = bf16[8,4,272,128]{3,2,1,0:T(8,128)(2,1)S(1)} async-done(((bf16[8,4,272,128]{3,2,1,0:T(8,128)(2,1)}), bf16[8,4,272,128]{3,2,1,0:T(8,128)(2,1)S(1)}, u32[]{:S(2)}, u32[]{:S(2)}) %all-to-all-start.1) | async-done | bytes 2228256 | tf_op jit(solution)/shard_map/all_to_all | solution.py:406
  55.5 21.6 %attention.1 = (bf16[8,4,256,128]{3,2,1,0:T(8,128)(2,1)}, bf16[8,128,128]{2,1,0:T(8,128)(2,1)}, bf16[8,128,128]{2,1,0:T(8,128)(2,1)}, bf16[8,128,128]{2,1,0:T(8,128)(2,1)}, bf16[8,128,128]{2,1,0:T(8,128)(2,1)}) custom-call(bf16[8,4,272,128]{3,2,1,0:T(8,128)(2,1)} %copy-done, bf16[16,128,128]{2,1,0:T(8,128)(2,1)} %get-tuple-element.58.refs_1_, ...), custom_call_target="tpu_custom_call" | custom-call | flops 10000000000 | bytes 8000000 | tf_op jit(solution)/shard_map/attention/pallas_call | solution.py:203
  77.2 10.6 %all-to-all-start.2 = ((bf16[8,4,256,128]{3,2,1,0:T(8,128)(2,1)}), bf16[8,4,256,128]{3,2,1,0:T(8,128)(2,1)}, u32[]{:S(2)}, u32[]{:S(2)}) async-start(bf16[8,4,256,128]{3,2,1,0:T(8,128)(2,1)} %get-tuple-element.71), calls=%async_computation.2 | async-start | bytes 4194304 | tf_op jit(solution)/shard_map/all_to_all | solution.py:406
  87.9 3.5 %collective-permute-start.7 = (bf16[8,128,128]{2,1,0:T(8,128)(2,1)S(1)}, bf16[8,128,128]{2,1,0:T(8,128)(2,1)}, u32[]{:S(2)}, u32[]{:S(2)}) collective-permute-start(bf16[8,128,128]{2,1,0:T(8,128)(2,1)S(1)} %copy-done.6), channel_id=1, source_target_pairs={{0,64},{4,68},{8,72},{12,76},{16,80},{20,84},{24,88},{28,92},{32,9... | collective-permute-start | bytes 786440 | tf_op jit(solution)/shard_map/ppermute | solution.py:466
  92.6 3.0 %collective-permute-done.6.refs_1_ = bf16[8,128,128]{2,1,0:T(8,128)(2,1)} collective-permute-done((bf16[8,128,128]{2,1,0:T(8,128)(2,1)S(1)}, bf16[8,128,128]{2,1,0:T(8,128)(2,1)}, u32[]{:S(2)}, u32[]{:S(2)}) %collective-permute-start.6) | collective-permute-done | bytes 262176 | tf_op jit(solution)/shard_map/ppermute | solution.py:466
  95.5 8.3 %collective-permute-done.7.refs_2_ = bf16[8,128,128]{2,1,0:T(8,128)(2,1)} collective-permute-done((bf16[8,128,128]{2,1,0:T(8,128)(2,1)S(1)}, bf16[8,128,128]{2,1,0:T(8,128)(2,1)}, u32[]{:S(2)}, u32[]{:S(2)}) %collective-permute-start.7) | collective-permute-done | bytes 262176 | tf_op jit(solution)/shard_map/ppermute | solution.py:466
  103.8 3.6 %collective-permute-done.8.refs_3_ = bf16[8,128,128]{2,1,0:T(8,128)(2,1)} collective-permute-done((bf16[8,128,128]{2,1,0:T(8,128)(2,1)S(1)}, bf16[8,128,128]{2,1,0:T(8,128)(2,1)}, u32[]{:S(2)}, u32[]{:S(2)}) %collective-permute-start.8) | collective-permute-done | bytes 262176 | tf_op jit(solution)/shard_map/ppermute | solution.py:466
  107.5 11.3 %all-to-all-done.2.part_hbm = bf16[8,4,256,128]{3,2,1,0:T(8,128)(2,1)} async-done(((bf16[8,4,256,128]{3,2,1,0:T(8,128)(2,1)}), bf16[8,4,256,128]{3,2,1,0:T(8,128)(2,1)}, u32[]{:S(2)}, u32[]{:S(2)}) %all-to-all-start.2) | async-done | bytes 2097184 | tf_op jit(solution)/shard_map/all_to_all | solution.py:406
  118.8 2.3 %gather.1 = bf16[4,256,128]{2,1,0:T(8,128)(2,1)} custom-call(bf16[8,4,256,128]{3,2,1,0:T(8,128)(2,1)} %all-to-all-done.2.part_hbm), custom_call_target="tpu_custom_call" | custom-call | tf_op jit(solution)/shard_map/gather/pallas_call | solution.py:184
  121.1 11.6 %all_to_all.25.part_ref = bf16[4,256,128]{2,1,0:T(8,128)(2,1)S(1)} all-to-all(bf16[4,256,128]{2,1,0:T(8,128)(2,1)} %gather.1), channel_id=1, replica_groups={{0,32,64,96},{4,36,68,100},{8,40,72,104},{12,44,76,108},{16,48,80,112},..., dimensions={0} | all-to-all | bytes 524288 | tf_op jit(solution)/shard_map/all_to_all | solution.py:406
  133.4 7.2 %all-gather = bf16[512,512]{1,0:T(8,128)(2,1)} all-gather(bf16[128,512]{1,0:T(8,128)(2,1)} %combine.1), channel_id=2, replica_groups=mesh['seq'=32,'dp'=4] {'dp'}, dimensions={0}, use_global_device_ids=true | all-gather | bytes 655360 | tf_op jit(solution)/shard_map/all_gather | solution.py:488
  140.6 3.8 %weight.1 = bf16[32,32,512]{2,1,0:T(8,128)(2,1)} custom-call(bf16[1024,128]{1,0:T(8,128)(2,1)} %get-tuple-element.81.refs_0_, bf16[1024,128]{1,0:T(8,128)(2,1)} %copy-done.1, bf16[1024,128]{1,0:T(8,128)(2,1)} %collective-permute-done.4.refs_2_, bf16[1024,128]{1,0:T(8,128)(2,1)} %collective-permute-done.5.refs_3_, bf16[4,128,512]{2,1,0:T(8,128)(2,1)} %bitcast.7), custom_call_target="tpu_custom_call" | custom-call | tf_op jit(solution)/shard_map/weight/pallas_call | solution.py:184
  144.4 5.8 %all-to-all-start.4 = ((bf16[32,32,512]{2,1,0:T(8,128)(2,1)}), bf16[32,32,512]{2,1,0:T(8,128)(2,1)}, u32[]{:S(2)}, u32[]{:S(2)}) async-start(bf16[32,32,512]{2,1,0:T(8,128)(2,1)} %weight.1), calls=%async_computation.4 | async-start | bytes 2097152 | tf_op jit(solution)/shard_map/all_to_all | solution.py:406
  150.2 2.3 %unpack.1 = bf16[128,4096]{1,0:T(8,128)(2,1)} custom-call(bf16[8,128,128]{2,1,0:T(8,128)(2,1)} %get-tuple-element.76.refs_0_, bf16[8,128,128]{2,1,0:T(8,128)(2,1)} %collective-permute-done.6.refs_1_, bf16[8,128,128]{2,1,0:T(8,128)(2,1)} %collective-permute-done.7.refs_2_, bf16[8,128,128]{2,1,0:T(8,128)(2,1)} %collective-permute-done.8.refs_3_), custom_call_target="tpu_custom_call" | custom-call | tf_op jit(solution)/shard_map/unpack/pallas_call | solution.py:184
  152.5 17.2 %all-to-all-done.4.part_hbm = bf16[32,32,512]{2,1,0:T(8,128)(2,1)} async-done(((bf16[32,32,512]{2,1,0:T(8,128)(2,1)}), bf16[32,32,512]{2,1,0:T(8,128)(2,1)}, u32[]{:S(2)}, u32[]{:S(2)}) %all-to-all-start.4) | async-done | bytes 1048608 | tf_op jit(solution)/shard_map/all_to_all | solution.py:406
  169.7 1.9 %total.1 = f32[32,512]{1,0:T(8,128)} custom-call(bf16[32,32,512]{2,1,0:T(8,128)(2,1)} %all-to-all-done.4.part_hbm), custom_call_target="tpu_custom_call" | custom-call | tf_op jit(solution)/shard_map/total/pallas_call | solution.py:184
  (29 shorter events, 10.2 us)
Async XLA Ops:
  2.3 11.2 %all-to-all-start = ((bf16[4,272,128]{2,1,0:T(8,128)(2,1)}), bf16[4,272,128]{2,1,0:T(8,128)(2,1)S(1)}, u32[]{:S(2)}, u32[]{:S(2)}) async-start(bf16[4,272,128]{2,1,0:T(8,128)(2,1)} %share.1), calls=%async_computation | async-start | bytes 557056 | tf_op jit(solution)/shard_map/all_to_all | solution.py:406
  15.2 10.6 %copy-start.4 = (bf16[16,128,128]{2,1,0:T(8,128)(2,1)S(1)}, bf16[16,128,128]{2,1,0:T(8,128)(2,1)}, u32[]{:S(2)}) copy-start(bf16[16,128,128]{2,1,0:T(8,128)(2,1)} %get-tuple-element.52) | copy-start | bytes 1572868
  15.2 38.4 %all-to-all-start.1 = ((bf16[8,4,272,128]{3,2,1,0:T(8,128)(2,1)}), bf16[8,4,272,128]{3,2,1,0:T(8,128)(2,1)S(1)}, u32[]{:S(2)}, u32[]{:S(2)}) async-start(bf16[8,4,272,128]{3,2,1,0:T(8,128)(2,1)} %broadcast_in_dim.12), calls=%async_computation.1 | async-start | bytes 4456448 | tf_op jit(solution)/shard_map/all_to_all | solution.py:406
  23.2 15.1 %collective-permute-start = (bf16[16,128,128]{2,1,0:T(8,128)(2,1)}, bf16[16,128,128]{2,1,0:T(8,128)(2,1)S(1)}, u32[]{:S(2)}, u32[]{:S(2)}) collective-permute-start(bf16[16,128,128]{2,1,0:T(8,128)(2,1)} %get-tuple-element.50), channel_id=1, source_target_pairs={{0,32},{4,36},{8,40},{12,44},{16,48},{20,52},{24,56},{28,60},{32,0... | collective-permute-start | bytes 1572872 | tf_op jit(solution)/shard_map/ppermute | solution.py:457
  23.7 23.5 %collective-permute-start.1 = (bf16[16,128,128]{2,1,0:T(8,128)(2,1)}, bf16[16,128,128]{2,1,0:T(8,128)(2,1)S(1)}, u32[]{:S(2)}, u32[]{:S(2)}) collective-permute-start(bf16[16,128,128]{2,1,0:T(8,128)(2,1)} %get-tuple-element.51), channel_id=1, source_target_pairs={{0,64},{4,68},{8,72},{12,76},{16,80},{20,84},{24,88},{28,92},{32,9... | collective-permute-start | bytes 1572872 | tf_op jit(solution)/shard_map/ppermute | solution.py:457
  25.8 23.9 %collective-permute-start.2 = (bf16[16,128,128]{2,1,0:T(8,128)(2,1)S(1)}, bf16[16,128,128]{2,1,0:T(8,128)(2,1)}, u32[]{:S(2)}, u32[]{:S(2)}) collective-permute-start(bf16[16,128,128]{2,1,0:T(8,128)(2,1)S(1)} %copy-done.4), channel_id=1, source_target_pairs={{0,96},{4,100},{8,104},{12,108},{16,112},{20,116},{24,120},{28,124... | collective-permute-start | bytes 1572872 | tf_op jit(solution)/shard_map/ppermute | solution.py:457
  38.2 17.3 %copy-start.2 = (bf16[16,128,128]{2,1,0:T(8,128)(2,1)}, bf16[16,128,128]{2,1,0:T(8,128)(2,1)S(1)}, u32[]{:S(2)}) copy-start(bf16[16,128,128]{2,1,0:T(8,128)(2,1)S(1)} %collective-permute-done.refs_2_) | copy-start | bytes 1572868
  47.2 0.8 copy-start.3
  53.6 1.9 %copy-start = (bf16[8,4,272,128]{3,2,1,0:T(8,128)(2,1)}, bf16[8,4,272,128]{3,2,1,0:T(8,128)(2,1)S(1)}, u32[]{:S(2)}) copy-start(bf16[8,4,272,128]{3,2,1,0:T(8,128)(2,1)S(1)} %all-to-all-done.1.refs_0_) | copy-start | bytes 6684676
  53.6 23.5 %collective-permute-start.3 = (bf16[1024,128]{1,0:T(8,128)(2,1)}, bf16[1024,128]{1,0:T(8,128)(2,1)S(1)}, u32[]{:S(2)}, u32[]{:S(2)}) collective-permute-start(bf16[1024,128]{1,0:T(8,128)(2,1)} %get-tuple-element.68), channel_id=1, source_target_pairs={{0,1},{1,0},{2,3},{3,2},{4,5},{5,4},{6,7},{7,6},{8,9},{9,8},{10,11... | collective-permute-start | bytes 786440 | tf_op jit(solution)/shard_map/ppermute | solution.py:462
  53.6 23.5 %collective-permute-start.4 = (bf16[1024,128]{1,0:T(8,128)(2,1)}, bf16[1024,128]{1,0:T(8,128)(2,1)}, u32[]{:S(2)}, u32[]{:S(2)}) collective-permute-start(bf16[1024,128]{1,0:T(8,128)(2,1)} %get-tuple-element.69), channel_id=1, source_target_pairs={{0,2},{1,3},{2,0},{3,1},{4,6},{5,7},{6,4},{7,5},{8,10},{9,11},{10,... | collective-permute-start | bytes 786440 | tf_op jit(solution)/shard_map/ppermute | solution.py:462
  54.7 22.5 %collective-permute-start.5 = (bf16[1024,128]{1,0:T(8,128)(2,1)}, bf16[1024,128]{1,0:T(8,128)(2,1)}, u32[]{:S(2)}, u32[]{:S(2)}) collective-permute-start(bf16[1024,128]{1,0:T(8,128)(2,1)} %get-tuple-element.70), channel_id=1, source_target_pairs={{0,3},{1,2},{2,1},{3,0},{4,7},{5,6},{6,5},{7,4},{8,11},{9,10},{10,... | collective-permute-start | bytes 786440 | tf_op jit(solution)/shard_map/ppermute | solution.py:462
  77.1 10.7 %copy-start.7 = (bf16[8,128,128]{2,1,0:T(8,128)(2,1)S(1)}, bf16[8,128,128]{2,1,0:T(8,128)(2,1)}, u32[]{:S(2)}) copy-start(bf16[8,128,128]{2,1,0:T(8,128)(2,1)} %get-tuple-element.73) | copy-start | bytes 786436
  77.1 10.8 %copy-start.6 = (bf16[8,128,128]{2,1,0:T(8,128)(2,1)S(1)}, bf16[8,128,128]{2,1,0:T(8,128)(2,1)}, u32[]{:S(2)}) copy-start(bf16[8,128,128]{2,1,0:T(8,128)(2,1)} %get-tuple-element.74) | copy-start | bytes 786436
  77.1 14.3 %copy-start.5 = (bf16[8,128,128]{2,1,0:T(8,128)(2,1)S(1)}, bf16[8,128,128]{2,1,0:T(8,128)(2,1)}, u32[]{:S(2)}) copy-start(bf16[8,128,128]{2,1,0:T(8,128)(2,1)} %get-tuple-element.75) | copy-start | bytes 786436
  77.1 44.0 %copy-start.1 = (bf16[1024,128]{1,0:T(8,128)(2,1)}, bf16[1024,128]{1,0:T(8,128)(2,1)S(1)}, u32[]{:S(2)}) copy-start(bf16[1024,128]{1,0:T(8,128)(2,1)S(1)} %collective-permute-done.3.refs_1_) | copy-start | bytes 786436
  77.2 41.6 %all-to-all-start.2 = ((bf16[8,4,256,128]{3,2,1,0:T(8,128)(2,1)}), bf16[8,4,256,128]{3,2,1,0:T(8,128)(2,1)}, u32[]{:S(2)}, u32[]{:S(2)}) async-start(bf16[8,4,256,128]{3,2,1,0:T(8,128)(2,1)} %get-tuple-element.71), calls=%async_computation.2 | async-start | bytes 4194304 | tf_op jit(solution)/shard_map/all_to_all | solution.py:406
  87.8 7.8 %collective-permute-start.6 = (bf16[8,128,128]{2,1,0:T(8,128)(2,1)S(1)}, bf16[8,128,128]{2,1,0:T(8,128)(2,1)}, u32[]{:S(2)}, u32[]{:S(2)}) collective-permute-start(bf16[8,128,128]{2,1,0:T(8,128)(2,1)S(1)} %copy-done.7), channel_id=1, source_target_pairs={{0,32},{4,36},{8,40},{12,44},{16,48},{20,52},{24,56},{28,60},{32,0... | collective-permute-start | bytes 786440 | tf_op jit(solution)/shard_map/ppermute | solution.py:466
  87.9 16.0 %collective-permute-start.7 = (bf16[8,128,128]{2,1,0:T(8,128)(2,1)S(1)}, bf16[8,128,128]{2,1,0:T(8,128)(2,1)}, u32[]{:S(2)}, u32[]{:S(2)}) collective-permute-start(bf16[8,128,128]{2,1,0:T(8,128)(2,1)S(1)} %copy-done.6), channel_id=1, source_target_pairs={{0,64},{4,68},{8,72},{12,76},{16,80},{20,84},{24,88},{28,92},{32,9... | collective-permute-start | bytes 786440 | tf_op jit(solution)/shard_map/ppermute | solution.py:466
  91.4 16.1 %collective-permute-start.8 = (bf16[8,128,128]{2,1,0:T(8,128)(2,1)S(1)}, bf16[8,128,128]{2,1,0:T(8,128)(2,1)}, u32[]{:S(2)}, u32[]{:S(2)}) collective-permute-start(bf16[8,128,128]{2,1,0:T(8,128)(2,1)S(1)} %copy-done.5), channel_id=1, source_target_pairs={{0,96},{4,100},{8,104},{12,108},{16,112},{20,116},{24,120},{28,124... | collective-permute-start | bytes 786440 | tf_op jit(solution)/shard_map/ppermute | solution.py:466
  144.4 25.3 %all-to-all-start.4 = ((bf16[32,32,512]{2,1,0:T(8,128)(2,1)}), bf16[32,32,512]{2,1,0:T(8,128)(2,1)}, u32[]{:S(2)}, u32[]{:S(2)}) async-start(bf16[32,32,512]{2,1,0:T(8,128)(2,1)} %weight.1), calls=%async_computation.4 | async-start | bytes 2097152 | tf_op jit(solution)/shard_map/all_to_all | solution.py:406

commit v9 on v8

--- a/solution.py
+++ b/solution.py
@@ -178,7 +178,7 @@
         final(j).wait()
 
 
-def local(body, out_shape, inputs, scratch, name):
+def local(body, out_shape, inputs, scratch, name, limit=VMEM_LIMIT):
     spec = pl.BlockSpec(memory_space=pltpu.HBM)
     many = isinstance(out_shape, tuple)
     return pl.pallas_call(
@@ -187,7 +187,7 @@
         in_specs=[spec] * len(inputs),
         out_specs=(spec,) * len(out_shape) if many else spec,
         scratch_shapes=scratch,
-        compiler_params=pltpu.CompilerParams(vmem_limit_bytes=VMEM_LIMIT),
+        compiler_params=pltpu.CompilerParams(vmem_limit_bytes=limit),
         name=name,
     )(*inputs)
 
@@ -381,25 +381,11 @@
     copy.wait()
 
 
-def total_kernel(part_hbm, out_hbm, part_ref, out_ref, sems):
-    seq = part_ref.shape[0]
-    pieces = sems.shape[0] - 1
-    some = seq // pieces
-    arrivals = []
-    for j in range(pieces):
-        at = pl.ds(j * some, some)
-        arrivals.append(pltpu.make_async_copy(part_hbm.at[at], part_ref.at[at], sems.at[j]))
-    for copy in arrivals:
-        copy.start()
-    total = jnp.zeros(out_ref.shape, jnp.float32)
-    for j in range(pieces):
-        arrivals[j].wait()
-        for s in range(j * some, (j + 1) * some):
-            total += part_ref[s].astype(jnp.float32)
+def total_kernel(part_ref, out_ref):
+    total = part_ref[0].astype(jnp.float32)
+    for s in range(1, part_ref.shape[0]):
+        total += part_ref[s].astype(jnp.float32)
     out_ref[...] = total
-    copy = pltpu.make_async_copy(out_ref, out_hbm, sems.at[pieces])
-    copy.start()
-    copy.wait()
 
 
 def exchange(array, axis, groups=None):
@@ -510,18 +496,16 @@
             pltpu.SemaphoreType.DMA((lines + 1,)),
         ],
         "unpack",
-    )
-    weight_grad = local(
+        SMALL_LIMIT,
+    )
+    weight_grad = pl.pallas_call(
         total_kernel,
-        shape(result[1:], jnp.float32),
-        [partial],
-        [
-            pltpu.VMEM(result, half),
-            pltpu.VMEM(result[1:], jnp.float32),
-            pltpu.SemaphoreType.DMA((5,)),
-        ],
-        "total",
-    )
+        out_shape=shape(result[1:], jnp.float32),
+        in_specs=[pl.BlockSpec(memory_space=pltpu.VMEM)],
+        out_specs=pl.BlockSpec(memory_space=pltpu.VMEM),
+        compiler_params=pltpu.CompilerParams(vmem_limit_bytes=SMALL_LIMIT),
+        name="total",
+    )(partial)
     return (query_grad[None], keyval_grad[None], weight_grad)
 
 

time: 174 us -> 172 us (0.989); the launches traced: 172 us -> 172 us
  Pallas kernels: 37.7 us -> 43.5 us
  starting transfers between devices: 40 us -> 34.5 us
  waiting for transfers between devices: 71.8 us -> 69.9 us
    pallas_call x1, Pallas kernels: 21.6 us -> 29.3 us  [attention(): pl.pallas_call(attention_kernel, out_shape=(shape((planes, lines, 256, DH...]
    all_to_all x4, starting transfers between devices: 28.7 us -> 23.1 us  [exchange(): lax.all_to_all(array, axis, split_axis=0, concat_axis=0, axis_index_group...]
    ppermute x3, waiting for transfers between devices: 14.9 us -> 10.7 us  [shards(): dq[k] = lax.ppermute(dq[k], 'seq', partners(k))]
    pallas_call x6 -> x5, Pallas kernels: 15.4 us -> 12.7 us  [local(): pl.pallas_call(body, out_shape=out_shape, in_specs=[spec] * len(inputs),...]
  transfers between devices with their start and end apart: 13 -> 13, of which waited for: 10 -> 10; matrix products, arithmetic and copies ran while one was open for 0% -> 0% of each run, Pallas kernels for 16% -> 20%
where the time goes in v9:
time: 172 us
  waiting for transfers between devices  69.9 us (41%)
  Pallas kernels  43.5 us (25%)
  starting transfers between devices  34.5 us (20%)
  blocking collectives  19.5 us (11%)
  local copies, waits for them, and re-layouts  3.82 us (2%)
    all_to_all x4, waiting for transfers between devices, exchange(): lax.all_to_all(array, axis, split_axis=0, concat_axis=0, axis_index_group...  37.2 us
    pallas_call x1, Pallas kernels, attention(): pl.pallas_call(attention_kernel, out_shape=(shape((planes, lines, 256, DH...  29.3 us
    all_to_all x4, starting transfers between devices, exchange(): lax.all_to_all(array, axis, split_axis=0, concat_axis=0, axis_index_group...  23.1 us
    ppermute x3, waiting for transfers between devices, shards(): parts[k] = lax.ppermute(parts[k], 'seq', partners(k))  22 us
    pallas_call x5, Pallas kernels, local(): pl.pallas_call(body, out_shape=out_shape, in_specs=[spec] * len(inputs),...  12.7 us
    all_to_all x1, blocking collectives, exchange(): lax.all_to_all(array, axis, split_axis=0, concat_axis=0, axis_index_group...  11.8 us
    ppermute x3, waiting for transfers between devices, shards(): dq[k] = lax.ppermute(dq[k], 'seq', partners(k))  10.7 us
    all_gather x1, blocking collectives, shards(): every = lax.all_gather(keyval_grad, 'dp', axis=0)  7.7 us
  transfers between devices with their start and end apart: 13, of which 10 were waited for; matrix products, arithmetic and copies ran while one was open for 0% of the time, Pallas kernels for 20%

profile of v9, /device:TPU:0, one launch (start us, length us, event | category | flops | bytes accessed | tf_op | source)
XLA Modules:
  0.0 172.0 jit_solution(11383652762176578914)
XLA Ops:
  2.3 4.4 %all-to-all-start = ((bf16[4,272,128]{2,1,0:T(8,128)(2,1)}), bf16[4,272,128]{2,1,0:T(8,128)(2,1)S(1)}, u32[]{:S(2)}, u32[]{:S(2)}) async-start(bf16[4,272,128]{2,1,0:T(8,128)(2,1)} %share.1), calls=%async_computation | async-start | bytes 557056 | tf_op jit(solution)/shard_map/all_to_all | solution.py:392
  6.7 3.5 %pack.1 = (bf16[16,128,128]{2,1,0:T(8,128)(2,1)}, bf16[16,128,128]{2,1,0:T(8,128)(2,1)}, bf16[16,128,128]{2,1,0:T(8,128)(2,1)}, bf16[16,128,128]{2,1,0:T(8,128)(...) custom-call(bf16[128,4096]{1,0:T(8,128)(2,1)} %bitcast.8, ...), custom_call_target="tpu_custom_call" | custom-call | tf_op jit(solution)/shard_map/pack/pallas_call | solution.py:184
  10.2 3.3 %all-to-all-done = bf16[4,272,128]{2,1,0:T(8,128)(2,1)S(1)} async-done(((bf16[4,272,128]{2,1,0:T(8,128)(2,1)}), bf16[4,272,128]{2,1,0:T(8,128)(2,1)S(1)}, u32[]{:S(2)}, u32[]{:S(2)}) %all-to-all-start) | async-done | bytes 278560 | tf_op jit(solution)/shard_map/all_to_all | solution.py:392
  15.2 7.9 %all-to-all-start.1 = ((bf16[8,4,272,128]{3,2,1,0:T(8,128)(2,1)}), bf16[8,4,272,128]{3,2,1,0:T(8,128)(2,1)S(1)}, u32[]{:S(2)}, u32[]{:S(2)}) async-start(bf16[8,4,272,128]{3,2,1,0:T(8,128)(2,1)} %broadcast_in_dim.12), calls=%async_computation.1 | async-start | bytes 4456448 | tf_op jit(solution)/shard_map/all_to_all | solution.py:392
  23.7 2.1 %collective-permute-start.1 = (bf16[16,128,128]{2,1,0:T(8,128)(2,1)}, bf16[16,128,128]{2,1,0:T(8,128)(2,1)S(1)}, u32[]{:S(2)}, u32[]{:S(2)}) collective-permute-start(bf16[16,128,128]{2,1,0:T(8,128)(2,1)} %get-tuple-element.51), channel_id=1, source_target_pairs={{0,64},{4,68},{8,72},{12,76},{16,80},{20,84},{24,88},{28,92},{32,9... | collective-permute-start | bytes 1572872 | tf_op jit(solution)/shard_map/ppermute | solution.py:443
  25.8 2.1 %collective-permute-start.2 = (bf16[16,128,128]{2,1,0:T(8,128)(2,1)}, bf16[16,128,128]{2,1,0:T(8,128)(2,1)}, u32[]{:S(2)}, u32[]{:S(2)}) collective-permute-start(bf16[16,128,128]{2,1,0:T(8,128)(2,1)} %get-tuple-element.52), channel_id=1, source_target_pairs={{0,96},{4,100},{8,104},{12,108},{16,112},{20,116},{24,120},{28,124... | collective-permute-start | bytes 1572872 | tf_op jit(solution)/shard_map/ppermute | solution.py:443
  27.8 10.4 %collective-permute-done.refs_2_ = bf16[16,128,128]{2,1,0:T(8,128)(2,1)S(1)} collective-permute-done((bf16[16,128,128]{2,1,0:T(8,128)(2,1)}, bf16[16,128,128]{2,1,0:T(8,128)(2,1)S(1)}, u32[]{:S(2)}, u32[]{:S(2)}) %collective-permute-start) | collective-permute-done | bytes 524320 | tf_op jit(solution)/shard_map/ppermute | solution.py:443
  38.2 9.0 %collective-permute-done.1.refs_3_ = bf16[16,128,128]{2,1,0:T(8,128)(2,1)S(1)} collective-permute-done((bf16[16,128,128]{2,1,0:T(8,128)(2,1)}, bf16[16,128,128]{2,1,0:T(8,128)(2,1)S(1)}, u32[]{:S(2)}, u32[]{:S(2)}) %collective-permute-start.1) | collective-permute-done | bytes 524320 | tf_op jit(solution)/shard_map/ppermute | solution.py:443
  47.2 2.7 %collective-permute-done.2.refs_4_ = bf16[16,128,128]{2,1,0:T(8,128)(2,1)} collective-permute-done((bf16[16,128,128]{2,1,0:T(8,128)(2,1)}, bf16[16,128,128]{2,1,0:T(8,128)(2,1)}, u32[]{:S(2)}, u32[]{:S(2)}) %collective-permute-start.2) | collective-permute-done | bytes 524320 | tf_op jit(solution)/shard_map/ppermute | solution.py:443
  49.9 3.8 %all-to-all-done.1.refs_0_ = bf16[8,4,272,128]{3,2,1,0:T(8,128)(2,1)S(1)} async-done(((bf16[8,4,272,128]{3,2,1,0:T(8,128)(2,1)}), bf16[8,4,272,128]{3,2,1,0:T(8,128)(2,1)S(1)}, u32[]{:S(2)}, u32[]{:S(2)}) %all-to-all-start.1) | async-done | bytes 2228256 | tf_op jit(solution)/shard_map/all_to_all | solution.py:392
  55.5 29.3 %attention.1 = (bf16[8,4,256,128]{3,2,1,0:T(8,128)(2,1)}, bf16[8,128,128]{2,1,0:T(8,128)(2,1)}, bf16[8,128,128]{2,1,0:T(8,128)(2,1)}, bf16[8,128,128]{2,1,0:T(8,128)(2,1)}, bf16[8,128,128]{2,1,0:T(8,128)(2,1)}) custom-call(bf16[8,4,272,128]{3,2,1,0:T(8,128)(2,1)} %copy-done.7, bf16[16,128,128]{2,1,0:T(8,128)(2,1)} %get-tuple-element.58.refs_1_, ...), custom_call_target="tpu_custom_call" | custom-call | flops 10000000000 | bytes 8000000 | tf_op jit(solution)/shard_map/attention/pallas_call | solution.py:203
  84.9 5.4 %all-to-all-start.2 = ((bf16[8,4,256,128]{3,2,1,0:T(8,128)(2,1)}), bf16[8,4,256,128]{3,2,1,0:T(8,128)(2,1)}, u32[]{:S(2)}, u32[]{:S(2)}) async-start(bf16[8,4,256,128]{3,2,1,0:T(8,128)(2,1)} %get-tuple-element.71), calls=%async_computation.2 | async-start | bytes 4194304 | tf_op jit(solution)/shard_map/all_to_all | solution.py:392
  91.0 2.0 %collective-permute-start.7 = (bf16[8,128,128]{2,1,0:T(8,128)(2,1)S(1)}, bf16[8,128,128]{2,1,0:T(8,128)(2,1)S(1)}, u32[]{:S(2)}, u32[]{:S(2)}) collective-permute-start(bf16[8,128,128]{2,1,0:T(8,128)(2,1)S(1)} %copy-done.12), channel_id=1, source_target_pairs={{0,64},{4,68},{8,72},{12,76},{16,80},{20,84},{24,88},{28,92},{32,9... | collective-permute-start | bytes 786440 | tf_op jit(solution)/shard_map/ppermute | solution.py:452
  92.9 2.1 %collective-permute-start.8 = (bf16[8,128,128]{2,1,0:T(8,128)(2,1)S(1)}, bf16[8,128,128]{2,1,0:T(8,128)(2,1)S(1)}, u32[]{:S(2)}, u32[]{:S(2)}) collective-permute-start(bf16[8,128,128]{2,1,0:T(8,128)(2,1)S(1)} %copy-done.11), channel_id=1, source_target_pairs={{0,96},{4,100},{8,104},{12,108},{16,112},{20,116},{24,120},{28,124... | collective-permute-start | bytes 786440 | tf_op jit(solution)/shard_map/ppermute | solution.py:452
  95.0 1.7 collective-permute-done.6.refs_1_
  97.4 4.6 %collective-permute-done.7.refs_2_ = bf16[8,128,128]{2,1,0:T(8,128)(2,1)S(1)} collective-permute-done((bf16[8,128,128]{2,1,0:T(8,128)(2,1)S(1)}, bf16[8,128,128]{2,1,0:T(8,128)(2,1)S(1)}, u32[]{:S(2)}, u32[]{:S(2)}) %collective-permute-start.7) | collective-permute-done | bytes 262176 | tf_op jit(solution)/shard_map/ppermute | solution.py:452
  102.7 4.4 %collective-permute-done.8.refs_3_ = bf16[8,128,128]{2,1,0:T(8,128)(2,1)S(1)} collective-permute-done((bf16[8,128,128]{2,1,0:T(8,128)(2,1)S(1)}, bf16[8,128,128]{2,1,0:T(8,128)(2,1)S(1)}, u32[]{:S(2)}, u32[]{:S(2)}) %collective-permute-start.8) | collective-permute-done | bytes 262176 | tf_op jit(solution)/shard_map/ppermute | solution.py:452
  107.8 12.0 %all-to-all-done.2.part_hbm = bf16[8,4,256,128]{3,2,1,0:T(8,128)(2,1)} async-done(((bf16[8,4,256,128]{3,2,1,0:T(8,128)(2,1)}), bf16[8,4,256,128]{3,2,1,0:T(8,128)(2,1)}, u32[]{:S(2)}, u32[]{:S(2)}) %all-to-all-start.2) | async-done | bytes 2097184 | tf_op jit(solution)/shard_map/all_to_all | solution.py:392
  119.9 2.3 %gather.1 = bf16[4,256,128]{2,1,0:T(8,128)(2,1)} custom-call(bf16[8,4,256,128]{3,2,1,0:T(8,128)(2,1)} %all-to-all-done.2.part_hbm), custom_call_target="tpu_custom_call" | custom-call | tf_op jit(solution)/shard_map/gather/pallas_call | solution.py:184
  122.2 11.8 %all_to_all.25.part_ref = bf16[4,256,128]{2,1,0:T(8,128)(2,1)S(1)} all-to-all(bf16[4,256,128]{2,1,0:T(8,128)(2,1)} %gather.1), channel_id=1, replica_groups={{0,32,64,96},{4,36,68,100},{8,40,72,104},{12,44,76,108},{16,48,80,112},..., dimensions={0} | all-to-all | bytes 524288 | tf_op jit(solution)/shard_map/all_to_all | solution.py:392
  134.6 7.7 %all-gather = bf16[512,512]{1,0:T(8,128)(2,1)} all-gather(bf16[128,512]{1,0:T(8,128)(2,1)} %combine.1), channel_id=2, replica_groups=mesh['seq'=32,'dp'=4] {'dp'}, dimensions={0}, use_global_device_ids=true | all-gather | bytes 655360 | tf_op jit(solution)/shard_map/all_gather | solution.py:474
  142.3 3.9 %weight.1 = bf16[32,32,512]{2,1,0:T(8,128)(2,1)} custom-call(bf16[1024,128]{1,0:T(8,128)(2,1)} %get-tuple-element.81.refs_0_, bf16[1024,128]{1,0:T(8,128)(2,1)} %collective-permute-done.3.refs_1_, bf16[1024,128]{1,0:T(8,128)(2,1)} %collective-permute-done.4.refs_2_, bf16[1024,128]{1,0:T(8,128)(2,1)} %collective-permute-done.5.refs_3_, ...), custom_call_target="tpu_custom_call" | custom-call | tf_op jit(solution)/shard_map/weight/pallas_call | solution.py:184
  146.2 5.4 %all-to-all-start.4 = ((bf16[32,32,512]{2,1,0:T(8,128)(2,1)}), bf16[32,32,512]{2,1,0:T(8,128)(2,1)S(1)}, u32[]{:S(2)}, u32[]{:S(2)}) async-start(bf16[32,32,512]{2,1,0:T(8,128)(2,1)} %weight.1), calls=%async_computation.4 | async-start | bytes 2097152 | tf_op jit(solution)/shard_map/all_to_all | solution.py:392
  153.1 18.1 %all-to-all-done.4.part_ref = bf16[32,32,512]{2,1,0:T(8,128)(2,1)S(1)} async-done(((bf16[32,32,512]{2,1,0:T(8,128)(2,1)}), bf16[32,32,512]{2,1,0:T(8,128)(2,1)S(1)}, u32[]{:S(2)}, u32[]{:S(2)}) %all-to-all-start.4) | async-done | bytes 1048608 | tf_op jit(solution)/shard_map/all_to_all | solution.py:392
  (41 shorter events, 11.5 us)
Async XLA Ops:
  2.3 11.2 %all-to-all-start = ((bf16[4,272,128]{2,1,0:T(8,128)(2,1)}), bf16[4,272,128]{2,1,0:T(8,128)(2,1)S(1)}, u32[]{:S(2)}, u32[]{:S(2)}) async-start(bf16[4,272,128]{2,1,0:T(8,128)(2,1)} %share.1), calls=%async_computation | async-start | bytes 557056 | tf_op jit(solution)/shard_map/all_to_all | solution.py:392
  15.2 39.4 %copy-start.10 = (bf16[1024,128]{1,0:T(8,128)(2,1)S(1)}, bf16[1024,128]{1,0:T(8,128)(2,1)}, u32[]{:S(2)}) copy-start(bf16[1024,128]{1,0:T(8,128)(2,1)} %get-tuple-element.70) | copy-start | bytes 786436
  15.2 38.4 %all-to-all-start.1 = ((bf16[8,4,272,128]{3,2,1,0:T(8,128)(2,1)}), bf16[8,4,272,128]{3,2,1,0:T(8,128)(2,1)S(1)}, u32[]{:S(2)}, u32[]{:S(2)}) async-start(bf16[8,4,272,128]{3,2,1,0:T(8,128)(2,1)} %broadcast_in_dim.12), calls=%async_computation.1 | async-start | bytes 4456448 | tf_op jit(solution)/shard_map/all_to_all | solution.py:392
  23.1 15.1 %collective-permute-start = (bf16[16,128,128]{2,1,0:T(8,128)(2,1)}, bf16[16,128,128]{2,1,0:T(8,128)(2,1)S(1)}, u32[]{:S(2)}, u32[]{:S(2)}) collective-permute-start(bf16[16,128,128]{2,1,0:T(8,128)(2,1)} %get-tuple-element.50), channel_id=1, source_target_pairs={{0,32},{4,36},{8,40},{12,44},{16,48},{20,52},{24,56},{28,60},{32,0... | collective-permute-start | bytes 1572872 | tf_op jit(solution)/shard_map/ppermute | solution.py:443
  23.7 23.5 %collective-permute-start.1 = (bf16[16,128,128]{2,1,0:T(8,128)(2,1)}, bf16[16,128,128]{2,1,0:T(8,128)(2,1)S(1)}, u32[]{:S(2)}, u32[]{:S(2)}) collective-permute-start(bf16[16,128,128]{2,1,0:T(8,128)(2,1)} %get-tuple-element.51), channel_id=1, source_target_pairs={{0,64},{4,68},{8,72},{12,76},{16,80},{20,84},{24,88},{28,92},{32,9... | collective-permute-start | bytes 1572872 | tf_op jit(solution)/shard_map/ppermute | solution.py:443
  25.8 24.1 %collective-permute-start.2 = (bf16[16,128,128]{2,1,0:T(8,128)(2,1)}, bf16[16,128,128]{2,1,0:T(8,128)(2,1)}, u32[]{:S(2)}, u32[]{:S(2)}) collective-permute-start(bf16[16,128,128]{2,1,0:T(8,128)(2,1)} %get-tuple-element.52), channel_id=1, source_target_pairs={{0,96},{4,100},{8,104},{12,108},{16,112},{20,116},{24,120},{28,124... | collective-permute-start | bytes 1572872 | tf_op jit(solution)/shard_map/ppermute | solution.py:443
  38.2 17.3 %copy-start.8 = (bf16[16,128,128]{2,1,0:T(8,128)(2,1)}, bf16[16,128,128]{2,1,0:T(8,128)(2,1)S(1)}, u32[]{:S(2)}) copy-start(bf16[16,128,128]{2,1,0:T(8,128)(2,1)S(1)} %collective-permute-done.refs_2_) | copy-start | bytes 1572868
  47.2 8.3 %copy-start.9 = (bf16[16,128,128]{2,1,0:T(8,128)(2,1)}, bf16[16,128,128]{2,1,0:T(8,128)(2,1)S(1)}, u32[]{:S(2)}) copy-start(bf16[16,128,128]{2,1,0:T(8,128)(2,1)S(1)} %collective-permute-done.1.refs_3_) | copy-start | bytes 1572868
  53.6 1.9 %copy-start.7 = (bf16[8,4,272,128]{3,2,1,0:T(8,128)(2,1)}, bf16[8,4,272,128]{3,2,1,0:T(8,128)(2,1)S(1)}, u32[]{:S(2)}) copy-start(bf16[8,4,272,128]{3,2,1,0:T(8,128)(2,1)S(1)} %all-to-all-done.1.refs_0_) | copy-start | bytes 6684676
  53.6 31.2 %collective-permute-start.3 = (bf16[1024,128]{1,0:T(8,128)(2,1)}, bf16[1024,128]{1,0:T(8,128)(2,1)}, u32[]{:S(2)}, u32[]{:S(2)}) collective-permute-start(bf16[1024,128]{1,0:T(8,128)(2,1)} %get-tuple-element.68), channel_id=1, source_target_pairs={{0,1},{1,0},{2,3},{3,2},{4,5},{5,4},{6,7},{7,6},{8,9},{9,8},{10,11... | collective-permute-start | bytes 786440 | tf_op jit(solution)/shard_map/ppermute | solution.py:448
  53.6 31.2 %collective-permute-start.4 = (bf16[1024,128]{1,0:T(8,128)(2,1)}, bf16[1024,128]{1,0:T(8,128)(2,1)}, u32[]{:S(2)}, u32[]{:S(2)}) collective-permute-start(bf16[1024,128]{1,0:T(8,128)(2,1)} %get-tuple-element.69), channel_id=1, source_target_pairs={{0,2},{1,3},{2,0},{3,1},{4,6},{5,7},{6,4},{7,5},{8,10},{9,11},{10,... | collective-permute-start | bytes 786440 | tf_op jit(solution)/shard_map/ppermute | solution.py:448
  54.7 30.2 %collective-permute-start.5 = (bf16[1024,128]{1,0:T(8,128)(2,1)S(1)}, bf16[1024,128]{1,0:T(8,128)(2,1)}, u32[]{:S(2)}, u32[]{:S(2)}) collective-permute-start(bf16[1024,128]{1,0:T(8,128)(2,1)S(1)} %copy-done.10), channel_id=1, source_target_pairs={{0,3},{1,2},{2,1},{3,0},{4,7},{5,6},{6,5},{7,4},{8,11},{9,10},{10,... | collective-permute-start | bytes 786440 | tf_op jit(solution)/shard_map/ppermute | solution.py:448
  84.8 5.5 %copy-start.13 = (bf16[8,128,128]{2,1,0:T(8,128)(2,1)S(1)}, bf16[8,128,128]{2,1,0:T(8,128)(2,1)}, u32[]{:S(2)}) copy-start(bf16[8,128,128]{2,1,0:T(8,128)(2,1)} %get-tuple-element.73) | copy-start | bytes 786436
  84.8 6.2 %copy-start.12 = (bf16[8,128,128]{2,1,0:T(8,128)(2,1)S(1)}, bf16[8,128,128]{2,1,0:T(8,128)(2,1)}, u32[]{:S(2)}) copy-start(bf16[8,128,128]{2,1,0:T(8,128)(2,1)} %get-tuple-element.74) | copy-start | bytes 786436
  84.8 8.1 %copy-start.11 = (bf16[8,128,128]{2,1,0:T(8,128)(2,1)S(1)}, bf16[8,128,128]{2,1,0:T(8,128)(2,1)}, u32[]{:S(2)}) copy-start(bf16[8,128,128]{2,1,0:T(8,128)(2,1)} %get-tuple-element.75) | copy-start | bytes 786436
  84.9 35.0 %all-to-all-start.2 = ((bf16[8,4,256,128]{3,2,1,0:T(8,128)(2,1)}), bf16[8,4,256,128]{3,2,1,0:T(8,128)(2,1)}, u32[]{:S(2)}, u32[]{:S(2)}) async-start(bf16[8,4,256,128]{3,2,1,0:T(8,128)(2,1)} %get-tuple-element.71), calls=%async_computation.2 | async-start | bytes 4194304 | tf_op jit(solution)/shard_map/all_to_all | solution.py:392
  90.3 6.5 %collective-permute-start.6 = (bf16[8,128,128]{2,1,0:T(8,128)(2,1)S(1)}, bf16[8,128,128]{2,1,0:T(8,128)(2,1)S(1)}, u32[]{:S(2)}, u32[]{:S(2)}) collective-permute-start(bf16[8,128,128]{2,1,0:T(8,128)(2,1)S(1)} %copy-done.13), channel_id=1, source_target_pairs={{0,32},{4,36},{8,40},{12,44},{16,48},{20,52},{24,56},{28,60},{32,0... | collective-permute-start | bytes 786440 | tf_op jit(solution)/shard_map/ppermute | solution.py:452
  91.0 11.0 %collective-permute-start.7 = (bf16[8,128,128]{2,1,0:T(8,128)(2,1)S(1)}, bf16[8,128,128]{2,1,0:T(8,128)(2,1)S(1)}, u32[]{:S(2)}, u32[]{:S(2)}) collective-permute-start(bf16[8,128,128]{2,1,0:T(8,128)(2,1)S(1)} %copy-done.12), channel_id=1, source_target_pairs={{0,64},{4,68},{8,72},{12,76},{16,80},{20,84},{24,88},{28,92},{32,9... | collective-permute-start | bytes 786440 | tf_op jit(solution)/shard_map/ppermute | solution.py:452
  92.9 14.2 %collective-permute-start.8 = (bf16[8,128,128]{2,1,0:T(8,128)(2,1)S(1)}, bf16[8,128,128]{2,1,0:T(8,128)(2,1)S(1)}, u32[]{:S(2)}, u32[]{:S(2)}) collective-permute-start(bf16[8,128,128]{2,1,0:T(8,128)(2,1)S(1)} %copy-done.11), channel_id=1, source_target_pairs={{0,96},{4,100},{8,104},{12,108},{16,112},{20,116},{24,120},{28,124... | collective-permute-start | bytes 786440 | tf_op jit(solution)/shard_map/ppermute | solution.py:452
  142.3 9.4 %copy-start = (bf16[8,128,128]{2,1,0:T(8,128)(2,1)S(1)}, bf16[8,128,128]{2,1,0:T(8,128)(2,1)}, u32[]{:S(2)}) copy-start(bf16[8,128,128]{2,1,0:T(8,128)(2,1)} %get-tuple-element.76.refs_0_) | copy-start | bytes 786436
  146.2 5.5 %copy-start.2 = (bf16[8,128,128]{2,1,0:T(8,128)(2,1)S(1)}, bf16[8,128,128]{2,1,0:T(8,128)(2,1)}, u32[]{:S(2)}) copy-start(bf16[8,128,128]{2,1,0:T(8,128)(2,1)} %copy-done.1) | copy-start | bytes 786436
  146.2 5.5 %copy-start.4 = (bf16[8,128,128]{2,1,0:T(8,128)(2,1)S(1)}, bf16[8,128,128]{2,1,0:T(8,128)(2,1)}, u32[]{:S(2)}) copy-start(bf16[8,128,128]{2,1,0:T(8,128)(2,1)} %copy-done.3) | copy-start | bytes 786436
  146.2 5.5 %copy-start.6 = (bf16[8,128,128]{2,1,0:T(8,128)(2,1)S(1)}, bf16[8,128,128]{2,1,0:T(8,128)(2,1)}, u32[]{:S(2)}) copy-start(bf16[8,128,128]{2,1,0:T(8,128)(2,1)} %copy-done.5) | copy-start | bytes 786436
  146.2 24.9 %all-to-all-start.4 = ((bf16[32,32,512]{2,1,0:T(8,128)(2,1)}), bf16[32,32,512]{2,1,0:T(8,128)(2,1)S(1)}, u32[]{:S(2)}, u32[]{:S(2)}) async-start(bf16[32,32,512]{2,1,0:T(8,128)(2,1)} %weight.1), calls=%async_computation.4 | async-start | bytes 2097152 | tf_op jit(solution)/shard_map/all_to_all | solution.py:392
  (3 other events, 2.1 us)
